TPU v7x, 512 devices: a whole 4x4x16 slice. The times are simulated.
512 devices in a mesh: dp: 4 (over y_lo, core), pipe: 16 (over z), tensor: 8 (over y_hi, x).
Axes of the slice: x: 4, y: 4 (y_hi: 2, y_lo: 2; y = y_hi * 2 + y_lo), z: 16, core: 2. Of those that a mesh axis runs over, the one named last changes fastest.
Arguments:
- inputs: bfloat16 [16, 4, 256, 8192], P('pipe', 'dp', None, 'tensor'), may hold values from -64 to 64
- norm_gain: float32 [16, 8192], P('pipe', 'tensor'), may hold values from 0.1 to 1.9
- queries: bfloat16 [16, 4, 256, 8192], P('pipe', 'dp', None, 'tensor'), may hold values from -8 to 8
- saved_keys: bfloat16 [16, 4, 256, 1024], P('pipe', 'dp', None, 'tensor'), may hold values from -8 to 8
- saved_values: bfloat16 [16, 4, 256, 1024], P('pipe', 'dp', None, 'tensor'), may hold values from -6 to 6
- attn_out_grad: bfloat16 [16, 4, 256, 8192], P('pipe', 'dp', None, 'tensor'), may hold values from -6 to 6
- kv_projection: bfloat16 [16, 2048, 8192], P('pipe', 'dp', 'tensor'), may hold values from -1 to 1
- top_grad: bfloat16 [4, 256, 8192], P('dp', None, 'tensor'), may hold values from -3 to 3
- doc_lengths: int32 [4, 4], P('dp'), may hold values from 1 to 128, 256 in all within a row
Outputs:
- section_grads: bfloat16 [16, 4, 256, 8192], P('pipe', 'dp', None, 'tensor')
- kv_projection_grad: bfloat16 [16, 2048, 8192], P('pipe', 'dp', 'tensor')
- norm_gain_grad: float32 [16, 8192], P('pipe', 'tensor')
Inputs may be any that keep to these rules, and one draw needn't show every extreme that they name: `doc_lengths`: each row sums to 256.
All inputs are finite; a program needn't handle non-finite values.
Results may differ from a plain program's by a relative error of at most 0.015.
Values may be sent and summed in bfloat16 or wider, within the bound.
No kernel may reach another device: no remote copies, remote signals or barrier semaphores. Data moves between devices by JAX's collectives and lax.ppermute only.
A program may use at most 128 MiB of HBM per device.

v0:
```python
import jax
import jax.numpy as jnp
from jax import lax
from jax.sharding import PartitionSpec as P

D = 8192
H = 64
KVH = 8
HD = 128


EPSILON = 1e-05


def from_behind(value, axis, steps):
    count = lax.axis_size(axis)
    leading, last = (max(0, -steps), min(count, count - steps))
    return lax.ppermute(value, axis, [(source, source + steps) for source in range(leading, last)])


def rounded_values(tensor):
    return lax.optimization_barrier(tensor.astype(jnp.bfloat16)).astype(jnp.float32)


def doc_mask(lengths, sequence_length):
    bounds = jnp.cumsum(lengths)
    places = jnp.arange(sequence_length, dtype=jnp.int32)
    owner = jnp.sum((places[:, None] >= bounds[None, :]).astype(jnp.int32), axis=1)
    return (owner[:, None] == owner[None, :]) & (places[:, None] >= places[None, :])


def attention_back(query, key_rows, value_rows, out_grad, allowed):
    kv_heads = key_rows.shape[-1] // HD
    group = H // KVH
    sequence_length = query.shape[0]
    query_heads = query.reshape(sequence_length, kv_heads, group, HD)
    key_heads = key_rows.reshape(sequence_length, kv_heads, HD)
    value_heads = value_rows.reshape(sequence_length, kv_heads, HD)
    grad_heads = out_grad.reshape(sequence_length, kv_heads, group, HD)
    factor = HD ** (-0.5)
    scores = (
        jnp.einsum("ikgd,jkd->kgij", query_heads, key_heads, preferred_element_type=jnp.float32)
        * factor
    )
    scores = jnp.where(allowed, scores, -1e30)
    row_max = jnp.max(scores, axis=-1, keepdims=True)
    expos = jnp.where(allowed, jnp.exp(scores - row_max), 0.0)
    probs = expos / jnp.sum(expos, axis=-1, keepdims=True)
    probs_b = probs.astype(jnp.bfloat16)
    grad_values = jnp.einsum(
        "kgij,ikgd->jkd", probs_b, grad_heads, preferred_element_type=jnp.float32
    ).astype(jnp.bfloat16)
    grad_probs = jnp.einsum(
        "ikgd,jkd->kgij", grad_heads, value_heads, preferred_element_type=jnp.float32
    )
    centre = jnp.sum(probs * grad_probs, axis=-1, keepdims=True)
    grad_scores = (probs * (grad_probs - centre) * factor).astype(jnp.bfloat16)
    grad_keys = jnp.einsum(
        "kgij,ikgd->jkd", grad_scores, query_heads, preferred_element_type=jnp.float32
    ).astype(jnp.bfloat16)
    return jnp.stack([grad_keys, grad_values], axis=2).reshape(sequence_length, kv_heads * 2 * HD)


def body(
    inputs,
    norm_gain,
    queries,
    saved_keys,
    saved_values,
    attn_out_grad,
    kv_projection,
    top_grad,
    doc_lengths,
):
    wide = inputs[0, 0].astype(jnp.float32)
    gain_row = norm_gain[0]
    sequence_length = wide.shape[0]
    row_sums = lax.psum(jnp.sum(wide * wide, axis=1), "tensor")
    row_rms = jnp.sqrt(row_sums / D + EPSILON)[:, None]
    unit_rows = wide / row_rms
    rms_scaled_rows = (unit_rows * gain_row).astype(jnp.bfloat16)
    allowed = doc_mask(doc_lengths[0], sequence_length)
    local_kv = attention_back(
        queries[0, 0], saved_keys[0, 0], saved_values[0, 0], attn_out_grad[0, 0], allowed
    )
    gradient_key_value = lax.all_gather(local_kv, "tensor", axis=1, tiled=True)
    columns = gradient_key_value
    grad_normed = jnp.dot(
        columns,
        lax.all_gather(kv_projection[0], "dp", axis=0, tiled=True),
        preferred_element_type=jnp.float32,
    )
    scaled = grad_normed * gain_row
    row_prods = lax.psum(jnp.sum(scaled * unit_rows, axis=1), "tensor")
    contrib = (scaled - unit_rows * (row_prods / D)[:, None]) / row_rms
    gradient_scale_factor = (lax.axis_size("dp") * sequence_length) ** (-0.5)
    gain_grad = lax.psum(jnp.sum(grad_normed * unit_rows, axis=0) * gradient_scale_factor, "dp")
    sections = lax.axis_size("pipe")
    section_index = lax.axis_index("pipe")
    pieces = 4
    rows_each = sequence_length // pieces
    blocks = contrib.reshape(pieces, rows_each, contrib.shape[1])

    def relay_step(step, carry):
        outgoing, collected = carry
        incoming = from_behind(outgoing.astype(jnp.bfloat16), "pipe", -1).astype(outgoing.dtype)
        block_id = step - (sections - 1 - section_index)
        in_range = (block_id >= 0) & (block_id < pieces)
        clamped = jnp.clip(block_id, 0, pieces - 1)
        summed = incoming + lax.dynamic_index_in_dim(blocks, clamped, 0, keepdims=False)
        updated = lax.dynamic_update_index_in_dim(collected, summed, clamped, 0)
        return (summed, jnp.where(in_range, updated, collected))

    start_state = (jnp.zeros_like(blocks[0]), jnp.zeros_like(blocks))
    final_out, collected = lax.fori_loop(0, sections + pieces - 1, relay_step, start_state)
    suffix = collected.reshape(sequence_length, contrib.shape[1])
    section_grads = (top_grad[0].astype(jnp.float32) + suffix).astype(jnp.bfloat16)
    columns = gradient_key_value
    term = lax.dot_general(
        columns, rms_scaled_rows, (((0,), (0,)), ((), ())), preferred_element_type=jnp.float32
    )
    kv_grad = lax.psum_scatter(
        rounded_values(term * gradient_scale_factor).astype(jnp.bfloat16),
        "dp",
        scatter_dimension=0,
        tiled=True,
    )
    return (section_grads[None, None], kv_grad[None], gain_grad[None])


def solution(mesh):
    placed = (
        P("pipe", "dp", None, "tensor"),
        P("pipe", "tensor"),
        P("pipe", "dp", None, "tensor"),
        P("pipe", "dp", None, "tensor"),
        P("pipe", "dp", None, "tensor"),
        P("pipe", "dp", None, "tensor"),
        P("pipe", "dp", "tensor"),
        P("dp", None, "tensor"),
        P("dp", None),
    )
    return jax.shard_map(
        body,
        mesh=mesh,
        in_specs=placed,
        out_specs=(P("pipe", "dp", None, "tensor"), P("pipe", "dp", "tensor"), P("pipe", "tensor")),
        check_vma=False,
    )
```

profile of v0, /device:TPU:96, one launch (start us, length us, event | category | flops | bytes accessed | tf_op | source)
XLA Modules:
  0.0 337.7 jit_solution(3464280872783450995)
XLA Ops:
  7.2 0.8 reduce-window.8
  8.1 0.1 convert_reduce_fusion
  8.1 0.1 fusion.25
  8.2 1.2 copy.26
  9.5 1.2 copy.27
  10.8 0.5 fusion.7
  11.2 0.5 fusion.9
  11.8 0.8 fusion.12
  12.6 0.8 fusion.3
  13.4 1.0 fusion.13
  14.4 0.7 pad_maximum_fusion
  15.2 0.7 all-gather.6.cloned.1.call-update
  15.9 0.2 fusion.14
  16.1 24.3 %psum.21 = f32[256]{0:T(256)S(1)} all-reduce(f32[256]{0:T(256)S(1)} %fusion.14), channel_id=1, replica_groups=mesh['dp'=4,'pipe'=16,'tensor'=8] {'tensor'}, use_global_device_ids=true, to_apply=%region_6.7 | all-reduce | flops 256 | bytes 2048 | tf_op jit(solution)/shard_map/psum | solution.py:78
  40.5 40.9 %all-gather.4.cloned.1.call-done = bf16[256,2048]{0,1:T(8,128)(2,1)} async-done(((bf16[256,256]{0,1:T(8,128)(2,1)}), bf16[256,2048]{0,1:T(8,128)(2,1)}) %all-gather.4.cloned.1.call-update) | async-done | bytes 1048592 | tf_op jit(solution)/shard_map/all_gather | solution.py:86
  81.4 4.5 %multiply_convert_fusion = bf16[2048,1024]{1,0:T(8,128)(2,1)} fusion(bf16[256,2048]{0,1:T(8,128)(2,1)} %all-gather.4.cloned.1.call-done, f32[1024]{0:T(1024)S(1)} %bitcast.138, bf16[1,1,256,1024]{3,2,1,0:T(8,128)(2,1)S(1)} %copy-done.1, f32[256]{0:T(256)S(1)} %add_sqrt_fusion), kind=kOutput, calls=%fused_computation.4 | convolution fusion | flops 1078984704 | bytes 5772288 | tf_op jit(solution)/shard_map/dot_general | solution.py:119
  85.9 50.2 %all-gather.6.cloned.1.call-done = bf16[1,2048,1024]{2,1,0:T(8,128)(2,1)} async-done(((bf16[1,512,1024]{2,1,0:T(8,128)(2,1)}), bf16[1,2048,1024]{2,1,0:T(8,128)(2,1)}) %all-gather.6.cloned.1.call-update) | async-done | bytes 4194320 | tf_op jit(solution)/shard_map/all_gather | solution.py:90
  136.1 3.6 %multiply_reduce_fusion = (f32[1024]{0:T(1024)S(1)}, f32[256]{0:T(256)S(1)}, f32[256,1024]{1,0:T(8,128)S(1)}) fusion(f32[256]{0:T(256)S(1)} %add_sqrt_fusion, bf16[1,1,256,1024]{3,2,1,0:T(8,128)(2,1)S(1)} %copy-done.1, f32[1024]{0:T(1024)S(1)} %bitcast.139, bf16[256,2048]{0,1:T(8,128)(2,1)S(1)} %copy-done.4, ...), kind=kOutput, calls=%fused_computation.31 | convolution fusion | flops 1075575552 | bytes 6825984 | tf_op jit(solution)/shard_map/dot_general | solution.py:88
  139.8 23.9 %psum.22 = f32[256]{0:T(256)S(1)} all-reduce(f32[256]{0:T(256)S(1)} %get-tuple-element.151), channel_id=1, replica_groups=mesh['dp'=4,'pipe'=16,'tensor'=8] {'tensor'}, use_global_device_ids=true, to_apply=%region_8.9 | all-reduce | flops 256 | bytes 2048 | tf_op jit(solution)/shard_map/psum | solution.py:94
  163.7 6.8 %psum.23 = f32[1,1024]{1,0:T(1,128)} all-reduce(f32[1,1024]{1,0:T(1,128)S(1)} %bitcast.137), channel_id=1, replica_groups=mesh['dp'=4,'pipe'=16,'tensor'=8] {'dp'}, use_global_device_ids=true, to_apply=%region_13.14 | all-reduce | flops 1024 | bytes 8192 | tf_op jit(solution)/shard_map/psum | solution.py:97
  170.4 0.3 subtract_divide_fusion
  170.7 0.1 broadcast_in_dim.47
  170.8 159.3 %while.18 = (s32[]{:T(128)}, bf16[64,1024]{1,0:T(8,128)(2,1)S(1)}, f32[4,64,1024]{2,1,0:T(8,128)S(1)}, s32[]{:T(128)}, f32[4,64,1024]{2,1,0:T(8,128)S(1)}, /*index=5*/s32[]{:T(128)}, s32[]{:T(128)}, s32[]{:T(128)}, s32[]{:T(128)}) while((s32[]{:T(128)}, bf16[64,1024]{1,0:T(8,128)(2,1)S(1)}, f32[4,64,1024]{2,1,0:T(8,128)S(1)}, ...), condition=%wide.region_10.11_spmd.clone, body=%wide.region_9.10_spmd.clone.sunk | while | flops 327689 | bytes 1835213 | solution.py:115
  170.9 2.5 collective-permute-start
  173.4 5.7 %collective-permute-done = bf16[64,1024]{1,0:T(8,128)(2,1)S(1)} collective-permute-done((bf16[64,1024]{1,0:T(8,128)(2,1)S(1)}, bf16[64,1024]{1,0:T(8,128)(2,1)S(1)}, u32[]{:S(2)}, u32[]{:S(2)}) %collective-permute-start) | collective-permute-done | bytes 131104 | tf_op jit(solution)/shard_map/while/body/eval_jaxpr/ppermute | solution.py:18
  179.1 0.1 fusion.43
  179.2 1.9 collective-permute-start
  181.2 6.1 %collective-permute-done = bf16[64,1024]{1,0:T(8,128)(2,1)S(1)} collective-permute-done((bf16[64,1024]{1,0:T(8,128)(2,1)S(1)}, bf16[64,1024]{1,0:T(8,128)(2,1)S(1)}, u32[]{:S(2)}, u32[]{:S(2)}) %collective-permute-start) | collective-permute-done | bytes 131104 | tf_op jit(solution)/shard_map/while/body/eval_jaxpr/ppermute | solution.py:18
  187.3 0.1 fusion.43
  187.4 1.9 collective-permute-start
  189.3 6.1 %collective-permute-done = bf16[64,1024]{1,0:T(8,128)(2,1)S(1)} collective-permute-done((bf16[64,1024]{1,0:T(8,128)(2,1)S(1)}, bf16[64,1024]{1,0:T(8,128)(2,1)S(1)}, u32[]{:S(2)}, u32[]{:S(2)}) %collective-permute-start) | collective-permute-done | bytes 131104 | tf_op jit(solution)/shard_map/while/body/eval_jaxpr/ppermute | solution.py:18
  195.6 1.9 collective-permute-start
  197.5 6.1 %collective-permute-done = bf16[64,1024]{1,0:T(8,128)(2,1)S(1)} collective-permute-done((bf16[64,1024]{1,0:T(8,128)(2,1)S(1)}, bf16[64,1024]{1,0:T(8,128)(2,1)S(1)}, u32[]{:S(2)}, u32[]{:S(2)}) %collective-permute-start) | collective-permute-done | bytes 131104 | tf_op jit(solution)/shard_map/while/body/eval_jaxpr/ppermute | solution.py:18
  203.8 1.9 collective-permute-start
  205.7 6.7 %collective-permute-done = bf16[64,1024]{1,0:T(8,128)(2,1)S(1)} collective-permute-done((bf16[64,1024]{1,0:T(8,128)(2,1)S(1)}, bf16[64,1024]{1,0:T(8,128)(2,1)S(1)}, u32[]{:S(2)}, u32[]{:S(2)}) %collective-permute-start) | collective-permute-done | bytes 131104 | tf_op jit(solution)/shard_map/while/body/eval_jaxpr/ppermute | solution.py:18
  212.5 1.9 collective-permute-start
  214.5 7.3 %collective-permute-done = bf16[64,1024]{1,0:T(8,128)(2,1)S(1)} collective-permute-done((bf16[64,1024]{1,0:T(8,128)(2,1)S(1)}, bf16[64,1024]{1,0:T(8,128)(2,1)S(1)}, u32[]{:S(2)}, u32[]{:S(2)}) %collective-permute-start) | collective-permute-done | bytes 131104 | tf_op jit(solution)/shard_map/while/body/eval_jaxpr/ppermute | solution.py:18
  221.8 1.9 collective-permute-start
  223.8 6.4 %collective-permute-done = bf16[64,1024]{1,0:T(8,128)(2,1)S(1)} collective-permute-done((bf16[64,1024]{1,0:T(8,128)(2,1)S(1)}, bf16[64,1024]{1,0:T(8,128)(2,1)S(1)}, u32[]{:S(2)}, u32[]{:S(2)}) %collective-permute-start) | collective-permute-done | bytes 131104 | tf_op jit(solution)/shard_map/while/body/eval_jaxpr/ppermute | solution.py:18
  230.3 1.9 collective-permute-start
  232.2 6.1 %collective-permute-done = bf16[64,1024]{1,0:T(8,128)(2,1)S(1)} collective-permute-done((bf16[64,1024]{1,0:T(8,128)(2,1)S(1)}, bf16[64,1024]{1,0:T(8,128)(2,1)S(1)}, u32[]{:S(2)}, u32[]{:S(2)}) %collective-permute-start) | collective-permute-done | bytes 131104 | tf_op jit(solution)/shard_map/while/body/eval_jaxpr/ppermute | solution.py:18
  238.5 1.9 collective-permute-start
  240.4 6.1 %collective-permute-done = bf16[64,1024]{1,0:T(8,128)(2,1)S(1)} collective-permute-done((bf16[64,1024]{1,0:T(8,128)(2,1)S(1)}, bf16[64,1024]{1,0:T(8,128)(2,1)S(1)}, u32[]{:S(2)}, u32[]{:S(2)}) %collective-permute-start) | collective-permute-done | bytes 131104 | tf_op jit(solution)/shard_map/while/body/eval_jaxpr/ppermute | solution.py:18
  246.7 1.9 collective-permute-start
  248.6 6.1 %collective-permute-done = bf16[64,1024]{1,0:T(8,128)(2,1)S(1)} collective-permute-done((bf16[64,1024]{1,0:T(8,128)(2,1)S(1)}, bf16[64,1024]{1,0:T(8,128)(2,1)S(1)}, u32[]{:S(2)}, u32[]{:S(2)}) %collective-permute-start) | collective-permute-done | bytes 131104 | tf_op jit(solution)/shard_map/while/body/eval_jaxpr/ppermute | solution.py:18
  254.8 1.9 collective-permute-start
  256.8 6.1 %collective-permute-done = bf16[64,1024]{1,0:T(8,128)(2,1)S(1)} collective-permute-done((bf16[64,1024]{1,0:T(8,128)(2,1)S(1)}, bf16[64,1024]{1,0:T(8,128)(2,1)S(1)}, u32[]{:S(2)}, u32[]{:S(2)}) %collective-permute-start) | collective-permute-done | bytes 131104 | tf_op jit(solution)/shard_map/while/body/eval_jaxpr/ppermute | solution.py:18
  263.0 1.9 collective-permute-start
  265.0 7.2 %collective-permute-done = bf16[64,1024]{1,0:T(8,128)(2,1)S(1)} collective-permute-done((bf16[64,1024]{1,0:T(8,128)(2,1)S(1)}, bf16[64,1024]{1,0:T(8,128)(2,1)S(1)}, u32[]{:S(2)}, u32[]{:S(2)}) %collective-permute-start) | collective-permute-done | bytes 131104 | tf_op jit(solution)/shard_map/while/body/eval_jaxpr/ppermute | solution.py:18
  272.3 1.9 collective-permute-start
  274.2 6.7 %collective-permute-done = bf16[64,1024]{1,0:T(8,128)(2,1)S(1)} collective-permute-done((bf16[64,1024]{1,0:T(8,128)(2,1)S(1)}, bf16[64,1024]{1,0:T(8,128)(2,1)S(1)}, u32[]{:S(2)}, u32[]{:S(2)}) %collective-permute-start) | collective-permute-done | bytes 131104 | tf_op jit(solution)/shard_map/while/body/eval_jaxpr/ppermute | solution.py:18
  281.1 1.9 collective-permute-start
  283.0 6.1 %collective-permute-done = bf16[64,1024]{1,0:T(8,128)(2,1)S(1)} collective-permute-done((bf16[64,1024]{1,0:T(8,128)(2,1)S(1)}, bf16[64,1024]{1,0:T(8,128)(2,1)S(1)}, u32[]{:S(2)}, u32[]{:S(2)}) %collective-permute-start) | collective-permute-done | bytes 131104 | tf_op jit(solution)/shard_map/while/body/eval_jaxpr/ppermute | solution.py:18
  289.3 1.9 collective-permute-start
  291.2 6.1 %collective-permute-done = bf16[64,1024]{1,0:T(8,128)(2,1)S(1)} collective-permute-done((bf16[64,1024]{1,0:T(8,128)(2,1)S(1)}, bf16[64,1024]{1,0:T(8,128)(2,1)S(1)}, u32[]{:S(2)}, u32[]{:S(2)}) %collective-permute-start) | collective-permute-done | bytes 131104 | tf_op jit(solution)/shard_map/while/body/eval_jaxpr/ppermute | solution.py:18
  297.5 1.9 collective-permute-start
  299.4 6.1 %collective-permute-done = bf16[64,1024]{1,0:T(8,128)(2,1)S(1)} collective-permute-done((bf16[64,1024]{1,0:T(8,128)(2,1)S(1)}, bf16[64,1024]{1,0:T(8,128)(2,1)S(1)}, u32[]{:S(2)}, u32[]{:S(2)}) %collective-permute-start) | collective-permute-done | bytes 131104 | tf_op jit(solution)/shard_map/while/body/eval_jaxpr/ppermute | solution.py:18
  305.6 1.9 collective-permute-start
  307.6 6.1 %collective-permute-done = bf16[64,1024]{1,0:T(8,128)(2,1)S(1)} collective-permute-done((bf16[64,1024]{1,0:T(8,128)(2,1)S(1)}, bf16[64,1024]{1,0:T(8,128)(2,1)S(1)}, u32[]{:S(2)}, u32[]{:S(2)}) %collective-permute-start) | collective-permute-done | bytes 131104 | tf_op jit(solution)/shard_map/while/body/eval_jaxpr/ppermute | solution.py:18
  313.8 1.9 collective-permute-start
  315.8 6.1 %collective-permute-done = bf16[64,1024]{1,0:T(8,128)(2,1)S(1)} collective-permute-done((bf16[64,1024]{1,0:T(8,128)(2,1)S(1)}, bf16[64,1024]{1,0:T(8,128)(2,1)S(1)}, u32[]{:S(2)}, u32[]{:S(2)}) %collective-permute-start) | collective-permute-done | bytes 131104 | tf_op jit(solution)/shard_map/while/body/eval_jaxpr/ppermute | solution.py:18
  322.0 1.9 collective-permute-start
  324.0 6.1 %collective-permute-done = bf16[64,1024]{1,0:T(8,128)(2,1)S(1)} collective-permute-done((bf16[64,1024]{1,0:T(8,128)(2,1)S(1)}, bf16[64,1024]{1,0:T(8,128)(2,1)S(1)}, u32[]{:S(2)}, u32[]{:S(2)}) %collective-permute-start) | collective-permute-done | bytes 131104 | tf_op jit(solution)/shard_map/while/body/eval_jaxpr/ppermute | solution.py:18
  330.2 0.9 fusion.17
  (58 shorter events, 1.8 us)
Async XLA Ops:
  7.2 3.6 %copy-start = (bf16[1,1,256,128]{3,2,1,0:T(8,128)(2,1)S(1)}, bf16[1,1,256,128]{3,2,1,0:T(8,128)(2,1)}, u32[]{:S(2)}) copy-start(bf16[1,1,256,128]{3,2,1,0:T(8,128)(2,1)} %param.14) | copy-start | bytes 196612
  7.2 74.2 %all-gather.4.cloned.1.call-start = ((), (), s32[]{:S(2)}) async-start(), calls=%async_computation.1 | async-start | bytes 1179648 | tf_op jit(solution)/shard_map/all_gather | solution.py:86
  11.7 0.8 copy-start.5
  13.4 2.5 copy-start.1
  13.4 68.0 %copy-start.3 = (f32[1,1024]{1,0:T(1,128)S(1)}, f32[1,1024]{1,0:T(1,128)}, u32[]{:S(2)}) copy-start(f32[1,1024]{1,0:T(1,128)} %param.12) | copy-start | bytes 12292
  15.1 121.0 %all-gather.6.cloned.1.call-start = ((), (), s32[]{:S(2)}) async-start(), calls=%async_computation.3 | async-start | bytes 5242880 | tf_op jit(solution)/shard_map/all_gather | solution.py:90
  15.9 315.3 %reduce-scatter.2.cloned.1.call-start = ((), (), s32[]{:S(2)}) async-start(), calls=%async_computation.2 | async-start | bytes 5242880 | tf_op jit(solution)/shard_map/reduce_scatter | solution.py:122
  85.9 50.2 %copy-start.4 = (bf16[256,2048]{0,1:T(8,128)(2,1)S(1)}, bf16[256,2048]{0,1:T(8,128)(2,1)}, u32[]{:S(2)}) copy-start(bf16[256,2048]{0,1:T(8,128)(2,1)} %all-gather.4.cloned.1.call-done) | copy-start | bytes 3145732
  170.8 159.3 %copy-start.2 = (bf16[1,256,1024]{2,1,0:T(8,128)(2,1)S(1)}, bf16[1,256,1024]{2,1,0:T(8,128)(2,1)}, u32[]{:S(2)}) copy-start(bf16[1,256,1024]{2,1,0:T(8,128)(2,1)} %param.18) | copy-start | bytes 1572868
  170.9 8.2 %collective-permute-start = (bf16[64,1024]{1,0:T(8,128)(2,1)S(1)}, bf16[64,1024]{1,0:T(8,128)(2,1)S(1)}, u32[]{:S(2)}, u32[]{:S(2)}) collective-permute-start(bf16[64,1024]{1,0:T(8,128)(2,1)S(1)} %select_convert_fusion.2), channel_id=1, source_target_pairs={{8,0},{16,8},{24,16},{32,24},{40,32},{48,40},{56,48},{64,56},{72,6... | collective-permute-start | bytes 393224 | tf_op jit(solution)/shard_map/while/body/eval_jaxpr/ppermute | solution.py:18
  179.2 8.1 %collective-permute-start = (bf16[64,1024]{1,0:T(8,128)(2,1)S(1)}, bf16[64,1024]{1,0:T(8,128)(2,1)S(1)}, u32[]{:S(2)}, u32[]{:S(2)}) collective-permute-start(bf16[64,1024]{1,0:T(8,128)(2,1)S(1)} %select_convert_fusion.2), channel_id=1, source_target_pairs={{8,0},{16,8},{24,16},{32,24},{40,32},{48,40},{56,48},{64,56},{72,6... | collective-permute-start | bytes 393224 | tf_op jit(solution)/shard_map/while/body/eval_jaxpr/ppermute | solution.py:18
  187.4 8.1 %collective-permute-start = (bf16[64,1024]{1,0:T(8,128)(2,1)S(1)}, bf16[64,1024]{1,0:T(8,128)(2,1)S(1)}, u32[]{:S(2)}, u32[]{:S(2)}) collective-permute-start(bf16[64,1024]{1,0:T(8,128)(2,1)S(1)} %select_convert_fusion.2), channel_id=1, source_target_pairs={{8,0},{16,8},{24,16},{32,24},{40,32},{48,40},{56,48},{64,56},{72,6... | collective-permute-start | bytes 393224 | tf_op jit(solution)/shard_map/while/body/eval_jaxpr/ppermute | solution.py:18
  195.6 8.1 %collective-permute-start = (bf16[64,1024]{1,0:T(8,128)(2,1)S(1)}, bf16[64,1024]{1,0:T(8,128)(2,1)S(1)}, u32[]{:S(2)}, u32[]{:S(2)}) collective-permute-start(bf16[64,1024]{1,0:T(8,128)(2,1)S(1)} %select_convert_fusion.2), channel_id=1, source_target_pairs={{8,0},{16,8},{24,16},{32,24},{40,32},{48,40},{56,48},{64,56},{72,6... | collective-permute-start | bytes 393224 | tf_op jit(solution)/shard_map/while/body/eval_jaxpr/ppermute | solution.py:18
  203.8 8.6 %collective-permute-start = (bf16[64,1024]{1,0:T(8,128)(2,1)S(1)}, bf16[64,1024]{1,0:T(8,128)(2,1)S(1)}, u32[]{:S(2)}, u32[]{:S(2)}) collective-permute-start(bf16[64,1024]{1,0:T(8,128)(2,1)S(1)} %select_convert_fusion.2), channel_id=1, source_target_pairs={{8,0},{16,8},{24,16},{32,24},{40,32},{48,40},{56,48},{64,56},{72,6... | collective-permute-start | bytes 393224 | tf_op jit(solution)/shard_map/while/body/eval_jaxpr/ppermute | solution.py:18
  212.5 9.2 %collective-permute-start = (bf16[64,1024]{1,0:T(8,128)(2,1)S(1)}, bf16[64,1024]{1,0:T(8,128)(2,1)S(1)}, u32[]{:S(2)}, u32[]{:S(2)}) collective-permute-start(bf16[64,1024]{1,0:T(8,128)(2,1)S(1)} %select_convert_fusion.2), channel_id=1, source_target_pairs={{8,0},{16,8},{24,16},{32,24},{40,32},{48,40},{56,48},{64,56},{72,6... | collective-permute-start | bytes 393224 | tf_op jit(solution)/shard_map/while/body/eval_jaxpr/ppermute | solution.py:18
  221.8 8.3 %collective-permute-start = (bf16[64,1024]{1,0:T(8,128)(2,1)S(1)}, bf16[64,1024]{1,0:T(8,128)(2,1)S(1)}, u32[]{:S(2)}, u32[]{:S(2)}) collective-permute-start(bf16[64,1024]{1,0:T(8,128)(2,1)S(1)} %select_convert_fusion.2), channel_id=1, source_target_pairs={{8,0},{16,8},{24,16},{32,24},{40,32},{48,40},{56,48},{64,56},{72,6... | collective-permute-start | bytes 393224 | tf_op jit(solution)/shard_map/while/body/eval_jaxpr/ppermute | solution.py:18
  230.3 8.1 %collective-permute-start = (bf16[64,1024]{1,0:T(8,128)(2,1)S(1)}, bf16[64,1024]{1,0:T(8,128)(2,1)S(1)}, u32[]{:S(2)}, u32[]{:S(2)}) collective-permute-start(bf16[64,1024]{1,0:T(8,128)(2,1)S(1)} %select_convert_fusion.2), channel_id=1, source_target_pairs={{8,0},{16,8},{24,16},{32,24},{40,32},{48,40},{56,48},{64,56},{72,6... | collective-permute-start | bytes 393224 | tf_op jit(solution)/shard_map/while/body/eval_jaxpr/ppermute | solution.py:18
  238.5 8.1 %collective-permute-start = (bf16[64,1024]{1,0:T(8,128)(2,1)S(1)}, bf16[64,1024]{1,0:T(8,128)(2,1)S(1)}, u32[]{:S(2)}, u32[]{:S(2)}) collective-permute-start(bf16[64,1024]{1,0:T(8,128)(2,1)S(1)} %select_convert_fusion.2), channel_id=1, source_target_pairs={{8,0},{16,8},{24,16},{32,24},{40,32},{48,40},{56,48},{64,56},{72,6... | collective-permute-start | bytes 393224 | tf_op jit(solution)/shard_map/while/body/eval_jaxpr/ppermute | solution.py:18
  246.7 8.1 %collective-permute-start = (bf16[64,1024]{1,0:T(8,128)(2,1)S(1)}, bf16[64,1024]{1,0:T(8,128)(2,1)S(1)}, u32[]{:S(2)}, u32[]{:S(2)}) collective-permute-start(bf16[64,1024]{1,0:T(8,128)(2,1)S(1)} %select_convert_fusion.2), channel_id=1, source_target_pairs={{8,0},{16,8},{24,16},{32,24},{40,32},{48,40},{56,48},{64,56},{72,6... | collective-permute-start | bytes 393224 | tf_op jit(solution)/shard_map/while/body/eval_jaxpr/ppermute | solution.py:18
  254.8 8.1 %collective-permute-start = (bf16[64,1024]{1,0:T(8,128)(2,1)S(1)}, bf16[64,1024]{1,0:T(8,128)(2,1)S(1)}, u32[]{:S(2)}, u32[]{:S(2)}) collective-permute-start(bf16[64,1024]{1,0:T(8,128)(2,1)S(1)} %select_convert_fusion.2), channel_id=1, source_target_pairs={{8,0},{16,8},{24,16},{32,24},{40,32},{48,40},{56,48},{64,56},{72,6... | collective-permute-start | bytes 393224 | tf_op jit(solution)/shard_map/while/body/eval_jaxpr/ppermute | solution.py:18
  263.0 9.1 %collective-permute-start = (bf16[64,1024]{1,0:T(8,128)(2,1)S(1)}, bf16[64,1024]{1,0:T(8,128)(2,1)S(1)}, u32[]{:S(2)}, u32[]{:S(2)}) collective-permute-start(bf16[64,1024]{1,0:T(8,128)(2,1)S(1)} %select_convert_fusion.2), channel_id=1, source_target_pairs={{8,0},{16,8},{24,16},{32,24},{40,32},{48,40},{56,48},{64,56},{72,6... | collective-permute-start | bytes 393224 | tf_op jit(solution)/shard_map/while/body/eval_jaxpr/ppermute | solution.py:18
  272.3 8.7 %collective-permute-start = (bf16[64,1024]{1,0:T(8,128)(2,1)S(1)}, bf16[64,1024]{1,0:T(8,128)(2,1)S(1)}, u32[]{:S(2)}, u32[]{:S(2)}) collective-permute-start(bf16[64,1024]{1,0:T(8,128)(2,1)S(1)} %select_convert_fusion.2), channel_id=1, source_target_pairs={{8,0},{16,8},{24,16},{32,24},{40,32},{48,40},{56,48},{64,56},{72,6... | collective-permute-start | bytes 393224 | tf_op jit(solution)/shard_map/while/body/eval_jaxpr/ppermute | solution.py:18
  281.1 8.1 %collective-permute-start = (bf16[64,1024]{1,0:T(8,128)(2,1)S(1)}, bf16[64,1024]{1,0:T(8,128)(2,1)S(1)}, u32[]{:S(2)}, u32[]{:S(2)}) collective-permute-start(bf16[64,1024]{1,0:T(8,128)(2,1)S(1)} %select_convert_fusion.2), channel_id=1, source_target_pairs={{8,0},{16,8},{24,16},{32,24},{40,32},{48,40},{56,48},{64,56},{72,6... | collective-permute-start | bytes 393224 | tf_op jit(solution)/shard_map/while/body/eval_jaxpr/ppermute | solution.py:18
  289.3 8.1 %collective-permute-start = (bf16[64,1024]{1,0:T(8,128)(2,1)S(1)}, bf16[64,1024]{1,0:T(8,128)(2,1)S(1)}, u32[]{:S(2)}, u32[]{:S(2)}) collective-permute-start(bf16[64,1024]{1,0:T(8,128)(2,1)S(1)} %select_convert_fusion.2), channel_id=1, source_target_pairs={{8,0},{16,8},{24,16},{32,24},{40,32},{48,40},{56,48},{64,56},{72,6... | collective-permute-start | bytes 393224 | tf_op jit(solution)/shard_map/while/body/eval_jaxpr/ppermute | solution.py:18
  297.5 8.1 %collective-permute-start = (bf16[64,1024]{1,0:T(8,128)(2,1)S(1)}, bf16[64,1024]{1,0:T(8,128)(2,1)S(1)}, u32[]{:S(2)}, u32[]{:S(2)}) collective-permute-start(bf16[64,1024]{1,0:T(8,128)(2,1)S(1)} %select_convert_fusion.2), channel_id=1, source_target_pairs={{8,0},{16,8},{24,16},{32,24},{40,32},{48,40},{56,48},{64,56},{72,6... | collective-permute-start | bytes 393224 | tf_op jit(solution)/shard_map/while/body/eval_jaxpr/ppermute | solution.py:18
  305.6 8.1 %collective-permute-start = (bf16[64,1024]{1,0:T(8,128)(2,1)S(1)}, bf16[64,1024]{1,0:T(8,128)(2,1)S(1)}, u32[]{:S(2)}, u32[]{:S(2)}) collective-permute-start(bf16[64,1024]{1,0:T(8,128)(2,1)S(1)} %select_convert_fusion.2), channel_id=1, source_target_pairs={{8,0},{16,8},{24,16},{32,24},{40,32},{48,40},{56,48},{64,56},{72,6... | collective-permute-start | bytes 393224 | tf_op jit(solution)/shard_map/while/body/eval_jaxpr/ppermute | solution.py:18
  313.8 8.1 %collective-permute-start = (bf16[64,1024]{1,0:T(8,128)(2,1)S(1)}, bf16[64,1024]{1,0:T(8,128)(2,1)S(1)}, u32[]{:S(2)}, u32[]{:S(2)}) collective-permute-start(bf16[64,1024]{1,0:T(8,128)(2,1)S(1)} %select_convert_fusion.2), channel_id=1, source_target_pairs={{8,0},{16,8},{24,16},{32,24},{40,32},{48,40},{56,48},{64,56},{72,6... | collective-permute-start | bytes 393224 | tf_op jit(solution)/shard_map/while/body/eval_jaxpr/ppermute | solution.py:18
  322.0 8.1 %collective-permute-start = (bf16[64,1024]{1,0:T(8,128)(2,1)S(1)}, bf16[64,1024]{1,0:T(8,128)(2,1)S(1)}, u32[]{:S(2)}, u32[]{:S(2)}) collective-permute-start(bf16[64,1024]{1,0:T(8,128)(2,1)S(1)} %select_convert_fusion.2), channel_id=1, source_target_pairs={{8,0},{16,8},{24,16},{32,24},{40,32},{48,40},{56,48},{64,56},{72,6... | collective-permute-start | bytes 393224 | tf_op jit(solution)/shard_map/while/body/eval_jaxpr/ppermute | solution.py:18
Sparse Core Ops, SparseCore 0:
  15.2 66.0 all-gather.3
  83.5 52.6 all-gather.5
  139.6 54.6 reduce-scatter.1
where the time goes:
time: 339 us; the launch traced here: 338 us
  waiting for transfers between devices  211 us (62%)
  blocking collectives  55 us (16%)
  starting transfers between devices  37.2 us (11%)
  between operations  13.9 us (4%)
  matrix products  11.2 us (3%)
  other arithmetic  5.27 us (2%)
    ppermute x19, waiting for transfers between devices, from_behind(): lax.ppermute(value, axis, [(source, source + steps) for source in range(l...  120 us
    all_gather x1, waiting for transfers between devices, body(): lax.all_gather(kv_projection[0], 'dp', axis=0, tiled=True)  50.2 us
    all_gather x1, waiting for transfers between devices, body(): gradient_key_value = lax.all_gather(local_kv, 'tensor', axis=1, tiled=True)  40.9 us
    ppermute x19, starting transfers between devices, from_behind(): lax.ppermute(value, axis, [(source, source + steps) for source in range(l...  37.1 us
    psum x1, blocking collectives, body(): row_sums = lax.psum(jnp.sum(wide * wide, axis=1), 'tensor')  24.3 us
    psum x1, blocking collectives, body(): row_prods = lax.psum(jnp.sum(scaled * unit_rows, axis=1), 'tensor')  23.9 us
  transfers between devices with their start and end apart: 22, of which 21 were waited for; matrix products, arithmetic and copies ran while one was open for 3% of the time, Pallas kernels for 0%

commit v1 on v0

v1 whole, which is shorter than its diff:
```python
import jax
import jax.numpy as jnp
from jax import lax
from jax.sharding import PartitionSpec as P

D = 8192
H = 64
KVH = 8
HD = 128
EPSILON = 1e-05


def doc_mask(lengths, sequence_length):
    bounds = jnp.cumsum(lengths)
    places = jnp.arange(sequence_length, dtype=jnp.int32)
    owner = jnp.sum((places[:, None] >= bounds[None, :]).astype(jnp.int32), axis=1)
    return (owner[:, None] == owner[None, :]) & (places[:, None] >= places[None, :])


def attention_back(query, key_rows, value_rows, out_grad, allowed):
    kv_heads = key_rows.shape[-1] // HD
    group = H // KVH
    sequence_length = query.shape[0]
    query_heads = query.reshape(sequence_length, kv_heads, group, HD)
    key_heads = key_rows.reshape(sequence_length, kv_heads, HD)
    value_heads = value_rows.reshape(sequence_length, kv_heads, HD)
    grad_heads = out_grad.reshape(sequence_length, kv_heads, group, HD)
    factor = HD ** (-0.5)
    scores = (
        jnp.einsum("ikgd,jkd->kgij", query_heads, key_heads, preferred_element_type=jnp.float32)
        * factor
    )
    scores = jnp.where(allowed, scores, -1e30)
    row_max = jnp.max(scores, axis=-1, keepdims=True)
    expos = jnp.where(allowed, jnp.exp(scores - row_max), 0.0)
    probs = expos / jnp.sum(expos, axis=-1, keepdims=True)
    probs_b = probs.astype(jnp.bfloat16)
    grad_values = jnp.einsum(
        "kgij,ikgd->jkd", probs_b, grad_heads, preferred_element_type=jnp.float32
    ).astype(jnp.bfloat16)
    grad_probs = jnp.einsum(
        "ikgd,jkd->kgij", grad_heads, value_heads, preferred_element_type=jnp.float32
    )
    centre = jnp.sum(probs * grad_probs, axis=-1, keepdims=True)
    grad_scores = (probs * (grad_probs - centre) * factor).astype(jnp.bfloat16)
    grad_keys = jnp.einsum(
        "kgij,ikgd->jkd", grad_scores, query_heads, preferred_element_type=jnp.float32
    ).astype(jnp.bfloat16)
    return jnp.stack([grad_keys, grad_values], axis=2).reshape(sequence_length, kv_heads * 2 * HD)


def sum_over(vector, axis):
    count = lax.axis_size(axis)
    copies = jnp.broadcast_to(vector.reshape(1, -1, 128), (count, vector.size // 128, 128))
    return jnp.sum(lax.all_to_all(copies, axis, 0, 0), axis=0).reshape(vector.shape)


def body(
    inputs,
    norm_gain,
    queries,
    saved_keys,
    saved_values,
    attn_out_grad,
    kv_projection,
    top_grad,
    doc_lengths,
):
    tensor, sections = lax.axis_size("tensor"), lax.axis_size("pipe")
    projection = lax.all_gather(kv_projection[0], "dp", axis=0, tiled=True)
    wide = inputs[0, 0].astype(jnp.float32)
    gain_row = norm_gain[0]
    tokens, width = wide.shape
    row_sums = sum_over(jnp.sum(wide * wide, axis=1), "tensor")
    row_rms = jnp.sqrt(row_sums / D + EPSILON)[:, None]
    unit_rows = wide / row_rms
    normed = (unit_rows * gain_row).astype(jnp.bfloat16)
    allowed = doc_mask(doc_lengths[0], tokens)
    local_kv = attention_back(
        queries[0, 0], saved_keys[0, 0], saved_values[0, 0], attn_out_grad[0, 0], allowed
    )
    copies = jnp.broadcast_to(local_kv[None], (tensor,) + local_kv.shape)
    grad_kv = lax.all_to_all(copies, "tensor", 0, 0)
    columns = jnp.concatenate([grad_kv[head] for head in range(tensor)], axis=1)
    grad_normed = jnp.dot(columns, projection, preferred_element_type=jnp.float32)
    scaled = grad_normed * gain_row
    row_prods = sum_over(jnp.sum(scaled * unit_rows, axis=1), "tensor")
    contrib = ((scaled - unit_rows * (row_prods / D)[:, None]) / row_rms).astype(jnp.bfloat16)
    scale = (lax.axis_size("dp") * tokens) ** (-0.5)
    parts = lax.all_to_all(contrib.reshape(sections, tokens // sections, width), "pipe", 0, 0)
    gain_grad = lax.psum(jnp.sum(grad_normed * unit_rows, axis=0) * scale, "dp")
    term = lax.dot_general(
        columns, normed, (((0,), (0,)), ((), ())), preferred_element_type=jnp.float32
    )
    kv_grad = lax.psum_scatter(
        (term * scale).astype(jnp.bfloat16), "dp", scatter_dimension=0, tiled=True
    )
    rows_each = tokens // sections
    own_top = lax.dynamic_slice_in_dim(
        top_grad[0], lax.axis_index("pipe") * rows_each, rows_each, 0
    )
    total = own_top.astype(jnp.float32)
    suffixes = [None] * sections
    for section in reversed(range(sections)):
        total = total + parts[section].astype(jnp.float32)
        suffixes[section] = total.astype(jnp.bfloat16)
    section_grads = lax.all_to_all(jnp.stack(suffixes), "pipe", 0, 0).reshape(tokens, width)
    return (section_grads[None, None], kv_grad[None], gain_grad[None])


def solution(mesh):
    placed = (
        P("pipe", "dp", None, "tensor"),
        P("pipe", "tensor"),
        P("pipe", "dp", None, "tensor"),
        P("pipe", "dp", None, "tensor"),
        P("pipe", "dp", None, "tensor"),
        P("pipe", "dp", None, "tensor"),
        P("pipe", "dp", "tensor"),
        P("dp", None, "tensor"),
        P("dp", None),
    )
    return jax.shard_map(
        body,
        mesh=mesh,
        in_specs=placed,
        out_specs=(P("pipe", "dp", None, "tensor"), P("pipe", "dp", "tensor"), P("pipe", "tensor")),
        check_vma=False,
    )
```

time: 339 us -> 195 us (0.58)
  the two profiles are of different devices: /device:TPU:96 before, /device:TPU:32 now
where the time goes in v1:
time: 195 us; the launch traced here: 194 us
  waiting for transfers between devices  94 us (48%)
  starting transfers between devices  34 us (17%)
  blocking collectives  21.1 us (11%)
  other arithmetic  16.4 us (8%)
  between operations  14.3 us (7%)
  matrix products  9.99 us (5%)
  local copies, waits for them, and re-layouts  4.16 us (2%)
    all_to_all x1, waiting for transfers between devices, body(): lax.all_to_all(contrib.reshape(sections, tokens // sections, width), 'pip...  27.4 us
    all_gather x1, waiting for transfers between devices, body(): projection = lax.all_gather(kv_projection[0], 'dp', axis=0, tiled=True)  25.4 us
    all_to_all x1, waiting for transfers between devices, body(): lax.all_to_all(jnp.stack(suffixes), 'pipe', 0, 0).reshape(tokens, width)  21.2 us
    all_to_all x1, waiting for transfers between devices, body(): grad_kv = lax.all_to_all(copies, 'tensor', 0, 0)  17.1 us
    all_to_all x1, starting transfers between devices, body(): lax.all_to_all(contrib.reshape(sections, tokens // sections, width), 'pip...  14.9 us
    all_to_all x1, blocking collectives, sum_over(): lax.all_to_all(copies, axis, 0, 0)  14.8 us
    unnamed x15, other arithmetic  11.7 us
    all_to_all x1, starting transfers between devices, sum_over(): lax.all_to_all(copies, axis, 0, 0)  6.93 us
  transfers between devices with their start and end apart: 6, of which 5 were waited for; matrix products, arithmetic and copies ran while one was open for 15% of the time, Pallas kernels for 0%

profile of v1, /device:TPU:32, one launch (start us, length us, event | category | flops | bytes accessed | tf_op | source)
XLA Modules:
  0.0 193.9 jit_solution(5926808204810705366)
XLA Ops:
  7.2 0.0 copy-start
  7.2 0.0 copy-start.2
  7.2 0.0 copy-start.5
  7.2 0.0 all-gather.3.cloned.1.call-start
  7.2 0.7 all-gather.3.cloned.1.call-update
  7.9 1.2 fusion.13
  9.2 0.6 broadcast_in_dim.56
  9.8 6.9 %all-to-all-start.1 = ((f32[8,2,128]{2,1,0:T(2,128)}), f32[8,2,128]{2,1,0:T(2,128)S(1)}, u32[]{:S(2)}, u32[]{:S(2)}) async-start(f32[8,2,128]{2,1,0:T(2,128)} %broadcast_in_dim.56), calls=%async_computation.1 | async-start | bytes 16384 | tf_op jit(solution)/shard_map/all_to_all | solution.py:55
  16.7 1.2 copy.39
  17.9 0.0 copy-done.2
  18.0 0.2 copy.40
  18.2 0.0 copy-done.5
  18.2 0.2 reduce-window.8
  18.4 0.1 convert_reduce_fusion
  18.4 0.1 fusion.23
  18.5 0.0 copy-done
  18.6 0.5 fusion.6
  19.0 0.5 fusion.8
  19.5 0.0 copy-start.4
  19.6 0.8 fusion.11
  20.3 0.1 copy-done.4
  20.4 0.8 fusion.2
  21.2 1.0 fusion.12
  22.2 0.1 copy.32
  22.3 2.1 %all-to-all-done.1 = f32[8,2,128]{2,1,0:T(2,128)S(1)} async-done(((f32[8,2,128]{2,1,0:T(2,128)}), f32[8,2,128]{2,1,0:T(2,128)S(1)}, u32[]{:S(2)}, u32[]{:S(2)}) %all-to-all-start.1) | async-done | bytes 8224 | tf_op jit(solution)/shard_map/all_to_all | solution.py:55
  24.4 1.0 broadcast_in_dim.54
  25.4 0.0 copy-start.1
  25.4 0.0 copy-start.3
  25.4 5.3 %all-to-all-start = ((bf16[8,256,256]{2,1,0:T(8,128)(2,1)}), bf16[8,256,256]{2,1,0:T(8,128)(2,1)S(1)}, u32[]{:S(2)}, u32[]{:S(2)}) async-start(bf16[8,256,256]{2,1,0:T(8,128)(2,1)} %broadcast_in_dim.54), calls=%async_computation | async-start | bytes 2097152 | tf_op jit(solution)/shard_map/all_to_all | solution.py:83
  30.7 0.0 reduce-scatter.2.cloned.1.call-start
  30.8 17.1 %all-to-all-done = bf16[8,256,256]{2,1,0:T(8,128)(2,1)S(1)} async-done(((bf16[8,256,256]{2,1,0:T(8,128)(2,1)}), bf16[8,256,256]{2,1,0:T(8,128)(2,1)S(1)}, u32[]{:S(2)}, u32[]{:S(2)}) %all-to-all-start) | async-done | bytes 1048608 | tf_op jit(solution)/shard_map/all_to_all | solution.py:83
  48.1 0.0 copy-done.1
  48.1 0.0 copy-done.3
  48.1 3.4 %multiply_convert_fusion = bf16[2048,1024]{1,0:T(8,128)(2,1)} fusion(bf16[256,2048]{1,0:T(8,128)(2,1)S(1)} %fusion.24, f32[1024]{0:T(1024)S(1)} %bitcast.163, bf16[1,1,256,1024]{3,2,1,0:T(8,128)(2,1)S(1)} %copy-done.1, f32[256]{0:T(256)S(1)} %sqrt_bitcast_fusion), kind=kOutput, calls=%fused_computation | convolution fusion | flops 1078984704 | bytes 5772288 | tf_op jit(solution)/shard_map/dot_general | solution.py:92
  51.4 0.0 reduce-scatter.2.cloned.1.call-update
  51.5 25.4 %all-gather.3.cloned.1.call-done = bf16[1,2048,1024]{2,1,0:T(8,128)(2,1)} async-done(((bf16[1,512,1024]{2,1,0:T(8,128)(2,1)}), bf16[1,2048,1024]{2,1,0:T(8,128)(2,1)}) %all-gather.3.cloned.1.call-update) | async-done | bytes 4194320 | tf_op jit(solution)/shard_map/all_gather | solution.py:70
  76.9 3.6 %multiply_reduce_fusion = (f32[1024]{0:T(1024)S(1)}, f32[256]{0:T(256)S(1)}, f32[256,1024]{1,0:T(8,128)S(1)}) fusion(f32[256]{0:T(256)S(1)} %sqrt_bitcast_fusion, bf16[1,1,256,1024]{3,2,1,0:T(8,128)(2,1)S(1)} %copy-done.1, f32[1024]{0:T(1024)S(1)} %bitcast.164, bf16[256,2048]{1,0:T(8,128)(2,1)S(1)} %fusion.24, ...), kind=kOutput, calls=%fused_computation.25 | convolution fusion | flops 1075575552 | bytes 6825984 | tf_op jit(solution)/shard_map/dot_general | solution.py:85
  80.5 14.8 %all_to_all.25 = f32[8,2,128]{2,1,0:T(2,128)S(1)} all-to-all(f32[8,2,128]{2,1,0:T(2,128)S(1)} %broadcast_in_dim.58), channel_id=1, replica_groups=mesh['dp'=4,'pipe'=16,'tensor'=8] {'tensor'}, dimensions={0} | all-to-all | bytes 16384 | tf_op jit(solution)/shard_map/all_to_all | solution.py:55
  95.3 1.1 divide_convert_fusion
  96.4 14.9 %all-to-all-start.3 = ((bf16[16,16,1024]{2,1,0:T(8,128)(2,1)}), bf16[16,16,1024]{2,1,0:T(8,128)(2,1)S(1)}, u32[]{:S(2)}, u32[]{:S(2)}) async-start(bf16[16,16,1024]{2,1,0:T(8,128)(2,1)} %bitcast.40), calls=%async_computation.3 | async-start | bytes 1048576 | tf_op jit(solution)/shard_map/all_to_all | solution.py:90
  111.3 27.4 %all-to-all-done.3 = bf16[16,16,1024]{2,1,0:T(8,128)(2,1)S(1)} async-done(((bf16[16,16,1024]{2,1,0:T(8,128)(2,1)}), bf16[16,16,1024]{2,1,0:T(8,128)(2,1)S(1)}, u32[]{:S(2)}, u32[]{:S(2)}) %all-to-all-start.3) | async-done | bytes 524320 | tf_op jit(solution)/shard_map/all_to_all | solution.py:90
  138.8 1.5 constant_dynamic-update-slice_fusion.15
  140.2 0.6 constant_dynamic-update-slice_fusion.14
  140.9 0.6 constant_dynamic-update-slice_fusion.13
  141.5 0.6 constant_dynamic-update-slice_fusion.12
  142.1 0.6 constant_dynamic-update-slice_fusion.11
  142.7 0.6 constant_dynamic-update-slice_fusion.10
  143.4 0.6 constant_dynamic-update-slice_fusion.9
  144.0 0.6 constant_dynamic-update-slice_fusion.8
  144.6 0.6 constant_dynamic-update-slice_fusion.7
  145.2 0.6 constant_dynamic-update-slice_fusion.6
  145.9 0.6 constant_dynamic-update-slice_fusion.5
  146.5 0.6 constant_dynamic-update-slice_fusion.4
  147.1 0.6 constant_dynamic-update-slice_fusion.3
  147.8 1.4 constant_dynamic-update-slice_fusion.2
  149.1 1.4 constant_dynamic-update-slice_fusion.1
  150.5 1.4 constant_dynamic-update-slice_fusion
  151.9 6.8 %all-to-all-start.4 = ((bf16[16,16,1024]{2,1,0:T(8,128)(2,1)}), bf16[16,16,1024]{2,1,0:T(8,128)(2,1)S(1)}, u32[]{:S(2)}, u32[]{:S(2)}) async-start(bf16[16,16,1024]{2,1,0:T(8,128)(2,1)} %constant_dynamic-update-slice_fusion), calls=%async_computation.4 | async-start | bytes 1048576 | tf_op jit(solution)/shard_map/all_to_all | solution.py:107
  158.7 6.4 %psum.7 = f32[1,1024]{1,0:T(1,128)} all-reduce(f32[1,1024]{1,0:T(1,128)S(1)} %bitcast.162), channel_id=1, replica_groups=mesh['dp'=4,'pipe'=16,'tensor'=8] {'dp'}, use_global_device_ids=true, to_apply=%region_11.12 | all-reduce | flops 1024 | bytes 8192 | tf_op jit(solution)/shard_map/psum | solution.py:91
  165.1 21.2 %all-to-all-done.4 = bf16[16,16,1024]{2,1,0:T(8,128)(2,1)S(1)} async-done(((bf16[16,16,1024]{2,1,0:T(8,128)(2,1)}), bf16[16,16,1024]{2,1,0:T(8,128)(2,1)S(1)}, u32[]{:S(2)}, u32[]{:S(2)}) %all-to-all-start.4) | async-done | bytes 524320 | tf_op jit(solution)/shard_map/all_to_all | solution.py:107
  186.3 0.0 reduce-scatter.2.cloned.1.call-done
  186.3 0.8 copy.64
  (15 shorter events, 0.2 us)
Async XLA Ops:
  7.2 11.4 %copy-start = (bf16[1,1,256,128]{3,2,1,0:T(8,128)(2,1)S(1)}, bf16[1,1,256,128]{3,2,1,0:T(8,128)(2,1)}, u32[]{:S(2)}) copy-start(bf16[1,1,256,128]{3,2,1,0:T(8,128)(2,1)} %param.12) | copy-start | bytes 196612
  7.2 10.8 %copy-start.2 = (bf16[1,1,256,1024]{3,2,1,0:T(8,128)(2,1)S(1)}, bf16[1,1,256,1024]{3,2,1,0:T(8,128)(2,1)}, u32[]{:S(2)}) copy-start(bf16[1,1,256,1024]{3,2,1,0:T(8,128)(2,1)} %param.14) | copy-start | bytes 1572868
  7.2 11.0 %copy-start.5 = (s32[1,4]{1,0:T(1,128)S(1)}, s32[1,4]{1,0:T(1,128)}, u32[]{:S(2)}) copy-start(s32[1,4]{1,0:T(1,128)} %param.17) | copy-start | bytes 52
  7.2 69.7 %all-gather.3.cloned.1.call-start = ((), (), s32[]{:S(2)}) async-start(), calls=%async_computation.7 | async-start | bytes 5242880 | tf_op jit(solution)/shard_map/all_gather | solution.py:70
  9.8 14.6 %all-to-all-start.1 = ((f32[8,2,128]{2,1,0:T(2,128)}), f32[8,2,128]{2,1,0:T(2,128)S(1)}, u32[]{:S(2)}, u32[]{:S(2)}) async-start(f32[8,2,128]{2,1,0:T(2,128)} %broadcast_in_dim.56), calls=%async_computation.1 | async-start | bytes 16384 | tf_op jit(solution)/shard_map/all_to_all | solution.py:55
  19.5 0.8 copy-start.4
  25.4 22.6 %copy-start.1 = (bf16[1,1,256,1024]{3,2,1,0:T(8,128)(2,1)S(1)}, bf16[1,1,256,1024]{3,2,1,0:T(8,128)(2,1)}, u32[]{:S(2)}) copy-start(bf16[1,1,256,1024]{3,2,1,0:T(8,128)(2,1)} %param.9) | copy-start | bytes 1572868
  25.4 22.6 %copy-start.3 = (f32[1,1024]{1,0:T(1,128)S(1)}, f32[1,1024]{1,0:T(1,128)}, u32[]{:S(2)}) copy-start(f32[1,1024]{1,0:T(1,128)} %param.10) | copy-start | bytes 12292
  25.4 22.5 %all-to-all-start = ((bf16[8,256,256]{2,1,0:T(8,128)(2,1)}), bf16[8,256,256]{2,1,0:T(8,128)(2,1)S(1)}, u32[]{:S(2)}, u32[]{:S(2)}) async-start(bf16[8,256,256]{2,1,0:T(8,128)(2,1)} %broadcast_in_dim.54), calls=%async_computation | async-start | bytes 2097152 | tf_op jit(solution)/shard_map/all_to_all | solution.py:83
  30.7 155.6 %reduce-scatter.2.cloned.1.call-start = ((), (), s32[]{:S(2)}) async-start(), calls=%async_computation.6 | async-start | bytes 5242880 | tf_op jit(solution)/shard_map/reduce_scatter | solution.py:95
  96.4 42.3 %all-to-all-start.3 = ((bf16[16,16,1024]{2,1,0:T(8,128)(2,1)}), bf16[16,16,1024]{2,1,0:T(8,128)(2,1)S(1)}, u32[]{:S(2)}, u32[]{:S(2)}) async-start(bf16[16,16,1024]{2,1,0:T(8,128)(2,1)} %bitcast.40), calls=%async_computation.3 | async-start | bytes 1048576 | tf_op jit(solution)/shard_map/all_to_all | solution.py:90
  151.9 34.4 %all-to-all-start.4 = ((bf16[16,16,1024]{2,1,0:T(8,128)(2,1)}), bf16[16,16,1024]{2,1,0:T(8,128)(2,1)S(1)}, u32[]{:S(2)}, u32[]{:S(2)}) async-start(bf16[16,16,1024]{2,1,0:T(8,128)(2,1)} %constant_dynamic-update-slice_fusion), calls=%async_computation.4 | async-start | bytes 1048576 | tf_op jit(solution)/shard_map/all_to_all | solution.py:107
Sparse Core Ops, SparseCore 0:
  10.1 66.7 all-gather.2
  80.3 57.1 reduce-scatter.1

commit v2 on v1

v2 whole, which is shorter than its diff:
```python
import functools

import jax
import jax.numpy as jnp
from jax import lax
from jax.experimental import pallas as pl
from jax.experimental.pallas import tpu as pltpu
from jax.sharding import PartitionSpec as P

D = 8192
H = 64
KVH = 8
HD = 128
GROUP = H // KVH
EPSILON = 1e-05
EXTRA = 16
LOG2E = 1.4426950408889634
F32 = jnp.float32
BF16 = jnp.bfloat16
VMEM = pl.BlockSpec(memory_space=pltpu.VMEM)
SMEM = pl.BlockSpec(memory_space=pltpu.SMEM)
ANY = pl.BlockSpec(memory_space=pl.ANY)
MIB = 1024 * 1024
PARAMS = pltpu.CompilerParams(vmem_limit_bytes=20 * MIB)
WHOLE = pltpu.CompilerParams(vmem_limit_bytes=60 * MIB)


def nt(a, b):
    return lax.dot_general(a, b, (((1,), (1,)), ((), ())), preferred_element_type=F32)


def tn(a, b):
    return lax.dot_general(a, b, (((0,), (0,)), ((), ())), preferred_element_type=F32)


def nn(a, b):
    return jnp.dot(a, b, preferred_element_type=F32)


def to_row(column):
    size = column.shape[0]
    across = lax.broadcasted_iota(jnp.int32, (size, size), 0)
    down = lax.broadcasted_iota(jnp.int32, (size, size), 1)
    return jnp.sum(jnp.where(across == down, column, 0.0), axis=0, keepdims=True)


def to_column(row):
    size = row.shape[1]
    across = lax.broadcasted_iota(jnp.int32, (size, size), 0)
    down = lax.broadcasted_iota(jnp.int32, (size, size), 1)
    return jnp.sum(jnp.where(across == down, row, 0.0), axis=1, keepdims=True)


def in_three_rows(row):
    high = row.astype(BF16).astype(F32)
    middle = (row - high).astype(BF16).astype(F32)
    low = row - high - middle
    place = lax.broadcasted_iota(jnp.int32, (EXTRA, row.shape[1]), 0)
    rows = jnp.where(place == 0, high, jnp.where(place == 1, middle, jnp.where(place == 2, low, 0.0)))
    return rows.astype(BF16)


def attention_kernel(lengths, query, key, value, out_grad, inputs, out, *scratch):
    query_v, key_v, value_v, grad_v, inputs_v, result, sems, out_sems = scratch
    tokens = query.shape[0]
    loads = [pltpu.make_async_copy(key, key_v, sems.at[0]), pltpu.make_async_copy(value, value_v, sems.at[1])]
    step = 2 * HD
    for part in range(GROUP // 2):
        span = pl.ds(part * step, step)
        loads.append(pltpu.make_async_copy(query.at[:, span], query_v.at[:, span], sems.at[2 + 2 * part]))
        loads.append(pltpu.make_async_copy(out_grad.at[:, span], grad_v.at[:, span], sems.at[3 + 2 * part]))
    loads.append(pltpu.make_async_copy(inputs, inputs_v, sems.at[2 + GROUP]))
    for load in loads:
        load.start()
    key_place = lax.broadcasted_iota(jnp.int32, (tokens, tokens), 0)
    query_place = lax.broadcasted_iota(jnp.int32, (tokens, tokens), 1)
    allowed = key_place <= query_place
    bound = 0
    for index in range(lengths.shape[1]):
        bound = bound + lengths[0, index]
        allowed &= (key_place >= bound) == (query_place >= bound)
    bias = jnp.where(allowed, 0.0, -1e30)
    factor = HD ** (-0.5)
    loads[0].wait()
    loads[1].wait()
    keys, values = key_v[...], value_v[...]
    grad_keys = jnp.zeros((tokens, HD), F32)
    grad_values = jnp.zeros((tokens, HD), F32)
    for head in range(GROUP):
        if head % 2 == 0:
            loads[2 + head].wait()
            loads[3 + head].wait()
        columns = slice(head * HD, (head + 1) * HD)
        rows, grads = query_v[:, columns], grad_v[:, columns]
        scores = nt(keys, rows) + bias
        top = jnp.max(scores, axis=0, keepdims=True)
        expos = jnp.exp2((scores - top) * (factor * LOG2E))
        probs = expos * (1.0 / jnp.sum(expos, axis=0, keepdims=True))
        grad_values += nn(probs.astype(BF16), grads)
        grad_probs = nt(values, grads)
        centre = jnp.sum(probs * grad_probs, axis=0, keepdims=True)
        grad_scores = (probs * ((grad_probs - centre) * factor)).astype(BF16)
        grad_keys += nn(grad_scores, rows)
    loads[2 + GROUP].wait()
    wide = inputs_v[...].astype(F32)
    extra = in_three_rows(to_row(jnp.sum(wide * wide, axis=1, keepdims=True)))
    grad_keys, grad_values = grad_keys.astype(BF16), grad_values.astype(BF16)
    result[:tokens, :HD] = grad_keys
    result[:tokens, HD:] = grad_values
    result[tokens:, :] = extra
    stores = [
        pltpu.make_async_copy(result, out.at[copy], out_sems.at[copy])
        for copy in range(out.shape[0])
    ]
    for store in stores:
        store.start()
    for store in stores:
        store.wait()


def project_kernel(order, grad_kv, *refs):
    pieces, (rows, gain), outs = refs[:4], refs[4:6], refs[6:11]
    mine, for_near, for_far, scaled_out, prods = outs
    inverse_out = refs[11]
    tokens, width = rows.shape
    half = width // 2
    sums = jnp.zeros((EXTRA, tokens), F32)
    for block in range(grad_kv.shape[0]):
        sums = sums + grad_kv[block, tokens:, :].astype(F32)
    inverse = to_column(1.0 / jnp.sqrt(jnp.sum(sums, axis=0, keepdims=True) * (1.0 / D) + EPSILON))
    inverse_out[...] = inverse
    places = ((mine, 0), (for_near, 0), (for_far, 0), (for_far, 1))
    for place, (target, slot) in enumerate(places):
        for part in range(2):
            span = slice(part * 2 * HD, (part + 1) * 2 * HD)
            target[slot, :tokens, span] = grad_kv[order[2 * place + part], :tokens, :]
        target[slot, tokens:, :] = jnp.zeros((EXTRA, half), BF16)
    total = None
    for (target, slot), piece in zip(places, pieces):
        term = nn(target[slot, :tokens, :], piece[...])
        total = term if total is None else total + term
    unit = rows[...].astype(F32) * inverse
    scaled = total * gain[...]
    scaled_out[...] = scaled
    normed = (unit * gain[...]).astype(BF16)
    gains = in_three_rows(jnp.sum(total * unit, axis=0, keepdims=True))
    for target, slot in ((mine, 1), (for_near, 1), (for_far, 2)):
        for part in range(2):
            span = slice(part * half, (part + 1) * half)
            target[slot + part, :tokens, :] = normed[:, span]
            target[slot + part, tokens:, :] = gains[:, span]
    sums = to_row(jnp.sum(scaled * unit, axis=1, keepdims=True))
    for copy in range(prods.shape[0]):
        prods[copy] = sums


def contrib_kernel(prods, scaled, rows, inverse, out):
    mean = to_column(jnp.sum(prods[...], axis=0) * (1.0 / D))
    scale = inverse[...]
    unit = rows[...].astype(F32) * scale
    out[...] = ((scaled[...] - unit * mean) * scale).astype(BF16)


def term_kernel(scale, mine, near, far, diagonal, out, gain_out):
    tokens = mine.shape[1] - EXTRA
    half = mine.shape[2]
    sources = ((mine, 0, 1), (near, 0, 1), (far, 0, 2), (diagonal, 0, 1))
    for part in range(2):
        span = slice(part * half, (part + 1) * half)
        total = None
        sums = []
        for source, share, normed in sources:
            term = tn(source[share, :tokens, :], source[normed + part, :tokens, :])
            term = (term * scale).astype(BF16).astype(F32)
            total = term if total is None else total + term
            extra = source[normed + part, tokens:, :].astype(F32)
            sums.append(jnp.sum(extra, axis=0, keepdims=True))
        out[:, span] = total.astype(BF16)
        gain_out[:, span] = ((sums[0] + sums[1]) + (sums[2] + sums[3])) * scale


def suffix_kernel(parts, above, out):
    total = above[...].astype(F32)
    for part in reversed(range(parts.shape[0])):
        total = total + parts[part].astype(F32)
        out[part] = total.astype(BF16)


def swap(value, axis, distance):
    count = lax.axis_size(axis)
    return lax.ppermute(value, axis, [(source, source ^ distance) for source in range(count)])


def body(
    inputs,
    norm_gain,
    queries,
    saved_keys,
    saved_values,
    attn_out_grad,
    kv_projection,
    top_grad,
    doc_lengths,
):
    tensor, sections, dp = lax.axis_size("tensor"), lax.axis_size("pipe"), lax.axis_size("dp")
    rows = inputs[0, 0]
    tokens, width = rows.shape
    mine, stage = lax.axis_index("dp"), lax.axis_index("pipe")

    own = kv_projection[0]
    far = swap(own, "dp", 2)
    near = swap(own, "dp", 1)

    copies = pl.pallas_call(
        attention_kernel,
        out_shape=jax.ShapeDtypeStruct((tensor, tokens + EXTRA, 2 * HD), BF16),
        in_specs=[SMEM] + [ANY] * 5,
        out_specs=ANY,
        scratch_shapes=[
            pltpu.VMEM((tokens, GROUP * HD), BF16),
            pltpu.VMEM((tokens, HD), BF16),
            pltpu.VMEM((tokens, HD), BF16),
            pltpu.VMEM((tokens, GROUP * HD), BF16),
            pltpu.VMEM((tokens, width), BF16),
            pltpu.VMEM((tokens + EXTRA, 2 * HD), BF16),
            pltpu.SemaphoreType.DMA((3 + GROUP,)),
            pltpu.SemaphoreType.DMA((tensor,)),
        ],
        compiler_params=WHOLE,
    )(doc_lengths, queries[0, 0], saved_keys[0, 0], saved_values[0, 0], attn_out_grad[0, 0], rows)
    grad_kv = lax.all_to_all(copies, "tensor", 0, 0)
    far, grad_kv = lax.optimization_barrier((far, grad_kv))
    far_near = swap(far, "dp", 1)
    order = [2 * (mine ^ place) + part for place in range(dp) for part in range(2)]

    mixed = tokens + EXTRA
    own_set, for_near, for_far, scaled, prods, inverse = pl.pallas_call(
        project_kernel,
        out_shape=(
            jax.ShapeDtypeStruct((3, mixed, width // 2), BF16),
            jax.ShapeDtypeStruct((3, mixed, width // 2), BF16),
            jax.ShapeDtypeStruct((4, mixed, width // 2), BF16),
            jax.ShapeDtypeStruct((tokens, width), F32),
            jax.ShapeDtypeStruct((tensor, 1, tokens), F32),
            jax.ShapeDtypeStruct((tokens, 1), F32),
        ),
        in_specs=[SMEM] + [VMEM] * 7,
        out_specs=(VMEM,) * 6,
        compiler_params=PARAMS,
    )(jnp.stack(order).astype(jnp.int32), grad_kv, own, near, far, far_near, rows, norm_gain)
    prods = lax.all_to_all(prods, "tensor", 0, 0)

    near_set = swap(for_near, "dp", 1)
    far_set = swap(for_far, "dp", 2)

    def local(kernel, shape, *operands):
        return pl.pallas_call(
            kernel,
            out_shape=jax.ShapeDtypeStruct(shape, BF16),
            in_specs=[VMEM] * len(operands),
            out_specs=VMEM,
            compiler_params=PARAMS,
        )(*operands)

    prods, near_set = lax.optimization_barrier((prods, near_set))
    contrib = local(contrib_kernel, (tokens, width), prods, scaled, rows, inverse)
    small = tokens // sections
    own_top = lax.dynamic_slice_in_dim(top_grad[0], stage * small, small, 0)
    parts = lax.all_to_all(contrib.reshape(sections, small, width), "pipe", 0, 0)
    parts, far_set = lax.optimization_barrier((parts, far_set))
    diagonal_set = swap(far_set[1:], "dp", 1)
    suffixes = local(suffix_kernel, parts.shape, parts, own_top)
    section_grads = lax.all_to_all(suffixes, "pipe", 0, 0).reshape(tokens, width)
    kv_grad, gain_grad = pl.pallas_call(
        functools.partial(term_kernel, (dp * tokens) ** (-0.5)),
        out_shape=(
            jax.ShapeDtypeStruct((tensor // dp * 2 * HD, width), BF16),
            jax.ShapeDtypeStruct((1, width), F32),
        ),
        in_specs=[VMEM] * 4,
        out_specs=(VMEM, VMEM),
        compiler_params=PARAMS,
    )(own_set, near_set, far_set, diagonal_set)

    return (section_grads[None, None], kv_grad[None], gain_grad)


def solution(mesh):
    placed = (
        P("pipe", "dp", None, "tensor"),
        P("pipe", "tensor"),
        P("pipe", "dp", None, "tensor"),
        P("pipe", "dp", None, "tensor"),
        P("pipe", "dp", None, "tensor"),
        P("pipe", "dp", None, "tensor"),
        P("pipe", "dp", "tensor"),
        P("dp", None, "tensor"),
        P("dp", None),
    )
    return jax.shard_map(
        body,
        mesh=mesh,
        in_specs=placed,
        out_specs=(P("pipe", "dp", None, "tensor"), P("pipe", "dp", "tensor"), P("pipe", "tensor")),
        check_vma=False,
    )
```

time: 195 us -> 149 us (0.76)
  the two profiles are of different devices: /device:TPU:32 before, /device:TPU:64 now
where the time goes in v2:
time: 149 us; the launch traced here: 148 us
  waiting for transfers between devices  72.5 us (49%)
  starting transfers between devices  47.4 us (32%)
  Pallas kernels  13.8 us (9%)
  blocking collectives  11.9 us (8%)
  local copies, waits for them, and re-layouts  2.06 us (1%)
    ppermute x6, waiting for transfers between devices, swap(): lax.ppermute(value, axis, [(source, source ^ distance) for source in rang...  29.7 us
    all_to_all x1, waiting for transfers between devices, body(): grad_kv = lax.all_to_all(copies, 'tensor', 0, 0)  22.9 us
    all_to_all x1, waiting for transfers between devices, body(): lax.all_to_all(suffixes, 'pipe', 0, 0).reshape(tokens, width)  19.8 us
    all_to_all x1, starting transfers between devices, body(): lax.all_to_all(contrib.reshape(sections, small, width), 'pipe', 0, 0)  14.8 us
    ppermute x6, starting transfers between devices, swap(): lax.ppermute(value, axis, [(source, source ^ distance) for source in rang...  13.8 us
    all_to_all x1, starting transfers between devices, body(): lax.all_to_all(suffixes, 'pipe', 0, 0).reshape(tokens, width)  12.1 us
    all_to_all x1, blocking collectives, body(): prods = lax.all_to_all(prods, 'tensor', 0, 0)  11.9 us
    all_to_all x1, starting transfers between devices, body(): grad_kv = lax.all_to_all(copies, 'tensor', 0, 0)  6.78 us
  transfers between devices with their start and end apart: 9, of which 5 were waited for; matrix products, arithmetic and copies ran while one was open for 0% of the time, Pallas kernels for 6%

profile of v2, /device:TPU:64, one launch (start us, length us, event | category | flops | bytes accessed | tf_op | source)
XLA Modules:
  0.0 148.5 jit_solution(2576047026189550792)
XLA Ops:
  0.6 0.0 copy-start
  0.6 3.6 %collective-permute-start = (bf16[512,1024]{1,0:T(8,128)(2,1)}, bf16[512,1024]{1,0:T(8,128)(2,1)}, u32[]{:S(2)}, u32[]{:S(2)}) collective-permute-start(bf16[512,1024]{1,0:T(8,128)(2,1)} %bitcast.22), channel_id=1, source_target_pairs={{0,256},{128,384},{256,0},{384,128},{1,257},{129,385},{257,1},{385... | collective-permute-start | bytes 3145736 | tf_op jit(solution)/shard_map/ppermute | solution.py:191
  4.3 6.2 %shard_map.112 = bf16[8,272,256]{2,1,0:T(8,128)(2,1)} custom-call(s32[1,4]{1,0:T(1,128)} %lengths.1, bf16[256,1024]{1,0:T(8,128)(2,1)} %bitcast.25, bf16[256,128]{1,0:T(8,128)(2,1)} %bitcast.27, bf16[256,128]{1,0:T(8,128)(2,1)} %bitcast.28, bf16[256,1024]{1,0:T(8,128)(2,1)} %bitcast.26, bf16[256,1024]{1,0:T(8,128)(2,1)} %bitcast.19), custom_call_target="tpu_custom_call" | custom-call | tf_op jit(solution)/shard_map/pallas_call | solution.py:214
  10.5 0.0 copy-start.2
  10.5 0.0 copy-start.1
  10.5 0.0 copy-start.5
  10.5 6.8 %all-to-all-start = ((bf16[8,272,256]{2,1,0:T(8,128)(2,1)}), bf16[8,272,256]{2,1,0:T(8,128)(2,1)S(1)}, u32[]{:S(2)}, u32[]{:S(2)}) async-start(bf16[8,272,256]{2,1,0:T(8,128)(2,1)} %shard_map.112), calls=%async_computation | async-start | bytes 2228224 | tf_op jit(solution)/shard_map/all_to_all | solution.py:231
  17.3 0.0 copy-done.2
  17.3 1.9 %collective-permute-start.1 = (bf16[512,1024]{1,0:T(8,128)(2,1)S(1)}, bf16[512,1024]{1,0:T(8,128)(2,1)}, u32[]{:S(2)}, u32[]{:S(2)}) collective-permute-start(bf16[512,1024]{1,0:T(8,128)(2,1)S(1)} %bitcast.23), channel_id=1, source_target_pairs={{0,128},{128,0},{256,384},{384,256},{1,129},{129,1},{257,385},{385... | collective-permute-start | bytes 3145736 | tf_op jit(solution)/shard_map/ppermute | solution.py:191
  19.2 22.9 %all-to-all-done.grad_kv = bf16[8,272,256]{2,1,0:T(8,128)(2,1)S(1)} async-done(((bf16[8,272,256]{2,1,0:T(8,128)(2,1)}), bf16[8,272,256]{2,1,0:T(8,128)(2,1)S(1)}, u32[]{:S(2)}, u32[]{:S(2)}) %all-to-all-start) | async-done | bytes 1114144 | tf_op jit(solution)/shard_map/all_to_all | solution.py:231
  42.2 0.0 collective-permute-done.refs_2_
  42.2 1.9 %collective-permute-start.2 = (bf16[512,1024]{1,0:T(8,128)(2,1)}, bf16[512,1024]{1,0:T(8,128)(2,1)}, u32[]{:S(2)}, u32[]{:S(2)}) collective-permute-start(bf16[512,1024]{1,0:T(8,128)(2,1)} %collective-permute-done.refs_2_), channel_id=1, source_target_pairs={{0,128},{128,0},{256,384},{384,256},{1,129},{129,1},{257,385},{385... | collective-permute-start | bytes 3145736 | tf_op jit(solution)/shard_map/ppermute | solution.py:191
  44.1 0.1 stack.35.order
  44.2 0.0 collective-permute-done.1.refs_1_
  44.2 2.9 %collective-permute-done.2.refs_3_ = bf16[512,1024]{1,0:T(8,128)(2,1)} collective-permute-done((bf16[512,1024]{1,0:T(8,128)(2,1)}, bf16[512,1024]{1,0:T(8,128)(2,1)}, u32[]{:S(2)}, u32[]{:S(2)}) %collective-permute-start.2) | collective-permute-done | bytes 1048608 | tf_op jit(solution)/shard_map/ppermute | solution.py:191
  47.1 0.0 copy-done.1
  47.1 0.0 copy-done.5
  47.1 3.3 %shard_map.113 = (bf16[3,272,512]{2,1,0:T(8,128)(2,1)S(1)}, bf16[3,272,512]{2,1,0:T(8,128)(2,1)S(1)}, bf16[4,272,512]{2,1,0:T(8,128)(2,1)S(1)}, f32[256,1024]{1,...) custom-call(s32[8]{0:T(128)S(1)} %stack.35.order, bf16[8,272,256]{2,1,0:T(8,128)(2,1)S(1)} %all-to-all-done.grad_kv, ...), custom_call_target="tpu_custom_call" | custom-call | tf_op jit(solution)/shard_map/pallas_call | solution.py:237
  50.4 0.0 copy-start.3
  50.4 0.0 copy-start.6
  50.4 2.0 %collective-permute-start.3 = (bf16[3,272,512]{2,1,0:T(8,128)(2,1)S(1)}, bf16[3,272,512]{2,1,0:T(8,128)(2,1)S(1)}, u32[]{:S(2)}, u32[]{:S(2)}) collective-permute-start(bf16[3,272,512]{2,1,0:T(8,128)(2,1)S(1)} %get-tuple-element.20), channel_id=1, source_target_pairs={{0,128},{128,0},{256,384},{384,256},{1,129},{129,1},{257,385},{385... | collective-permute-start | bytes 2506760 | tf_op jit(solution)/shard_map/ppermute | solution.py:191
  52.4 11.9 %all_to_all.20.prods = f32[8,1,256]{2,1,0:T(1,128)S(1)} all-to-all(f32[8,1,256]{2,1,0:T(1,128)S(1)} %get-tuple-element.19), channel_id=1, replica_groups=mesh['dp'=4,'pipe'=16,'tensor'=8] {'tensor'}, dimensions={0} | all-to-all | bytes 16384 | tf_op jit(solution)/shard_map/all_to_all | solution.py:251
  64.3 0.0 collective-permute-done.3.near
  64.3 1.1 shard_map.114
  65.4 0.0 copy-done.3
  65.4 0.0 copy-done.6
  65.4 14.8 %all-to-all-start.2 = ((bf16[16,16,1024]{2,1,0:T(8,128)(2,1)}), bf16[16,16,1024]{2,1,0:T(8,128)(2,1)S(1)}, u32[]{:S(2)}, u32[]{:S(2)}) async-start(bf16[16,16,1024]{2,1,0:T(8,128)(2,1)} %bitcast.14), calls=%async_computation.2 | async-start | bytes 1048576 | tf_op jit(solution)/shard_map/all_to_all | solution.py:269
  80.2 2.3 %collective-permute-start.4 = (bf16[4,272,512]{2,1,0:T(8,128)(2,1)}, bf16[4,272,512]{2,1,0:T(8,128)(2,1)S(1)}, u32[]{:S(2)}, u32[]{:S(2)}) collective-permute-start(bf16[4,272,512]{2,1,0:T(8,128)(2,1)} %copy-done.6), channel_id=1, source_target_pairs={{0,256},{128,384},{256,0},{384,128},{1,257},{129,385},{257,1},{385... | collective-permute-start | bytes 3342344 | tf_op jit(solution)/shard_map/ppermute | solution.py:191
  82.5 0.0 copy-done
  82.6 24.5 %collective-permute-done.4.far = bf16[4,272,512]{2,1,0:T(8,128)(2,1)S(1)} collective-permute-done((bf16[4,272,512]{2,1,0:T(8,128)(2,1)}, bf16[4,272,512]{2,1,0:T(8,128)(2,1)S(1)}, u32[]{:S(2)}, u32[]{:S(2)}) %collective-permute-start.4) | collective-permute-done | bytes 1114144 | tf_op jit(solution)/shard_map/ppermute | solution.py:191
  107.1 0.0 all-to-all-done.2.parts
  107.1 0.9 shard_map.115
  108.0 0.0 copy-start.4
  108.0 12.1 %all-to-all-start.3 = ((bf16[16,16,1024]{2,1,0:T(8,128)(2,1)}), bf16[16,16,1024]{2,1,0:T(8,128)(2,1)}, u32[]{:S(2)}, u32[]{:S(2)}) async-start(bf16[16,16,1024]{2,1,0:T(8,128)(2,1)} %shard_map.115), calls=%async_computation.3 | async-start | bytes 1048576 | tf_op jit(solution)/shard_map/all_to_all | solution.py:273
  120.2 0.1 slice.3
  120.2 1.9 %collective-permute-start.5 = (bf16[3,272,512]{2,1,0:T(8,128)(2,1)S(1)}, bf16[3,272,512]{2,1,0:T(8,128)(2,1)S(1)}, u32[]{:S(2)}, u32[]{:S(2)}) collective-permute-start(bf16[3,272,512]{2,1,0:T(8,128)(2,1)S(1)} %slice.3), channel_id=1, source_target_pairs={{0,128},{128,0},{256,384},{384,256},{1,129},{129,1},{257,385},{385... | collective-permute-start | bytes 2506760 | tf_op jit(solution)/shard_map/ppermute | solution.py:191
  122.2 2.3 %collective-permute-done.5.diagonal = bf16[3,272,512]{2,1,0:T(8,128)(2,1)S(1)} collective-permute-done((bf16[3,272,512]{2,1,0:T(8,128)(2,1)S(1)}, bf16[3,272,512]{2,1,0:T(8,128)(2,1)S(1)}, u32[]{:S(2)}, u32[]{:S(2)}) %collective-permute-start.5) | collective-permute-done | bytes 835616 | tf_op jit(solution)/shard_map/ppermute | solution.py:191
  124.5 0.0 copy-done.4
  124.5 2.3 %shard_map.116 = (bf16[512,1024]{1,0:T(8,128)(2,1)}, f32[1,1024]{1,0:T(1,128)}) custom-call(bf16[3,272,512]{2,1,0:T(8,128)(2,1)S(1)} %copy-done.4, bf16[3,272,512]{2,1,0:T(8,128)(2,1)S(1)} %collective-permute-done.3.near, bf16[4,272,512]{2,1,0:T(8,128)(2,1)S(1)} %collective-permute-done.4.far, bf16[3,272,512]{2,1,0:T(8,128)(2,1)S(1)} %collective-permute-done.5.diagonal), custom_call_target="tpu_custom_call" | custom-call | tf_op jit(solution)/shard_map/pallas_call | solution.py:274
  126.8 19.8 %all-to-all-done.3 = bf16[16,16,1024]{2,1,0:T(8,128)(2,1)} async-done(((bf16[16,16,1024]{2,1,0:T(8,128)(2,1)}), bf16[16,16,1024]{2,1,0:T(8,128)(2,1)}, u32[]{:S(2)}, u32[]{:S(2)}) %all-to-all-start.3) | async-done | bytes 524320 | tf_op jit(solution)/shard_map/all_to_all | solution.py:273
  146.6 1.9 %copy.13 = bf16[1,1,256,1024]{3,2,1,0:T(8,128)(2,1)} copy(bf16[1,1,256,1024]{3,2,1,0:T(8,128)(2,1)} %bitcast.16) | data formatting | bytes 1048576
  (1 shorter events, 0.0 us)
Async XLA Ops:
  0.6 81.9 %copy-start = (bf16[1,256,1024]{2,1,0:T(8,128)(2,1)S(1)}, bf16[1,256,1024]{2,1,0:T(8,128)(2,1)}, u32[]{:S(2)}) copy-start(bf16[1,256,1024]{2,1,0:T(8,128)(2,1)} %param.16) | copy-start | bytes 1572868
  0.6 41.5 %collective-permute-start = (bf16[512,1024]{1,0:T(8,128)(2,1)}, bf16[512,1024]{1,0:T(8,128)(2,1)}, u32[]{:S(2)}, u32[]{:S(2)}) collective-permute-start(bf16[512,1024]{1,0:T(8,128)(2,1)} %bitcast.22), channel_id=1, source_target_pairs={{0,256},{128,384},{256,0},{384,128},{1,257},{129,385},{257,1},{385... | collective-permute-start | bytes 3145736 | tf_op jit(solution)/shard_map/ppermute | solution.py:191
  10.5 6.8 %copy-start.2 = (bf16[1,512,1024]{2,1,0:T(8,128)(2,1)S(1)}, bf16[1,512,1024]{2,1,0:T(8,128)(2,1)}, u32[]{:S(2)}) copy-start(bf16[1,512,1024]{2,1,0:T(8,128)(2,1)} %param.15) | copy-start | bytes 3145732
  10.5 36.6 %copy-start.1 = (bf16[1,1,256,1024]{3,2,1,0:T(8,128)(2,1)S(1)}, bf16[1,1,256,1024]{3,2,1,0:T(8,128)(2,1)}, u32[]{:S(2)}) copy-start(bf16[1,1,256,1024]{3,2,1,0:T(8,128)(2,1)} %param.9) | copy-start | bytes 1572868
  10.5 36.5 %copy-start.5 = (f32[1,1024]{1,0:T(1,128)S(1)}, f32[1,1024]{1,0:T(1,128)}, u32[]{:S(2)}) copy-start(f32[1,1024]{1,0:T(1,128)} %refs_5_.1) | copy-start | bytes 12292
  10.5 31.6 %all-to-all-start = ((bf16[8,272,256]{2,1,0:T(8,128)(2,1)}), bf16[8,272,256]{2,1,0:T(8,128)(2,1)S(1)}, u32[]{:S(2)}, u32[]{:S(2)}) async-start(bf16[8,272,256]{2,1,0:T(8,128)(2,1)} %shard_map.112), calls=%async_computation | async-start | bytes 2228224 | tf_op jit(solution)/shard_map/all_to_all | solution.py:231
  17.3 26.9 %collective-permute-start.1 = (bf16[512,1024]{1,0:T(8,128)(2,1)S(1)}, bf16[512,1024]{1,0:T(8,128)(2,1)}, u32[]{:S(2)}, u32[]{:S(2)}) collective-permute-start(bf16[512,1024]{1,0:T(8,128)(2,1)S(1)} %bitcast.23), channel_id=1, source_target_pairs={{0,128},{128,0},{256,384},{384,256},{1,129},{129,1},{257,385},{385... | collective-permute-start | bytes 3145736 | tf_op jit(solution)/shard_map/ppermute | solution.py:191
  42.2 4.9 %collective-permute-start.2 = (bf16[512,1024]{1,0:T(8,128)(2,1)}, bf16[512,1024]{1,0:T(8,128)(2,1)}, u32[]{:S(2)}, u32[]{:S(2)}) collective-permute-start(bf16[512,1024]{1,0:T(8,128)(2,1)} %collective-permute-done.refs_2_), channel_id=1, source_target_pairs={{0,128},{128,0},{256,384},{384,256},{1,129},{129,1},{257,385},{385... | collective-permute-start | bytes 3145736 | tf_op jit(solution)/shard_map/ppermute | solution.py:191
  50.4 15.1 %copy-start.3 = (bf16[3,272,512]{2,1,0:T(8,128)(2,1)}, bf16[3,272,512]{2,1,0:T(8,128)(2,1)S(1)}, u32[]{:S(2)}) copy-start(bf16[3,272,512]{2,1,0:T(8,128)(2,1)S(1)} %get-tuple-element.26.mine) | copy-start | bytes 2506756
  50.4 15.1 %copy-start.6 = (bf16[4,272,512]{2,1,0:T(8,128)(2,1)}, bf16[4,272,512]{2,1,0:T(8,128)(2,1)S(1)}, u32[]{:S(2)}) copy-start(bf16[4,272,512]{2,1,0:T(8,128)(2,1)S(1)} %get-tuple-element.24) | copy-start | bytes 3342340
  50.4 13.9 %collective-permute-start.3 = (bf16[3,272,512]{2,1,0:T(8,128)(2,1)S(1)}, bf16[3,272,512]{2,1,0:T(8,128)(2,1)S(1)}, u32[]{:S(2)}, u32[]{:S(2)}) collective-permute-start(bf16[3,272,512]{2,1,0:T(8,128)(2,1)S(1)} %get-tuple-element.20), channel_id=1, source_target_pairs={{0,128},{128,0},{256,384},{384,256},{1,129},{129,1},{257,385},{385... | collective-permute-start | bytes 2506760 | tf_op jit(solution)/shard_map/ppermute | solution.py:191
  65.4 41.7 %all-to-all-start.2 = ((bf16[16,16,1024]{2,1,0:T(8,128)(2,1)}), bf16[16,16,1024]{2,1,0:T(8,128)(2,1)S(1)}, u32[]{:S(2)}, u32[]{:S(2)}) async-start(bf16[16,16,1024]{2,1,0:T(8,128)(2,1)} %bitcast.14), calls=%async_computation.2 | async-start | bytes 1048576 | tf_op jit(solution)/shard_map/all_to_all | solution.py:269
  80.2 26.9 %collective-permute-start.4 = (bf16[4,272,512]{2,1,0:T(8,128)(2,1)}, bf16[4,272,512]{2,1,0:T(8,128)(2,1)S(1)}, u32[]{:S(2)}, u32[]{:S(2)}) collective-permute-start(bf16[4,272,512]{2,1,0:T(8,128)(2,1)} %copy-done.6), channel_id=1, source_target_pairs={{0,256},{128,384},{256,0},{384,128},{1,257},{129,385},{257,1},{385... | collective-permute-start | bytes 3342344 | tf_op jit(solution)/shard_map/ppermute | solution.py:191
  108.0 16.5 %copy-start.4 = (bf16[3,272,512]{2,1,0:T(8,128)(2,1)S(1)}, bf16[3,272,512]{2,1,0:T(8,128)(2,1)}, u32[]{:S(2)}) copy-start(bf16[3,272,512]{2,1,0:T(8,128)(2,1)} %copy-done.3) | copy-start | bytes 2506756
  108.0 38.6 %all-to-all-start.3 = ((bf16[16,16,1024]{2,1,0:T(8,128)(2,1)}), bf16[16,16,1024]{2,1,0:T(8,128)(2,1)}, u32[]{:S(2)}, u32[]{:S(2)}) async-start(bf16[16,16,1024]{2,1,0:T(8,128)(2,1)} %shard_map.115), calls=%async_computation.3 | async-start | bytes 1048576 | tf_op jit(solution)/shard_map/all_to_all | solution.py:273
  120.2 4.2 %collective-permute-start.5 = (bf16[3,272,512]{2,1,0:T(8,128)(2,1)S(1)}, bf16[3,272,512]{2,1,0:T(8,128)(2,1)S(1)}, u32[]{:S(2)}, u32[]{:S(2)}) collective-permute-start(bf16[3,272,512]{2,1,0:T(8,128)(2,1)S(1)} %slice.3), channel_id=1, source_target_pairs={{0,128},{128,0},{256,384},{384,256},{1,129},{129,1},{257,385},{385... | collective-permute-start | bytes 2506760 | tf_op jit(solution)/shard_map/ppermute | solution.py:191

commit v3 on v2

--- a/solution.py
+++ b/solution.py
@@ -22,6 +22,7 @@
 ANY = pl.BlockSpec(memory_space=pl.ANY)
 MIB = 1024 * 1024
 PARAMS = pltpu.CompilerParams(vmem_limit_bytes=20 * MIB)
+SMALL = pltpu.CompilerParams(vmem_limit_bytes=12 * MIB)
 WHOLE = pltpu.CompilerParams(vmem_limit_bytes=60 * MIB)
 
 
@@ -118,10 +119,8 @@
         store.wait()
 
 
-def project_kernel(order, grad_kv, *refs):
-    pieces, (rows, gain), outs = refs[:4], refs[4:6], refs[6:11]
-    mine, for_near, for_far, scaled_out, prods = outs
-    inverse_out = refs[11]
+def gather_kernel(order, grad_kv, own, near, far, rows, gain, *outs):
+    mine, for_near, for_far, for_diagonal, total_out, inverse_out = outs
     tokens, width = rows.shape
     half = width // 2
     sums = jnp.zeros((EXTRA, tokens), F32)
@@ -129,26 +128,25 @@
         sums = sums + grad_kv[block, tokens:, :].astype(F32)
     inverse = to_column(1.0 / jnp.sqrt(jnp.sum(sums, axis=0, keepdims=True) * (1.0 / D) + EPSILON))
     inverse_out[...] = inverse
-    places = ((mine, 0), (for_near, 0), (for_far, 0), (for_far, 1))
-    for place, (target, slot) in enumerate(places):
+    for place, target in enumerate((mine, for_near, for_far, for_diagonal)):
         for part in range(2):
             span = slice(part * 2 * HD, (part + 1) * 2 * HD)
-            target[slot, :tokens, span] = grad_kv[order[2 * place + part], :tokens, :]
-        target[slot, tokens:, :] = jnp.zeros((EXTRA, half), BF16)
-    total = None
-    for (target, slot), piece in zip(places, pieces):
-        term = nn(target[slot, :tokens, :], piece[...])
-        total = term if total is None else total + term
-    unit = rows[...].astype(F32) * inverse
+            target[0, :, span] = grad_kv[order[2 * place + part], :tokens, :]
+    total_out[...] = (
+        nn(mine[0], own[...]) + nn(for_near[0], near[...]) + nn(for_far[0], far[...])
+    )
+    normed = (rows[...].astype(F32) * inverse * gain[...]).astype(BF16)
+    for target in (mine, for_near, for_far):
+        target[1] = normed[:, :half]
+        target[2] = normed[:, half:]
+
+
+def project_kernel(part, share, piece, rows, gain, inverse, scaled_out, prods, gains_out):
+    total = part[...] + nn(share[0], piece[...])
+    unit = rows[...].astype(F32) * inverse[...]
     scaled = total * gain[...]
     scaled_out[...] = scaled
-    normed = (unit * gain[...]).astype(BF16)
-    gains = in_three_rows(jnp.sum(total * unit, axis=0, keepdims=True))
-    for target, slot in ((mine, 1), (for_near, 1), (for_far, 2)):
-        for part in range(2):
-            span = slice(part * half, (part + 1) * half)
-            target[slot + part, :tokens, :] = normed[:, span]
-            target[slot + part, tokens:, :] = gains[:, span]
+    gains_out[...] = jnp.sum(total * unit, axis=0, keepdims=True)
     sums = to_row(jnp.sum(scaled * unit, axis=1, keepdims=True))
     for copy in range(prods.shape[0]):
         prods[copy] = sums
@@ -161,22 +159,16 @@
     out[...] = ((scaled[...] - unit * mean) * scale).astype(BF16)
 
 
-def term_kernel(scale, mine, near, far, diagonal, out, gain_out):
-    tokens = mine.shape[1] - EXTRA
+def term_kernel(scale, mine, near, far, share, diagonal, out):
     half = mine.shape[2]
-    sources = ((mine, 0, 1), (near, 0, 1), (far, 0, 2), (diagonal, 0, 1))
+    sources = ((mine, mine, 1), (near, near, 1), (far, far, 1), (share, diagonal, 0))
     for part in range(2):
-        span = slice(part * half, (part + 1) * half)
         total = None
-        sums = []
-        for source, share, normed in sources:
-            term = tn(source[share, :tokens, :], source[normed + part, :tokens, :])
+        for heads, source, normed in sources:
+            term = tn(heads[0], source[normed + part])
             term = (term * scale).astype(BF16).astype(F32)
             total = term if total is None else total + term
-            extra = source[normed + part, tokens:, :].astype(F32)
-            sums.append(jnp.sum(extra, axis=0, keepdims=True))
-        out[:, span] = total.astype(BF16)
-        gain_out[:, span] = ((sums[0] + sums[1]) + (sums[2] + sums[3])) * scale
+        out[:, part * half : (part + 1) * half] = total.astype(BF16)
 
 
 def suffix_kernel(parts, above, out):
@@ -184,6 +176,10 @@
     for part in reversed(range(parts.shape[0])):
         total = total + parts[part].astype(F32)
         out[part] = total.astype(BF16)
+
+
+def copy_kernel(source, out):
+    out[...] = source[...]
 
 
 def swap(value, axis, distance):
@@ -233,24 +229,37 @@
     far_near = swap(far, "dp", 1)
     order = [2 * (mine ^ place) + part for place in range(dp) for part in range(2)]
 
-    mixed = tokens + EXTRA
-    own_set, for_near, for_far, scaled, prods, inverse = pl.pallas_call(
+    def blocks(count):
+        return jax.ShapeDtypeStruct((count, tokens, width // 2), BF16)
+
+    wide = jax.ShapeDtypeStruct((tokens, width), F32)
+    own_set, for_near, for_far, for_diagonal, total, inverse = pl.pallas_call(
+        gather_kernel,
+        out_shape=(
+            blocks(3),
+            blocks(3),
+            blocks(3),
+            blocks(1),
+            wide,
+            jax.ShapeDtypeStruct((tokens, 1), F32),
+        ),
+        in_specs=[SMEM] + [VMEM] * 6,
+        out_specs=(VMEM,) * 6,
+        compiler_params=PARAMS,
+    )(jnp.stack(order).astype(jnp.int32), grad_kv, own, near, far, rows, norm_gain)
+    scaled, prods, gains = pl.pallas_call(
         project_kernel,
         out_shape=(
-            jax.ShapeDtypeStruct((3, mixed, width // 2), BF16),
-            jax.ShapeDtypeStruct((3, mixed, width // 2), BF16),
-            jax.ShapeDtypeStruct((4, mixed, width // 2), BF16),
-            jax.ShapeDtypeStruct((tokens, width), F32),
+            wide,
             jax.ShapeDtypeStruct((tensor, 1, tokens), F32),
-            jax.ShapeDtypeStruct((tokens, 1), F32),
+            jax.ShapeDtypeStruct((1, width), F32),
         ),
-        in_specs=[SMEM] + [VMEM] * 7,
-        out_specs=(VMEM,) * 6,
+        in_specs=[VMEM] * 6,
+        out_specs=(VMEM,) * 3,
         compiler_params=PARAMS,
-    )(jnp.stack(order).astype(jnp.int32), grad_kv, own, near, far, far_near, rows, norm_gain)
+    )(total, for_diagonal, far_near, rows, norm_gain, inverse)
     prods = lax.all_to_all(prods, "tensor", 0, 0)
 
-    near_set = swap(for_near, "dp", 1)
     far_set = swap(for_far, "dp", 2)
 
     def local(kernel, shape, *operands):
@@ -259,28 +268,29 @@
             out_shape=jax.ShapeDtypeStruct(shape, BF16),
             in_specs=[VMEM] * len(operands),
             out_specs=VMEM,
-            compiler_params=PARAMS,
+            compiler_params=SMALL,
         )(*operands)
 
-    prods, near_set = lax.optimization_barrier((prods, near_set))
     contrib = local(contrib_kernel, (tokens, width), prods, scaled, rows, inverse)
     small = tokens // sections
     own_top = lax.dynamic_slice_in_dim(top_grad[0], stage * small, small, 0)
     parts = lax.all_to_all(contrib.reshape(sections, small, width), "pipe", 0, 0)
-    parts, far_set = lax.optimization_barrier((parts, far_set))
+    parts, far_set, gains = lax.optimization_barrier((parts, far_set, gains))
+    near_set = swap(for_near, "dp", 1)
+    diagonal_share = swap(for_diagonal, "dp", 3)
     diagonal_set = swap(far_set[1:], "dp", 1)
     suffixes = local(suffix_kernel, parts.shape, parts, own_top)
     section_grads = lax.all_to_all(suffixes, "pipe", 0, 0).reshape(tokens, width)
-    kv_grad, gain_grad = pl.pallas_call(
-        functools.partial(term_kernel, (dp * tokens) ** (-0.5)),
-        out_shape=(
-            jax.ShapeDtypeStruct((tensor // dp * 2 * HD, width), BF16),
-            jax.ShapeDtypeStruct((1, width), F32),
-        ),
-        in_specs=[VMEM] * 4,
-        out_specs=(VMEM, VMEM),
-        compiler_params=PARAMS,
-    )(own_set, near_set, far_set, diagonal_set)
+    section_grads = local(copy_kernel, (tokens, width), section_grads)
+    scale = (dp * tokens) ** (-0.5)
+    kv_grad = pl.pallas_call(
+        functools.partial(term_kernel, scale),
+        out_shape=jax.ShapeDtypeStruct((tensor // dp * 2 * HD, width), BF16),
+        in_specs=[VMEM] * 5,
+        out_specs=VMEM,
+        compiler_params=SMALL,
+    )(own_set, near_set, far_set, diagonal_share, diagonal_set)
+    gain_grad = lax.psum(gains * scale, "dp")
 
     return (section_grads[None, None], kv_grad[None], gain_grad)
 

time: 149 us -> 141 us (0.946)
  the two profiles are of different devices: /device:TPU:64 before, /device:TPU:32 now
where the time goes in v3:
time: 141 us
  waiting for transfers between devices  54.6 us (39%)
  starting transfers between devices  44.9 us (32%)
  blocking collectives  22.7 us (16%)
  Pallas kernels  16 us (11%)
  local copies, waits for them, and re-layouts  1.55 us (1%)
    all_to_all x1, waiting for transfers between devices, body(): grad_kv = lax.all_to_all(copies, 'tensor', 0, 0)  22.9 us
    ppermute x7, waiting for transfers between devices, swap(): lax.ppermute(value, axis, [(source, source ^ distance) for source in rang...  17.5 us
    ppermute x7, starting transfers between devices, swap(): lax.ppermute(value, axis, [(source, source ^ distance) for source in rang...  16.1 us
    all_to_all x1, starting transfers between devices, body(): lax.all_to_all(contrib.reshape(sections, small, width), 'pipe', 0, 0)  15.2 us
    all_to_all x1, blocking collectives, body(): prods = lax.all_to_all(prods, 'tensor', 0, 0)  11.9 us
    psum x1, blocking collectives, body(): gain_grad = lax.psum(gains * scale, 'dp')  10.9 us
    all_to_all x1, waiting for transfers between devices, body(): lax.all_to_all(contrib.reshape(sections, small, width), 'pipe', 0, 0)  8.1 us
    all_to_all x1, starting transfers between devices, body(): lax.all_to_all(suffixes, 'pipe', 0, 0).reshape(tokens, width)  6.81 us
  transfers between devices with their start and end apart: 10, of which 4 were waited for; matrix products, arithmetic and copies ran while one was open for 1% of the time, Pallas kernels for 9%

profile of v3, /device:TPU:32, one launch (start us, length us, event | category | flops | bytes accessed | tf_op | source)
XLA Modules:
  0.0 140.5 jit_solution(15462163170534050622)
XLA Ops:
  0.6 0.0 copy-start
  0.6 3.6 %collective-permute-start = (bf16[512,1024]{1,0:T(8,128)(2,1)}, bf16[512,1024]{1,0:T(8,128)(2,1)}, u32[]{:S(2)}, u32[]{:S(2)}) collective-permute-start(bf16[512,1024]{1,0:T(8,128)(2,1)} %bitcast.8.own), channel_id=1, source_target_pairs={{0,256},{128,384},{256,0},{384,128},{1,257},{129,385},{257,1},{385... | collective-permute-start | bytes 3145736 | tf_op jit(solution)/shard_map/ppermute | solution.py:187
  4.3 6.2 %shard_map.112 = bf16[8,272,256]{2,1,0:T(8,128)(2,1)} custom-call(s32[1,4]{1,0:T(1,128)} %lengths.1, bf16[256,1024]{1,0:T(8,128)(2,1)} %bitcast.27, bf16[256,128]{1,0:T(8,128)(2,1)} %bitcast.29, bf16[256,128]{1,0:T(8,128)(2,1)} %bitcast.30, bf16[256,1024]{1,0:T(8,128)(2,1)} %bitcast.28, bf16[256,1024]{1,0:T(8,128)(2,1)} %bitcast.20), custom_call_target="tpu_custom_call" | custom-call | tf_op jit(solution)/shard_map/pallas_call | solution.py:210
  10.5 0.0 copy-start.1
  10.5 0.0 copy-start.5
  10.5 6.8 %all-to-all-start = ((bf16[8,272,256]{2,1,0:T(8,128)(2,1)}), bf16[8,272,256]{2,1,0:T(8,128)(2,1)S(1)}, u32[]{:S(2)}, u32[]{:S(2)}) async-start(bf16[8,272,256]{2,1,0:T(8,128)(2,1)} %shard_map.112), calls=%async_computation | async-start | bytes 2228224 | tf_op jit(solution)/shard_map/all_to_all | solution.py:227
  17.3 1.9 %collective-permute-start.1 = (bf16[512,1024]{1,0:T(8,128)(2,1)}, bf16[512,1024]{1,0:T(8,128)(2,1)}, u32[]{:S(2)}, u32[]{:S(2)}) collective-permute-start(bf16[512,1024]{1,0:T(8,128)(2,1)} %bitcast.8.own), channel_id=1, source_target_pairs={{0,128},{128,0},{256,384},{384,256},{1,129},{129,1},{257,385},{385... | collective-permute-start | bytes 3145736 | tf_op jit(solution)/shard_map/ppermute | solution.py:187
  19.2 22.9 %all-to-all-done.grad_kv = bf16[8,272,256]{2,1,0:T(8,128)(2,1)S(1)} async-done(((bf16[8,272,256]{2,1,0:T(8,128)(2,1)}), bf16[8,272,256]{2,1,0:T(8,128)(2,1)S(1)}, u32[]{:S(2)}, u32[]{:S(2)}) %all-to-all-start) | async-done | bytes 1114144 | tf_op jit(solution)/shard_map/all_to_all | solution.py:227
  42.2 0.0 collective-permute-done.far
  42.2 1.9 %collective-permute-start.2 = (bf16[512,1024]{1,0:T(8,128)(2,1)}, bf16[512,1024]{1,0:T(8,128)(2,1)S(1)}, u32[]{:S(2)}, u32[]{:S(2)}) collective-permute-start(bf16[512,1024]{1,0:T(8,128)(2,1)} %collective-permute-done.far), channel_id=1, source_target_pairs={{0,128},{128,0},{256,384},{384,256},{1,129},{129,1},{257,385},{385... | collective-permute-start | bytes 3145736 | tf_op jit(solution)/shard_map/ppermute | solution.py:187
  44.1 0.1 stack.35.order
  44.2 0.0 collective-permute-done.1.near
  44.2 0.0 copy-done.1
  44.2 0.0 copy-done.5
  44.2 2.9 %shard_map.113 = (bf16[3,256,512]{2,1,0:T(8,128)(2,1)S(1)}, bf16[3,256,512]{2,1,0:T(8,128)(2,1)S(1)}, bf16[3,256,512]{2,1,0:T(8,128)(2,1)S(1)}, bf16[1,256,512]{...) custom-call(s32[8]{0:T(128)S(1)} %stack.35.order, bf16[8,272,256]{2,1,0:T(8,128)(2,1)S(1)} %all-to-all-done.grad_kv, ...), custom_call_target="tpu_custom_call" | custom-call | tf_op jit(solution)/shard_map/pallas_call | solution.py:236
  47.1 0.0 copy-start.2
  47.1 0.0 copy-start.4
  47.1 0.0 copy-start.7
  47.2 0.0 copy-start.6
  47.2 0.0 collective-permute-done.2.piece
  47.2 0.6 shard_map.114
  47.8 0.2 copy-done.2
  48.0 0.1 copy-done.4
  48.1 0.3 copy-done.7
  48.4 11.9 %all_to_all.20.prods = f32[8,1,256]{2,1,0:T(1,128)S(1)} all-to-all(f32[8,1,256]{2,1,0:T(1,128)S(1)} %get-tuple-element.22), channel_id=1, replica_groups=mesh['dp'=4,'pipe'=16,'tensor'=8] {'tensor'}, dimensions={0} | all-to-all | bytes 16384 | tf_op jit(solution)/shard_map/all_to_all | solution.py:261
  60.2 0.0 copy-start.8
  60.2 1.1 shard_map.115
  61.3 0.0 copy-done.6
  61.3 15.2 %all-to-all-start.2 = ((bf16[16,16,1024]{2,1,0:T(8,128)(2,1)}), bf16[16,16,1024]{2,1,0:T(8,128)(2,1)S(1)}, u32[]{:S(2)}, u32[]{:S(2)}) async-start(bf16[16,16,1024]{2,1,0:T(8,128)(2,1)} %bitcast.14), calls=%async_computation.2 | async-start | bytes 1048576 | tf_op jit(solution)/shard_map/all_to_all | solution.py:277
  76.5 0.0 copy-done.8
  76.5 2.4 %collective-permute-start.3 = (bf16[3,256,512]{2,1,0:T(8,128)(2,1)S(1)}, bf16[3,256,512]{2,1,0:T(8,128)(2,1)S(1)}, u32[]{:S(2)}, u32[]{:S(2)}) collective-permute-start(bf16[3,256,512]{2,1,0:T(8,128)(2,1)S(1)} %copy-done.8), channel_id=1, source_target_pairs={{0,256},{128,384},{256,0},{384,128},{1,257},{129,385},{257,1},{385... | collective-permute-start | bytes 2359304 | tf_op jit(solution)/shard_map/ppermute | solution.py:187
  78.9 0.0 copy-done
  78.9 17.5 %collective-permute-done.3.far = bf16[3,256,512]{2,1,0:T(8,128)(2,1)S(1)} collective-permute-done((bf16[3,256,512]{2,1,0:T(8,128)(2,1)S(1)}, bf16[3,256,512]{2,1,0:T(8,128)(2,1)S(1)}, u32[]{:S(2)}, u32[]{:S(2)}) %collective-permute-start.3) | collective-permute-done | bytes 786464 | tf_op jit(solution)/shard_map/ppermute | solution.py:187
  96.4 8.1 %all-to-all-done.2.parts = bf16[16,16,1024]{2,1,0:T(8,128)(2,1)S(1)} async-done(((bf16[16,16,1024]{2,1,0:T(8,128)(2,1)}), bf16[16,16,1024]{2,1,0:T(8,128)(2,1)S(1)}, u32[]{:S(2)}, u32[]{:S(2)}) %all-to-all-start.2) | async-done | bytes 524320 | tf_op jit(solution)/shard_map/all_to_all | solution.py:277
  104.5 0.9 shard_map.116
  105.4 0.0 copy-start.3
  105.4 6.8 %all-to-all-start.3 = ((bf16[16,16,1024]{2,1,0:T(8,128)(2,1)}), bf16[16,16,1024]{2,1,0:T(8,128)(2,1)S(1)}, u32[]{:S(2)}, u32[]{:S(2)}) async-start(bf16[16,16,1024]{2,1,0:T(8,128)(2,1)} %shard_map.116), calls=%async_computation.3 | async-start | bytes 1048576 | tf_op jit(solution)/shard_map/all_to_all | solution.py:283
  112.2 1.9 %collective-permute-start.4 = (bf16[3,256,512]{2,1,0:T(8,128)(2,1)}, bf16[3,256,512]{2,1,0:T(8,128)(2,1)S(1)}, u32[]{:S(2)}, u32[]{:S(2)}) collective-permute-start(bf16[3,256,512]{2,1,0:T(8,128)(2,1)} %copy-done.6), channel_id=1, source_target_pairs={{0,128},{128,0},{256,384},{384,256},{1,129},{129,1},{257,385},{385... | collective-permute-start | bytes 2359304 | tf_op jit(solution)/shard_map/ppermute | solution.py:187
  114.1 0.8 slice.3
  114.9 2.4 %collective-permute-start.6 = (bf16[2,256,512]{2,1,0:T(8,128)(2,1)}, bf16[2,256,512]{2,1,0:T(8,128)(2,1)}, u32[]{:S(2)}, u32[]{:S(2)}) collective-permute-start(bf16[2,256,512]{2,1,0:T(8,128)(2,1)} %slice.3), channel_id=1, source_target_pairs={{0,128},{128,0},{256,384},{384,256},{1,129},{129,1},{257,385},{385... | collective-permute-start | bytes 1572872 | tf_op jit(solution)/shard_map/ppermute | solution.py:187
  117.3 2.0 %collective-permute-start.5 = (bf16[1,256,512]{2,1,0:T(8,128)(2,1)}, bf16[1,256,512]{2,1,0:T(8,128)(2,1)}, u32[]{:S(2)}, u32[]{:S(2)}) collective-permute-start(bf16[1,256,512]{2,1,0:T(8,128)(2,1)} %copy-done.4), channel_id=1, source_target_pairs={{0,384},{128,256},{256,128},{384,0},{1,385},{129,257},{257,129},{3... | collective-permute-start | bytes 786440 | tf_op jit(solution)/shard_map/ppermute | solution.py:187
  119.3 10.9 %psum.7 = f32[1,1024]{1,0:T(1,128)} all-reduce(f32[1,1024]{1,0:T(1,128)S(1)} %broadcast_multiply_fusion), channel_id=1, replica_groups=mesh['dp'=4,'pipe'=16,'tensor'=8] {'dp'}, use_global_device_ids=true, to_apply=%region_0.0 | all-reduce | flops 1024 | bytes 8192 | tf_op jit(solution)/shard_map/psum | solution.py:293
  130.2 0.0 collective-permute-done.5.share
  130.2 0.0 collective-permute-done.4.near
  130.2 0.0 collective-permute-done.6.diagonal
  130.2 0.0 copy-done.3
  130.2 3.4 %shard_map.118 = bf16[512,1024]{1,0:T(8,128)(2,1)} custom-call(bf16[3,256,512]{2,1,0:T(8,128)(2,1)S(1)} %copy-done.3, bf16[3,256,512]{2,1,0:T(8,128)(2,1)S(1)} %collective-permute-done.4.near, bf16[3,256,512]{2,1,0:T(8,128)(2,1)S(1)} %collective-permute-done.3.far, bf16[1,256,512]{2,1,0:T(8,128)(2,1)} %collective-permute-done.5.share, ...), custom_call_target="tpu_custom_call" | custom-call | tf_op jit(solution)/shard_map/pallas_call | solution.py:286
  133.6 6.1 %all-to-all-done.3 = bf16[16,16,1024]{2,1,0:T(8,128)(2,1)S(1)} async-done(((bf16[16,16,1024]{2,1,0:T(8,128)(2,1)}), bf16[16,16,1024]{2,1,0:T(8,128)(2,1)S(1)}, u32[]{:S(2)}, u32[]{:S(2)}) %all-to-all-start.3) | async-done | bytes 524320 | tf_op jit(solution)/shard_map/all_to_all | solution.py:283
  139.7 0.8 shard_map.117
  (2 shorter events, 0.0 us)
Async XLA Ops:
  0.6 78.3 %copy-start = (bf16[1,256,1024]{2,1,0:T(8,128)(2,1)S(1)}, bf16[1,256,1024]{2,1,0:T(8,128)(2,1)}, u32[]{:S(2)}) copy-start(bf16[1,256,1024]{2,1,0:T(8,128)(2,1)} %param.16) | copy-start | bytes 1572868
  0.6 41.5 %collective-permute-start = (bf16[512,1024]{1,0:T(8,128)(2,1)}, bf16[512,1024]{1,0:T(8,128)(2,1)}, u32[]{:S(2)}, u32[]{:S(2)}) collective-permute-start(bf16[512,1024]{1,0:T(8,128)(2,1)} %bitcast.8.own), channel_id=1, source_target_pairs={{0,256},{128,384},{256,0},{384,128},{1,257},{129,385},{257,1},{385... | collective-permute-start | bytes 3145736 | tf_op jit(solution)/shard_map/ppermute | solution.py:187
  10.5 33.7 %copy-start.1 = (bf16[1,1,256,1024]{3,2,1,0:T(8,128)(2,1)S(1)}, bf16[1,1,256,1024]{3,2,1,0:T(8,128)(2,1)}, u32[]{:S(2)}) copy-start(bf16[1,1,256,1024]{3,2,1,0:T(8,128)(2,1)} %param.9) | copy-start | bytes 1572868
  10.5 33.7 %copy-start.5 = (f32[1,1024]{1,0:T(1,128)S(1)}, f32[1,1024]{1,0:T(1,128)}, u32[]{:S(2)}) copy-start(f32[1,1024]{1,0:T(1,128)} %gain.3) | copy-start | bytes 12292
  10.5 31.6 %all-to-all-start = ((bf16[8,272,256]{2,1,0:T(8,128)(2,1)}), bf16[8,272,256]{2,1,0:T(8,128)(2,1)S(1)}, u32[]{:S(2)}, u32[]{:S(2)}) async-start(bf16[8,272,256]{2,1,0:T(8,128)(2,1)} %shard_map.112), calls=%async_computation | async-start | bytes 2228224 | tf_op jit(solution)/shard_map/all_to_all | solution.py:227
  17.3 26.9 %collective-permute-start.1 = (bf16[512,1024]{1,0:T(8,128)(2,1)}, bf16[512,1024]{1,0:T(8,128)(2,1)}, u32[]{:S(2)}, u32[]{:S(2)}) collective-permute-start(bf16[512,1024]{1,0:T(8,128)(2,1)} %bitcast.8.own), channel_id=1, source_target_pairs={{0,128},{128,0},{256,384},{384,256},{1,129},{129,1},{257,385},{385... | collective-permute-start | bytes 3145736 | tf_op jit(solution)/shard_map/ppermute | solution.py:187
  42.2 5.0 %collective-permute-start.2 = (bf16[512,1024]{1,0:T(8,128)(2,1)}, bf16[512,1024]{1,0:T(8,128)(2,1)S(1)}, u32[]{:S(2)}, u32[]{:S(2)}) collective-permute-start(bf16[512,1024]{1,0:T(8,128)(2,1)} %collective-permute-done.far), channel_id=1, source_target_pairs={{0,128},{128,0},{256,384},{384,256},{1,129},{129,1},{257,385},{385... | collective-permute-start | bytes 3145736 | tf_op jit(solution)/shard_map/ppermute | solution.py:187
  47.1 0.9 copy-start.2
  47.1 1.0 copy-start.4
  47.1 1.2 copy-start.7
  47.2 14.2 %copy-start.6 = (bf16[3,256,512]{2,1,0:T(8,128)(2,1)}, bf16[3,256,512]{2,1,0:T(8,128)(2,1)S(1)}, u32[]{:S(2)}) copy-start(bf16[3,256,512]{2,1,0:T(8,128)(2,1)S(1)} %get-tuple-element.28) | copy-start | bytes 2359300
  60.2 16.3 %copy-start.8 = (bf16[3,256,512]{2,1,0:T(8,128)(2,1)S(1)}, bf16[3,256,512]{2,1,0:T(8,128)(2,1)}, u32[]{:S(2)}) copy-start(bf16[3,256,512]{2,1,0:T(8,128)(2,1)} %copy-done.7) | copy-start | bytes 2359300
  61.3 43.2 %all-to-all-start.2 = ((bf16[16,16,1024]{2,1,0:T(8,128)(2,1)}), bf16[16,16,1024]{2,1,0:T(8,128)(2,1)S(1)}, u32[]{:S(2)}, u32[]{:S(2)}) async-start(bf16[16,16,1024]{2,1,0:T(8,128)(2,1)} %bitcast.14), calls=%async_computation.2 | async-start | bytes 1048576 | tf_op jit(solution)/shard_map/all_to_all | solution.py:277
  76.5 19.9 %collective-permute-start.3 = (bf16[3,256,512]{2,1,0:T(8,128)(2,1)S(1)}, bf16[3,256,512]{2,1,0:T(8,128)(2,1)S(1)}, u32[]{:S(2)}, u32[]{:S(2)}) collective-permute-start(bf16[3,256,512]{2,1,0:T(8,128)(2,1)S(1)} %copy-done.8), channel_id=1, source_target_pairs={{0,256},{128,384},{256,0},{384,128},{1,257},{129,385},{257,1},{385... | collective-permute-start | bytes 2359304 | tf_op jit(solution)/shard_map/ppermute | solution.py:187
  105.4 24.8 %copy-start.3 = (bf16[3,256,512]{2,1,0:T(8,128)(2,1)S(1)}, bf16[3,256,512]{2,1,0:T(8,128)(2,1)}, u32[]{:S(2)}) copy-start(bf16[3,256,512]{2,1,0:T(8,128)(2,1)} %copy-done.2) | copy-start | bytes 2359300
  105.4 34.3 %all-to-all-start.3 = ((bf16[16,16,1024]{2,1,0:T(8,128)(2,1)}), bf16[16,16,1024]{2,1,0:T(8,128)(2,1)S(1)}, u32[]{:S(2)}, u32[]{:S(2)}) async-start(bf16[16,16,1024]{2,1,0:T(8,128)(2,1)} %shard_map.116), calls=%async_computation.3 | async-start | bytes 1048576 | tf_op jit(solution)/shard_map/all_to_all | solution.py:283
  112.2 18.0 %collective-permute-start.4 = (bf16[3,256,512]{2,1,0:T(8,128)(2,1)}, bf16[3,256,512]{2,1,0:T(8,128)(2,1)S(1)}, u32[]{:S(2)}, u32[]{:S(2)}) collective-permute-start(bf16[3,256,512]{2,1,0:T(8,128)(2,1)} %copy-done.6), channel_id=1, source_target_pairs={{0,128},{128,0},{256,384},{384,256},{1,129},{129,1},{257,385},{385... | collective-permute-start | bytes 2359304 | tf_op jit(solution)/shard_map/ppermute | solution.py:187
  114.9 15.3 %collective-permute-start.6 = (bf16[2,256,512]{2,1,0:T(8,128)(2,1)}, bf16[2,256,512]{2,1,0:T(8,128)(2,1)}, u32[]{:S(2)}, u32[]{:S(2)}) collective-permute-start(bf16[2,256,512]{2,1,0:T(8,128)(2,1)} %slice.3), channel_id=1, source_target_pairs={{0,128},{128,0},{256,384},{384,256},{1,129},{129,1},{257,385},{385... | collective-permute-start | bytes 1572872 | tf_op jit(solution)/shard_map/ppermute | solution.py:187
  117.3 12.9 %collective-permute-start.5 = (bf16[1,256,512]{2,1,0:T(8,128)(2,1)}, bf16[1,256,512]{2,1,0:T(8,128)(2,1)}, u32[]{:S(2)}, u32[]{:S(2)}) collective-permute-start(bf16[1,256,512]{2,1,0:T(8,128)(2,1)} %copy-done.4), channel_id=1, source_target_pairs={{0,384},{128,256},{256,128},{384,0},{1,385},{129,257},{257,129},{3... | collective-permute-start | bytes 786440 | tf_op jit(solution)/shard_map/ppermute | solution.py:187

commit v4 on v3

--- a/solution.py
+++ b/solution.py
@@ -205,7 +205,6 @@
 
     own = kv_projection[0]
     far = swap(own, "dp", 2)
-    near = swap(own, "dp", 1)
 
     copies = pl.pallas_call(
         attention_kernel,
@@ -223,9 +222,11 @@
             pltpu.SemaphoreType.DMA((tensor,)),
         ],
         compiler_params=WHOLE,
+        cost_estimate=pl.CostEstimate(flops=int(3e+10), bytes_accessed=4000000, transcendentals=0),
     )(doc_lengths, queries[0, 0], saved_keys[0, 0], saved_values[0, 0], attn_out_grad[0, 0], rows)
+    copies, whole = lax.optimization_barrier((copies, own))
     grad_kv = lax.all_to_all(copies, "tensor", 0, 0)
-    far, grad_kv = lax.optimization_barrier((far, grad_kv))
+    near = swap(whole, "dp", 1)
     far_near = swap(far, "dp", 1)
     order = [2 * (mine ^ place) + part for place in range(dp) for part in range(2)]
 
@@ -246,6 +247,7 @@
         in_specs=[SMEM] + [VMEM] * 6,
         out_specs=(VMEM,) * 6,
         compiler_params=PARAMS,
+        cost_estimate=pl.CostEstimate(flops=int(3e+10), bytes_accessed=0, transcendentals=0),
     )(jnp.stack(order).astype(jnp.int32), grad_kv, own, near, far, rows, norm_gain)
     scaled, prods, gains = pl.pallas_call(
         project_kernel,

time: 141 us -> 140 us (level)
  waiting for transfers between devices: 54.6 us -> 52.1 us
    all_to_all x1, waiting for transfers between devices: 22.9 us -> 2.27 us  [body(): grad_kv = lax.all_to_all(copies, 'tensor', 0, 0)]
    ppermute x7, waiting for transfers between devices: 17.5 us -> 35.9 us  [swap(): lax.ppermute(value, axis, [(source, source ^ distance) for source in rang...]
  transfers between devices with their start and end apart: 10 -> 10, of which waited for: 4 -> 5; matrix products, arithmetic and copies ran while one was open for 1% -> 1% of each run, Pallas kernels for 9% -> 9%
where the time goes in v4:
time: 140 us; the launch traced here: 139 us
  waiting for transfers between devices  52.1 us (37%)
  starting transfers between devices  45.3 us (32%)
  blocking collectives  23 us (16%)
  Pallas kernels  16 us (11%)
  local copies, waits for them, and re-layouts  1.79 us (1%)
    ppermute x7, waiting for transfers between devices, swap(): lax.ppermute(value, axis, [(source, source ^ distance) for source in rang...  35.9 us
    ppermute x7, starting transfers between devices, swap(): lax.ppermute(value, axis, [(source, source ^ distance) for source in rang...  16.7 us
    all_to_all x1, starting transfers between devices, body(): lax.all_to_all(contrib.reshape(sections, small, width), 'pipe', 0, 0)  15.2 us
    all_to_all x1, blocking collectives, body(): prods = lax.all_to_all(prods, 'tensor', 0, 0)  12.2 us
    psum x1, blocking collectives, body(): gain_grad = lax.psum(gains * scale, 'dp')  10.9 us
    all_to_all x1, waiting for transfers between devices, body(): lax.all_to_all(contrib.reshape(sections, small, width), 'pipe', 0, 0)  8.09 us
    all_to_all x1, starting transfers between devices, body(): lax.all_to_all(suffixes, 'pipe', 0, 0).reshape(tokens, width)  6.81 us
    all_to_all x1, starting transfers between devices, body(): grad_kv = lax.all_to_all(copies, 'tensor', 0, 0)  6.65 us
  transfers between devices with their start and end apart: 10, of which 5 were waited for; matrix products, arithmetic and copies ran while one was open for 1% of the time, Pallas kernels for 9%

profile of v4, /device:TPU:32, one launch (start us, length us, event | category | flops | bytes accessed | tf_op | source)
XLA Modules:
  0.0 139.1 jit_solution(8496782591666286599)
XLA Ops:
  0.6 0.0 copy-start
  0.6 3.6 %collective-permute-start.1 = (bf16[512,1024]{1,0:T(8,128)(2,1)}, bf16[512,1024]{1,0:T(8,128)(2,1)}, u32[]{:S(2)}, u32[]{:S(2)}) collective-permute-start(bf16[512,1024]{1,0:T(8,128)(2,1)} %bitcast.13.own), channel_id=1, source_target_pairs={{0,256},{128,384},{256,0},{384,128},{1,257},{129,385},{257,1},{385... | collective-permute-start | bytes 3145736 | tf_op jit(solution)/shard_map/ppermute | solution.py:187
  4.3 6.2 %shard_map.112 = bf16[8,272,256]{2,1,0:T(8,128)(2,1)} custom-call(s32[1,4]{1,0:T(1,128)} %lengths.1, bf16[256,1024]{1,0:T(8,128)(2,1)} %bitcast.27, bf16[256,128]{1,0:T(8,128)(2,1)} %bitcast.29, bf16[256,128]{1,0:T(8,128)(2,1)} %bitcast.30, bf16[256,1024]{1,0:T(8,128)(2,1)} %bitcast.28, bf16[256,1024]{1,0:T(8,128)(2,1)} %bitcast.20), custom_call_target="tpu_custom_call" | custom-call | flops 30000001024 | bytes 4000000 | tf_op jit(solution)/shard_map/pallas_call | solution.py:209
  10.5 0.0 copy-start.1
  10.5 0.0 copy-start.5
  10.5 2.1 %collective-permute-start = (bf16[512,1024]{1,0:T(8,128)(2,1)}, bf16[512,1024]{1,0:T(8,128)(2,1)}, u32[]{:S(2)}, u32[]{:S(2)}) collective-permute-start(bf16[512,1024]{1,0:T(8,128)(2,1)} %bitcast.13.own), channel_id=1, source_target_pairs={{0,128},{128,0},{256,384},{384,256},{1,129},{129,1},{257,385},{385... | collective-permute-start | bytes 3145736 | tf_op jit(solution)/shard_map/ppermute | solution.py:187
  12.6 6.7 %all-to-all-start = ((bf16[8,272,256]{2,1,0:T(8,128)(2,1)}), bf16[8,272,256]{2,1,0:T(8,128)(2,1)S(1)}, u32[]{:S(2)}, u32[]{:S(2)}) async-start(bf16[8,272,256]{2,1,0:T(8,128)(2,1)} %shard_map.112), calls=%async_computation | async-start | bytes 2228224 | tf_op jit(solution)/shard_map/all_to_all | solution.py:228
  19.2 0.1 stack.35.order
  19.3 18.7 %collective-permute-done.1.far = bf16[512,1024]{1,0:T(8,128)(2,1)} collective-permute-done((bf16[512,1024]{1,0:T(8,128)(2,1)}, bf16[512,1024]{1,0:T(8,128)(2,1)}, u32[]{:S(2)}, u32[]{:S(2)}) %collective-permute-start.1) | collective-permute-done | bytes 1048608 | tf_op jit(solution)/shard_map/ppermute | solution.py:187
  38.0 1.9 %collective-permute-start.2 = (bf16[512,1024]{1,0:T(8,128)(2,1)}, bf16[512,1024]{1,0:T(8,128)(2,1)S(1)}, u32[]{:S(2)}, u32[]{:S(2)}) collective-permute-start(bf16[512,1024]{1,0:T(8,128)(2,1)} %collective-permute-done.1.far), channel_id=1, source_target_pairs={{0,128},{128,0},{256,384},{384,256},{1,129},{129,1},{257,385},{385... | collective-permute-start | bytes 3145736 | tf_op jit(solution)/shard_map/ppermute | solution.py:187
  39.9 2.3 %all-to-all-done.grad_kv = bf16[8,272,256]{2,1,0:T(8,128)(2,1)S(1)} async-done(((bf16[8,272,256]{2,1,0:T(8,128)(2,1)}), bf16[8,272,256]{2,1,0:T(8,128)(2,1)S(1)}, u32[]{:S(2)}, u32[]{:S(2)}) %all-to-all-start) | async-done | bytes 1114144 | tf_op jit(solution)/shard_map/all_to_all | solution.py:228
  42.2 0.0 collective-permute-done.near
  42.2 0.0 copy-done.1
  42.2 0.0 copy-done.5
  42.2 2.9 %shard_map.113 = (bf16[3,256,512]{2,1,0:T(8,128)(2,1)S(1)}, bf16[3,256,512]{2,1,0:T(8,128)(2,1)S(1)}, bf16[3,256,512]{2,1,0:T(8,128)(2,1)S(1)}, bf16[1,256,512]{...) custom-call(s32[8]{0:T(128)S(1)} %stack.35.order, bf16[8,272,256]{2,1,0:T(8,128)(2,1)S(1)} %all-to-all-done.grad_kv, ...), custom_call_target="tpu_custom_call" | custom-call | flops 30000001024 | tf_op jit(solution)/shard_map/pallas_call | solution.py:237
  45.1 0.0 copy-start.2
  45.1 0.0 copy-start.4
  45.1 0.0 copy-start.6
  45.1 0.0 copy-start.7
  45.1 0.0 collective-permute-done.2.piece
  45.2 0.6 shard_map.114
  45.8 0.2 copy-done.2
  46.0 0.1 copy-done.4
  46.1 0.3 copy-done.6
  46.3 0.3 copy-done.7
  46.6 12.2 %all_to_all.20.prods = f32[8,1,256]{2,1,0:T(1,128)S(1)} all-to-all(f32[8,1,256]{2,1,0:T(1,128)S(1)} %get-tuple-element.22), channel_id=1, replica_groups=mesh['dp'=4,'pipe'=16,'tensor'=8] {'tensor'}, dimensions={0} | all-to-all | bytes 16384 | tf_op jit(solution)/shard_map/all_to_all | solution.py:263
  58.8 0.0 copy-start.8
  58.8 1.1 shard_map.115
  59.9 15.2 %all-to-all-start.2 = ((bf16[16,16,1024]{2,1,0:T(8,128)(2,1)}), bf16[16,16,1024]{2,1,0:T(8,128)(2,1)S(1)}, u32[]{:S(2)}, u32[]{:S(2)}) async-start(bf16[16,16,1024]{2,1,0:T(8,128)(2,1)} %bitcast.14), calls=%async_computation.2 | async-start | bytes 1048576 | tf_op jit(solution)/shard_map/all_to_all | solution.py:279
  75.1 0.0 copy-done.8
  75.1 2.6 %collective-permute-start.3 = (bf16[3,256,512]{2,1,0:T(8,128)(2,1)S(1)}, bf16[3,256,512]{2,1,0:T(8,128)(2,1)S(1)}, u32[]{:S(2)}, u32[]{:S(2)}) collective-permute-start(bf16[3,256,512]{2,1,0:T(8,128)(2,1)S(1)} %copy-done.8), channel_id=1, source_target_pairs={{0,256},{128,384},{256,0},{384,128},{1,257},{129,385},{257,1},{385... | collective-permute-start | bytes 2359304 | tf_op jit(solution)/shard_map/ppermute | solution.py:187
  77.7 0.0 copy-done
  77.7 17.2 %collective-permute-done.3.far = bf16[3,256,512]{2,1,0:T(8,128)(2,1)S(1)} collective-permute-done((bf16[3,256,512]{2,1,0:T(8,128)(2,1)S(1)}, bf16[3,256,512]{2,1,0:T(8,128)(2,1)S(1)}, u32[]{:S(2)}, u32[]{:S(2)}) %collective-permute-start.3) | collective-permute-done | bytes 786464 | tf_op jit(solution)/shard_map/ppermute | solution.py:187
  94.9 8.1 %all-to-all-done.2.parts = bf16[16,16,1024]{2,1,0:T(8,128)(2,1)S(1)} async-done(((bf16[16,16,1024]{2,1,0:T(8,128)(2,1)}), bf16[16,16,1024]{2,1,0:T(8,128)(2,1)S(1)}, u32[]{:S(2)}, u32[]{:S(2)}) %all-to-all-start.2) | async-done | bytes 524320 | tf_op jit(solution)/shard_map/all_to_all | solution.py:279
  103.0 0.9 shard_map.116
  103.9 0.0 copy-start.3
  103.9 6.8 %all-to-all-start.3 = ((bf16[16,16,1024]{2,1,0:T(8,128)(2,1)}), bf16[16,16,1024]{2,1,0:T(8,128)(2,1)S(1)}, u32[]{:S(2)}, u32[]{:S(2)}) async-start(bf16[16,16,1024]{2,1,0:T(8,128)(2,1)} %shard_map.116), calls=%async_computation.3 | async-start | bytes 1048576 | tf_op jit(solution)/shard_map/all_to_all | solution.py:285
  110.7 1.9 %collective-permute-start.4 = (bf16[3,256,512]{2,1,0:T(8,128)(2,1)}, bf16[3,256,512]{2,1,0:T(8,128)(2,1)S(1)}, u32[]{:S(2)}, u32[]{:S(2)}) collective-permute-start(bf16[3,256,512]{2,1,0:T(8,128)(2,1)} %copy-done.6), channel_id=1, source_target_pairs={{0,128},{128,0},{256,384},{384,256},{1,129},{129,1},{257,385},{385... | collective-permute-start | bytes 2359304 | tf_op jit(solution)/shard_map/ppermute | solution.py:187
  112.7 0.8 slice.3
  113.5 2.4 %collective-permute-start.6 = (bf16[2,256,512]{2,1,0:T(8,128)(2,1)}, bf16[2,256,512]{2,1,0:T(8,128)(2,1)}, u32[]{:S(2)}, u32[]{:S(2)}) collective-permute-start(bf16[2,256,512]{2,1,0:T(8,128)(2,1)} %slice.3), channel_id=1, source_target_pairs={{0,128},{128,0},{256,384},{384,256},{1,129},{129,1},{257,385},{385... | collective-permute-start | bytes 1572872 | tf_op jit(solution)/shard_map/ppermute | solution.py:187
  115.9 2.2 %collective-permute-start.5 = (bf16[1,256,512]{2,1,0:T(8,128)(2,1)}, bf16[1,256,512]{2,1,0:T(8,128)(2,1)}, u32[]{:S(2)}, u32[]{:S(2)}) collective-permute-start(bf16[1,256,512]{2,1,0:T(8,128)(2,1)} %copy-done.4), channel_id=1, source_target_pairs={{0,384},{128,256},{256,128},{384,0},{1,385},{129,257},{257,129},{3... | collective-permute-start | bytes 786440 | tf_op jit(solution)/shard_map/ppermute | solution.py:187
  118.1 10.9 %psum.7 = f32[1,1024]{1,0:T(1,128)} all-reduce(f32[1,1024]{1,0:T(1,128)S(1)} %broadcast_multiply_fusion), channel_id=1, replica_groups=mesh['dp'=4,'pipe'=16,'tensor'=8] {'dp'}, use_global_device_ids=true, to_apply=%region_0.0 | all-reduce | flops 1024 | bytes 8192 | tf_op jit(solution)/shard_map/psum | solution.py:295
  129.0 0.0 collective-permute-done.5.share
  129.0 0.0 collective-permute-done.4.near
  129.0 0.0 collective-permute-done.6.diagonal
  129.0 0.0 copy-done.3
  129.0 3.4 %shard_map.118 = bf16[512,1024]{1,0:T(8,128)(2,1)} custom-call(bf16[3,256,512]{2,1,0:T(8,128)(2,1)S(1)} %copy-done.3, bf16[3,256,512]{2,1,0:T(8,128)(2,1)S(1)} %collective-permute-done.4.near, bf16[3,256,512]{2,1,0:T(8,128)(2,1)S(1)} %collective-permute-done.3.far, bf16[1,256,512]{2,1,0:T(8,128)(2,1)} %collective-permute-done.5.share, ...), custom_call_target="tpu_custom_call" | custom-call | tf_op jit(solution)/shard_map/pallas_call | solution.py:288
  132.4 5.8 %all-to-all-done.3 = bf16[16,16,1024]{2,1,0:T(8,128)(2,1)S(1)} async-done(((bf16[16,16,1024]{2,1,0:T(8,128)(2,1)}), bf16[16,16,1024]{2,1,0:T(8,128)(2,1)S(1)}, u32[]{:S(2)}, u32[]{:S(2)}) %all-to-all-start.3) | async-done | bytes 524320 | tf_op jit(solution)/shard_map/all_to_all | solution.py:285
  138.3 0.8 shard_map.117
  (2 shorter events, 0.0 us)
Async XLA Ops:
  0.6 77.1 %copy-start = (bf16[1,256,1024]{2,1,0:T(8,128)(2,1)S(1)}, bf16[1,256,1024]{2,1,0:T(8,128)(2,1)}, u32[]{:S(2)}) copy-start(bf16[1,256,1024]{2,1,0:T(8,128)(2,1)} %param.16) | copy-start | bytes 1572868
  0.6 37.3 %collective-permute-start.1 = (bf16[512,1024]{1,0:T(8,128)(2,1)}, bf16[512,1024]{1,0:T(8,128)(2,1)}, u32[]{:S(2)}, u32[]{:S(2)}) collective-permute-start(bf16[512,1024]{1,0:T(8,128)(2,1)} %bitcast.13.own), channel_id=1, source_target_pairs={{0,256},{128,384},{256,0},{384,128},{1,257},{129,385},{257,1},{385... | collective-permute-start | bytes 3145736 | tf_op jit(solution)/shard_map/ppermute | solution.py:187
  10.5 31.7 %copy-start.1 = (bf16[1,1,256,1024]{3,2,1,0:T(8,128)(2,1)S(1)}, bf16[1,1,256,1024]{3,2,1,0:T(8,128)(2,1)}, u32[]{:S(2)}) copy-start(bf16[1,1,256,1024]{3,2,1,0:T(8,128)(2,1)} %param.9) | copy-start | bytes 1572868
  10.5 31.7 %copy-start.5 = (f32[1,1024]{1,0:T(1,128)S(1)}, f32[1,1024]{1,0:T(1,128)}, u32[]{:S(2)}) copy-start(f32[1,1024]{1,0:T(1,128)} %gain.3) | copy-start | bytes 12292
  10.5 31.6 %collective-permute-start = (bf16[512,1024]{1,0:T(8,128)(2,1)}, bf16[512,1024]{1,0:T(8,128)(2,1)}, u32[]{:S(2)}, u32[]{:S(2)}) collective-permute-start(bf16[512,1024]{1,0:T(8,128)(2,1)} %bitcast.13.own), channel_id=1, source_target_pairs={{0,128},{128,0},{256,384},{384,256},{1,129},{129,1},{257,385},{385... | collective-permute-start | bytes 3145736 | tf_op jit(solution)/shard_map/ppermute | solution.py:187
  12.6 29.6 %all-to-all-start = ((bf16[8,272,256]{2,1,0:T(8,128)(2,1)}), bf16[8,272,256]{2,1,0:T(8,128)(2,1)S(1)}, u32[]{:S(2)}, u32[]{:S(2)}) async-start(bf16[8,272,256]{2,1,0:T(8,128)(2,1)} %shard_map.112), calls=%async_computation | async-start | bytes 2228224 | tf_op jit(solution)/shard_map/all_to_all | solution.py:228
  38.0 7.2 %collective-permute-start.2 = (bf16[512,1024]{1,0:T(8,128)(2,1)}, bf16[512,1024]{1,0:T(8,128)(2,1)S(1)}, u32[]{:S(2)}, u32[]{:S(2)}) collective-permute-start(bf16[512,1024]{1,0:T(8,128)(2,1)} %collective-permute-done.1.far), channel_id=1, source_target_pairs={{0,128},{128,0},{256,384},{384,256},{1,129},{129,1},{257,385},{385... | collective-permute-start | bytes 3145736 | tf_op jit(solution)/shard_map/ppermute | solution.py:187
  45.1 0.9 copy-start.2
  45.1 1.0 copy-start.4
  45.1 1.2 copy-start.6
  45.1 1.5 %copy-start.7 = (bf16[3,256,512]{2,1,0:T(8,128)(2,1)}, bf16[3,256,512]{2,1,0:T(8,128)(2,1)S(1)}, u32[]{:S(2)}) copy-start(bf16[3,256,512]{2,1,0:T(8,128)(2,1)S(1)} %get-tuple-element.24) | copy-start | bytes 2359300
  58.8 16.3 %copy-start.8 = (bf16[3,256,512]{2,1,0:T(8,128)(2,1)S(1)}, bf16[3,256,512]{2,1,0:T(8,128)(2,1)}, u32[]{:S(2)}) copy-start(bf16[3,256,512]{2,1,0:T(8,128)(2,1)} %copy-done.7) | copy-start | bytes 2359300
  59.9 43.2 %all-to-all-start.2 = ((bf16[16,16,1024]{2,1,0:T(8,128)(2,1)}), bf16[16,16,1024]{2,1,0:T(8,128)(2,1)S(1)}, u32[]{:S(2)}, u32[]{:S(2)}) async-start(bf16[16,16,1024]{2,1,0:T(8,128)(2,1)} %bitcast.14), calls=%async_computation.2 | async-start | bytes 1048576 | tf_op jit(solution)/shard_map/all_to_all | solution.py:279
  75.1 19.9 %collective-permute-start.3 = (bf16[3,256,512]{2,1,0:T(8,128)(2,1)S(1)}, bf16[3,256,512]{2,1,0:T(8,128)(2,1)S(1)}, u32[]{:S(2)}, u32[]{:S(2)}) collective-permute-start(bf16[3,256,512]{2,1,0:T(8,128)(2,1)S(1)} %copy-done.8), channel_id=1, source_target_pairs={{0,256},{128,384},{256,0},{384,128},{1,257},{129,385},{257,1},{385... | collective-permute-start | bytes 2359304 | tf_op jit(solution)/shard_map/ppermute | solution.py:187
  103.9 25.1 %copy-start.3 = (bf16[3,256,512]{2,1,0:T(8,128)(2,1)S(1)}, bf16[3,256,512]{2,1,0:T(8,128)(2,1)}, u32[]{:S(2)}) copy-start(bf16[3,256,512]{2,1,0:T(8,128)(2,1)} %copy-done.2) | copy-start | bytes 2359300
  103.9 34.3 %all-to-all-start.3 = ((bf16[16,16,1024]{2,1,0:T(8,128)(2,1)}), bf16[16,16,1024]{2,1,0:T(8,128)(2,1)S(1)}, u32[]{:S(2)}, u32[]{:S(2)}) async-start(bf16[16,16,1024]{2,1,0:T(8,128)(2,1)} %shard_map.116), calls=%async_computation.3 | async-start | bytes 1048576 | tf_op jit(solution)/shard_map/all_to_all | solution.py:285
  110.7 18.3 %collective-permute-start.4 = (bf16[3,256,512]{2,1,0:T(8,128)(2,1)}, bf16[3,256,512]{2,1,0:T(8,128)(2,1)S(1)}, u32[]{:S(2)}, u32[]{:S(2)}) collective-permute-start(bf16[3,256,512]{2,1,0:T(8,128)(2,1)} %copy-done.6), channel_id=1, source_target_pairs={{0,128},{128,0},{256,384},{384,256},{1,129},{129,1},{257,385},{385... | collective-permute-start | bytes 2359304 | tf_op jit(solution)/shard_map/ppermute | solution.py:187
  113.5 15.5 %collective-permute-start.6 = (bf16[2,256,512]{2,1,0:T(8,128)(2,1)}, bf16[2,256,512]{2,1,0:T(8,128)(2,1)}, u32[]{:S(2)}, u32[]{:S(2)}) collective-permute-start(bf16[2,256,512]{2,1,0:T(8,128)(2,1)} %slice.3), channel_id=1, source_target_pairs={{0,128},{128,0},{256,384},{384,256},{1,129},{129,1},{257,385},{385... | collective-permute-start | bytes 1572872 | tf_op jit(solution)/shard_map/ppermute | solution.py:187
  115.9 13.1 %collective-permute-start.5 = (bf16[1,256,512]{2,1,0:T(8,128)(2,1)}, bf16[1,256,512]{2,1,0:T(8,128)(2,1)}, u32[]{:S(2)}, u32[]{:S(2)}) collective-permute-start(bf16[1,256,512]{2,1,0:T(8,128)(2,1)} %copy-done.4), channel_id=1, source_target_pairs={{0,384},{128,256},{256,128},{384,0},{1,385},{129,257},{257,129},{3... | collective-permute-start | bytes 786440 | tf_op jit(solution)/shard_map/ppermute | solution.py:187

commit v5 on v4

--- a/solution.py
+++ b/solution.py
@@ -120,7 +120,7 @@
 
 
 def gather_kernel(order, grad_kv, own, near, far, rows, gain, *outs):
-    mine, for_near, for_far, for_diagonal, total_out, inverse_out = outs
+    shares, (norm_out, total_out, inverse_out) = outs[:4], outs[4:]
     tokens, width = rows.shape
     half = width // 2
     sums = jnp.zeros((EXTRA, tokens), F32)
@@ -128,21 +128,18 @@
         sums = sums + grad_kv[block, tokens:, :].astype(F32)
     inverse = to_column(1.0 / jnp.sqrt(jnp.sum(sums, axis=0, keepdims=True) * (1.0 / D) + EPSILON))
     inverse_out[...] = inverse
-    for place, target in enumerate((mine, for_near, for_far, for_diagonal)):
+    for place, share in enumerate(shares):
         for part in range(2):
             span = slice(part * 2 * HD, (part + 1) * 2 * HD)
-            target[0, :, span] = grad_kv[order[2 * place + part], :tokens, :]
+            share[:, span] = grad_kv[order[2 * place + part], :tokens, :]
     total_out[...] = (
-        nn(mine[0], own[...]) + nn(for_near[0], near[...]) + nn(for_far[0], far[...])
+        nn(shares[0][...], own[...]) + nn(shares[1][...], near[...]) + nn(shares[2][...], far[...])
     )
-    normed = (rows[...].astype(F32) * inverse * gain[...]).astype(BF16)
-    for target in (mine, for_near, for_far):
-        target[1] = normed[:, :half]
-        target[2] = normed[:, half:]
+    norm_out[...] = (rows[...].astype(F32) * inverse * gain[...]).astype(BF16)
 
 
 def project_kernel(part, share, piece, rows, gain, inverse, scaled_out, prods, gains_out):
-    total = part[...] + nn(share[0], piece[...])
+    total = part[...] + nn(share[...], piece[...])
     unit = rows[...].astype(F32) * inverse[...]
     scaled = total * gain[...]
     scaled_out[...] = scaled
@@ -159,16 +156,13 @@
     out[...] = ((scaled[...] - unit * mean) * scale).astype(BF16)
 
 
-def term_kernel(scale, mine, near, far, share, diagonal, out):
-    half = mine.shape[2]
-    sources = ((mine, mine, 1), (near, near, 1), (far, far, 1), (share, diagonal, 0))
-    for part in range(2):
-        total = None
-        for heads, source, normed in sources:
-            term = tn(heads[0], source[normed + part])
-            term = (term * scale).astype(BF16).astype(F32)
-            total = term if total is None else total + term
-        out[:, part * half : (part + 1) * half] = total.astype(BF16)
+def term_kernel(scale, *refs):
+    shares, norms, out = refs[:4], refs[4:8], refs[8]
+    total = None
+    for share, norm in zip(shares, norms):
+        term = (tn(share[...], norm[...]) * scale).astype(BF16).astype(F32)
+        total = term if total is None else total + term
+    out[...] = total.astype(BF16)
 
 
 def suffix_kernel(parts, above, out):
@@ -230,24 +224,20 @@
     far_near = swap(far, "dp", 1)
     order = [2 * (mine ^ place) + part for place in range(dp) for part in range(2)]
 
-    def blocks(count):
-        return jax.ShapeDtypeStruct((count, tokens, width // 2), BF16)
-
     wide = jax.ShapeDtypeStruct((tokens, width), F32)
-    own_set, for_near, for_far, for_diagonal, total, inverse = pl.pallas_call(
+    share_shape = jax.ShapeDtypeStruct((tokens, tensor // dp * 2 * HD), BF16)
+    *shares, norm, total, inverse = pl.pallas_call(
         gather_kernel,
-        out_shape=(
-            blocks(3),
-            blocks(3),
-            blocks(3),
-            blocks(1),
+        out_shape=(share_shape,) * dp
+        + (
+            jax.ShapeDtypeStruct((tokens, width), BF16),
             wide,
             jax.ShapeDtypeStruct((tokens, 1), F32),
         ),
         in_specs=[SMEM] + [VMEM] * 6,
-        out_specs=(VMEM,) * 6,
+        out_specs=(VMEM,) * (dp + 3),
         compiler_params=PARAMS,
-        cost_estimate=pl.CostEstimate(flops=int(3e+10), bytes_accessed=0, transcendentals=0),
+        cost_estimate=pl.CostEstimate(flops=int(3e10), bytes_accessed=0, transcendentals=0),
     )(jnp.stack(order).astype(jnp.int32), grad_kv, own, near, far, rows, norm_gain)
     scaled, prods, gains = pl.pallas_call(
         project_kernel,
@@ -259,10 +249,10 @@
         in_specs=[VMEM] * 6,
         out_specs=(VMEM,) * 3,
         compiler_params=PARAMS,
-    )(total, for_diagonal, far_near, rows, norm_gain, inverse)
+    )(total, shares[3], far_near, rows, norm_gain, inverse)
     prods = lax.all_to_all(prods, "tensor", 0, 0)
 
-    far_set = swap(for_far, "dp", 2)
+    far_norm, far_share = swap(norm, "dp", 2), swap(shares[2], "dp", 2)
 
     def local(kernel, shape, *operands):
         return pl.pallas_call(
@@ -277,10 +267,9 @@
     small = tokens // sections
     own_top = lax.dynamic_slice_in_dim(top_grad[0], stage * small, small, 0)
     parts = lax.all_to_all(contrib.reshape(sections, small, width), "pipe", 0, 0)
-    parts, far_set, gains = lax.optimization_barrier((parts, far_set, gains))
-    near_set = swap(for_near, "dp", 1)
-    diagonal_share = swap(for_diagonal, "dp", 3)
-    diagonal_set = swap(far_set[1:], "dp", 1)
+    parts, far_norm, far_share, gains = lax.optimization_barrier((parts, far_norm, far_share, gains))
+    norms = [norm, swap(norm, "dp", 1), far_norm, swap(far_norm, "dp", 1)]
+    shares = [shares[0], swap(shares[1], "dp", 1), far_share, swap(shares[3], "dp", 3)]
     suffixes = local(suffix_kernel, parts.shape, parts, own_top)
     section_grads = lax.all_to_all(suffixes, "pipe", 0, 0).reshape(tokens, width)
     section_grads = local(copy_kernel, (tokens, width), section_grads)
@@ -288,10 +277,10 @@
     kv_grad = pl.pallas_call(
         functools.partial(term_kernel, scale),
         out_shape=jax.ShapeDtypeStruct((tensor // dp * 2 * HD, width), BF16),
-        in_specs=[VMEM] * 5,
+        in_specs=[VMEM] * (2 * dp),
         out_specs=VMEM,
         compiler_params=SMALL,
-    )(own_set, near_set, far_set, diagonal_share, diagonal_set)
+    )(*shares, *norms)
     gain_grad = lax.psum(gains * scale, "dp")
 
     return (section_grads[None, None], kv_grad[None], gain_grad)

time: 140 us -> 139 us (level)
  starting transfers between devices: 45.3 us -> 50.9 us
  waiting for transfers between devices: 52.1 us -> 48.7 us
  blocking collectives: 23 us -> 20.6 us
    ppermute x7 -> x9, starting transfers between devices: 16.7 us -> 22.4 us  [swap(): lax.ppermute(value, axis, [(source, source ^ distance) for source in rang...]
    ppermute x7 -> x9, waiting for transfers between devices: 35.9 us -> 32.6 us  [swap(): lax.ppermute(value, axis, [(source, source ^ distance) for source in rang...]
    psum x1, blocking collectives: 10.9 us -> 8.45 us  [body(): gain_grad = lax.psum(gains * scale, 'dp')]
  transfers between devices with their start and end apart: 10 -> 12, of which waited for: 5 -> 5; matrix products, arithmetic and copies ran while one was open for 1% -> 0% of each run, Pallas kernels for 9% -> 9%
where the time goes in v5:
time: 139 us; the launch traced here: 138 us
  starting transfers between devices  50.9 us (37%)
  waiting for transfers between devices  48.7 us (35%)
  blocking collectives  20.6 us (15%)
  Pallas kernels  15.9 us (11%)
  local copies, waits for them, and re-layouts  1.45 us (1%)
    ppermute x9, waiting for transfers between devices, swap(): lax.ppermute(value, axis, [(source, source ^ distance) for source in rang...  32.6 us
    ppermute x9, starting transfers between devices, swap(): lax.ppermute(value, axis, [(source, source ^ distance) for source in rang...  22.4 us
    all_to_all x1, starting transfers between devices, body(): lax.all_to_all(contrib.reshape(sections, small, width), 'pipe', 0, 0)  15.2 us
    all_to_all x1, blocking collectives, body(): prods = lax.all_to_all(prods, 'tensor', 0, 0)  12.2 us
    psum x1, blocking collectives, body(): gain_grad = lax.psum(gains * scale, 'dp')  8.45 us
    all_to_all x1, waiting for transfers between devices, body(): lax.all_to_all(contrib.reshape(sections, small, width), 'pipe', 0, 0)  8.08 us
    all_to_all x1, starting transfers between devices, body(): lax.all_to_all(suffixes, 'pipe', 0, 0).reshape(tokens, width)  6.68 us
    all_to_all x1, starting transfers between devices, body(): grad_kv = lax.all_to_all(copies, 'tensor', 0, 0)  6.65 us
  transfers between devices with their start and end apart: 12, of which 5 were waited for; matrix products, arithmetic and copies ran while one was open for 0% of the time, Pallas kernels for 9%

profile of v5, /device:TPU:32, one launch (start us, length us, event | category | flops | bytes accessed | tf_op | source)
XLA Modules:
  0.0 138.5 jit_solution(9966968616242287202)
XLA Ops:
  0.6 0.0 copy-start
  0.6 3.6 %collective-permute-start.1 = (bf16[512,1024]{1,0:T(8,128)(2,1)}, bf16[512,1024]{1,0:T(8,128)(2,1)}, u32[]{:S(2)}, u32[]{:S(2)}) collective-permute-start(bf16[512,1024]{1,0:T(8,128)(2,1)} %bitcast.13.own), channel_id=1, source_target_pairs={{0,256},{128,384},{256,0},{384,128},{1,257},{129,385},{257,1},{385... | collective-permute-start | bytes 3145736 | tf_op jit(solution)/shard_map/ppermute | solution.py:181
  4.3 6.2 %shard_map.112 = bf16[8,272,256]{2,1,0:T(8,128)(2,1)} custom-call(s32[1,4]{1,0:T(1,128)} %lengths.1, bf16[256,1024]{1,0:T(8,128)(2,1)} %bitcast.27, bf16[256,128]{1,0:T(8,128)(2,1)} %bitcast.29, bf16[256,128]{1,0:T(8,128)(2,1)} %bitcast.30, bf16[256,1024]{1,0:T(8,128)(2,1)} %bitcast.28, bf16[256,1024]{1,0:T(8,128)(2,1)} %bitcast.20), custom_call_target="tpu_custom_call" | custom-call | flops 30000001024 | bytes 4000000 | tf_op jit(solution)/shard_map/pallas_call | solution.py:203
  10.5 0.0 copy-start.1
  10.5 0.0 copy-start.7
  10.5 2.1 %collective-permute-start = (bf16[512,1024]{1,0:T(8,128)(2,1)}, bf16[512,1024]{1,0:T(8,128)(2,1)}, u32[]{:S(2)}, u32[]{:S(2)}) collective-permute-start(bf16[512,1024]{1,0:T(8,128)(2,1)} %bitcast.13.own), channel_id=1, source_target_pairs={{0,128},{128,0},{256,384},{384,256},{1,129},{129,1},{257,385},{385... | collective-permute-start | bytes 3145736 | tf_op jit(solution)/shard_map/ppermute | solution.py:181
  12.6 6.7 %all-to-all-start = ((bf16[8,272,256]{2,1,0:T(8,128)(2,1)}), bf16[8,272,256]{2,1,0:T(8,128)(2,1)S(1)}, u32[]{:S(2)}, u32[]{:S(2)}) async-start(bf16[8,272,256]{2,1,0:T(8,128)(2,1)} %shard_map.112), calls=%async_computation | async-start | bytes 2228224 | tf_op jit(solution)/shard_map/all_to_all | solution.py:222
  19.2 0.1 stack.35.order
  19.3 18.7 %collective-permute-done.1.far = bf16[512,1024]{1,0:T(8,128)(2,1)} collective-permute-done((bf16[512,1024]{1,0:T(8,128)(2,1)}, bf16[512,1024]{1,0:T(8,128)(2,1)}, u32[]{:S(2)}, u32[]{:S(2)}) %collective-permute-start.1) | collective-permute-done | bytes 1048608 | tf_op jit(solution)/shard_map/ppermute | solution.py:181
  38.0 1.9 %collective-permute-start.2 = (bf16[512,1024]{1,0:T(8,128)(2,1)}, bf16[512,1024]{1,0:T(8,128)(2,1)S(1)}, u32[]{:S(2)}, u32[]{:S(2)}) collective-permute-start(bf16[512,1024]{1,0:T(8,128)(2,1)} %collective-permute-done.1.far), channel_id=1, source_target_pairs={{0,128},{128,0},{256,384},{384,256},{1,129},{129,1},{257,385},{385... | collective-permute-start | bytes 3145736 | tf_op jit(solution)/shard_map/ppermute | solution.py:181
  39.9 2.3 %all-to-all-done.grad_kv = bf16[8,272,256]{2,1,0:T(8,128)(2,1)S(1)} async-done(((bf16[8,272,256]{2,1,0:T(8,128)(2,1)}), bf16[8,272,256]{2,1,0:T(8,128)(2,1)S(1)}, u32[]{:S(2)}, u32[]{:S(2)}) %all-to-all-start) | async-done | bytes 1114144 | tf_op jit(solution)/shard_map/all_to_all | solution.py:222
  42.2 0.0 collective-permute-done.near
  42.2 0.0 copy-done.1
  42.2 0.0 copy-done.7
  42.2 2.9 %shard_map.113 = (bf16[256,512]{1,0:T(8,128)(2,1)S(1)}, bf16[256,512]{1,0:T(8,128)(2,1)S(1)}, bf16[256,512]{1,0:T(8,128)(2,1)S(1)}, bf16[256,512]{1,0:T(8,128)(2...) custom-call(s32[8]{0:T(128)S(1)} %stack.35.order, ...), custom_call_target="tpu_custom_call" | custom-call | flops 30000001024 | tf_op jit(solution)/shard_map/pallas_call | solution.py:229
  45.1 0.0 copy-start.2
  45.1 0.0 copy-start.4
  45.1 0.0 copy-start.8
  45.1 0.0 copy-start.9
  45.1 0.0 collective-permute-done.2.piece
  45.1 0.6 shard_map.114
  45.7 0.1 copy-done.2
  45.9 0.1 copy-done.4
  46.0 0.1 copy-done.8
  46.0 0.1 copy-done.9
  46.1 12.2 %all_to_all.20.prods = f32[8,1,256]{2,1,0:T(1,128)S(1)} all-to-all(f32[8,1,256]{2,1,0:T(1,128)S(1)} %get-tuple-element.24), channel_id=1, replica_groups=mesh['dp'=4,'pipe'=16,'tensor'=8] {'tensor'}, dimensions={0} | all-to-all | bytes 16384 | tf_op jit(solution)/shard_map/all_to_all | solution.py:253
  58.3 0.0 copy-start.3
  58.3 0.0 copy-start.10
  58.3 1.1 shard_map.115
  59.4 15.2 %all-to-all-start.2 = ((bf16[16,16,1024]{2,1,0:T(8,128)(2,1)}), bf16[16,16,1024]{2,1,0:T(8,128)(2,1)S(1)}, u32[]{:S(2)}, u32[]{:S(2)}) async-start(bf16[16,16,1024]{2,1,0:T(8,128)(2,1)} %bitcast.14), calls=%async_computation.2 | async-start | bytes 1048576 | tf_op jit(solution)/shard_map/all_to_all | solution.py:269
  74.6 0.0 copy-done.3
  74.6 2.6 %collective-permute-start.3 = (bf16[256,1024]{1,0:T(8,128)(2,1)S(1)}, bf16[256,1024]{1,0:T(8,128)(2,1)S(1)}, u32[]{:S(2)}, u32[]{:S(2)}) collective-permute-start(bf16[256,1024]{1,0:T(8,128)(2,1)S(1)} %copy-done.3), channel_id=1, source_target_pairs={{0,256},{128,384},{256,0},{384,128},{1,257},{129,385},{257,1},{385... | collective-permute-start | bytes 1572872 | tf_op jit(solution)/shard_map/ppermute | solution.py:181
  77.2 0.0 copy-done.10
  77.2 3.3 %collective-permute-start.4 = (bf16[256,512]{1,0:T(8,128)(2,1)S(1)}, bf16[256,512]{1,0:T(8,128)(2,1)S(1)}, u32[]{:S(2)}, u32[]{:S(2)}) collective-permute-start(bf16[256,512]{1,0:T(8,128)(2,1)S(1)} %copy-done.10), channel_id=1, source_target_pairs={{0,256},{128,384},{256,0},{384,128},{1,257},{129,385},{257,1},{385... | collective-permute-start | bytes 786440 | tf_op jit(solution)/shard_map/ppermute | solution.py:181
  80.5 0.0 copy-done
  80.5 14.0 %collective-permute-done.4.refs_2_ = bf16[256,512]{1,0:T(8,128)(2,1)S(1)} collective-permute-done((bf16[256,512]{1,0:T(8,128)(2,1)S(1)}, bf16[256,512]{1,0:T(8,128)(2,1)S(1)}, u32[]{:S(2)}, u32[]{:S(2)}) %collective-permute-start.4) | collective-permute-done | bytes 262176 | tf_op jit(solution)/shard_map/ppermute | solution.py:181
  94.5 0.0 copy-start.5
  94.5 0.0 collective-permute-done.3.refs_6_
  94.5 8.1 %all-to-all-done.2.parts = bf16[16,16,1024]{2,1,0:T(8,128)(2,1)S(1)} async-done(((bf16[16,16,1024]{2,1,0:T(8,128)(2,1)}), bf16[16,16,1024]{2,1,0:T(8,128)(2,1)S(1)}, u32[]{:S(2)}, u32[]{:S(2)}) %all-to-all-start.2) | async-done | bytes 524320 | tf_op jit(solution)/shard_map/all_to_all | solution.py:269
  102.6 0.9 shard_map.116
  103.4 0.0 copy-done.5
  103.4 6.7 %all-to-all-start.3 = ((bf16[16,16,1024]{2,1,0:T(8,128)(2,1)}), bf16[16,16,1024]{2,1,0:T(8,128)(2,1)S(1)}, u32[]{:S(2)}, u32[]{:S(2)}) async-start(bf16[16,16,1024]{2,1,0:T(8,128)(2,1)} %shard_map.116), calls=%async_computation.3 | async-start | bytes 1048576 | tf_op jit(solution)/shard_map/all_to_all | solution.py:274
  110.1 1.9 %collective-permute-start.7 = (bf16[256,1024]{1,0:T(8,128)(2,1)S(1)}, bf16[256,1024]{1,0:T(8,128)(2,1)S(1)}, u32[]{:S(2)}, u32[]{:S(2)}) collective-permute-start(bf16[256,1024]{1,0:T(8,128)(2,1)S(1)} %copy-done.3), channel_id=1, source_target_pairs={{0,128},{128,0},{256,384},{384,256},{1,129},{129,1},{257,385},{385... | collective-permute-start | bytes 1572872 | tf_op jit(solution)/shard_map/ppermute | solution.py:181
  112.0 2.4 %collective-permute-start.8 = (bf16[256,1024]{1,0:T(8,128)(2,1)S(1)}, bf16[256,1024]{1,0:T(8,128)(2,1)S(1)}, u32[]{:S(2)}, u32[]{:S(2)}) collective-permute-start(bf16[256,1024]{1,0:T(8,128)(2,1)S(1)} %collective-permute-done.3.refs_6_), channel_id=1, source_target_pairs={{0,128},{128,0},{256,384},{384,256},{1,129},{129,1},{257,385},{385... | collective-permute-start | bytes 1572872 | tf_op jit(solution)/shard_map/ppermute | solution.py:181
  114.5 2.2 %collective-permute-start.6 = (bf16[256,512]{1,0:T(8,128)(2,1)}, bf16[256,512]{1,0:T(8,128)(2,1)}, u32[]{:S(2)}, u32[]{:S(2)}) collective-permute-start(bf16[256,512]{1,0:T(8,128)(2,1)} %copy-done.4), channel_id=1, source_target_pairs={{0,384},{128,256},{256,128},{384,0},{1,385},{129,257},{257,129},{3... | collective-permute-start | bytes 786440 | tf_op jit(solution)/shard_map/ppermute | solution.py:181
  116.7 2.4 %collective-permute-start.5 = (bf16[256,512]{1,0:T(8,128)(2,1)}, bf16[256,512]{1,0:T(8,128)(2,1)}, u32[]{:S(2)}, u32[]{:S(2)}) collective-permute-start(bf16[256,512]{1,0:T(8,128)(2,1)} %copy-done.8), channel_id=1, source_target_pairs={{0,128},{128,0},{256,384},{384,256},{1,129},{129,1},{257,385},{385... | collective-permute-start | bytes 786440 | tf_op jit(solution)/shard_map/ppermute | solution.py:181
  119.1 8.5 %psum.7 = f32[1,1024]{1,0:T(1,128)} all-reduce(f32[1,1024]{1,0:T(1,128)S(1)} %broadcast_multiply_fusion), channel_id=1, replica_groups=mesh['dp'=4,'pipe'=16,'tensor'=8] {'dp'}, use_global_device_ids=true, to_apply=%region_0.0 | all-reduce | flops 1024 | bytes 8192 | tf_op jit(solution)/shard_map/psum | solution.py:284
  127.6 0.0 collective-permute-done.6.refs_3_
  127.6 0.0 collective-permute-done.5.refs_1_
  127.6 0.0 collective-permute-done.7.refs_5_
  127.6 0.0 collective-permute-done.8.refs_7_
  127.6 0.0 copy-start.6
  127.6 0.9 copy-done.6
  128.5 3.4 %shard_map.118 = bf16[512,1024]{1,0:T(8,128)(2,1)} custom-call(bf16[256,512]{1,0:T(8,128)(2,1)S(1)} %get-tuple-element.30.refs_0_, bf16[256,512]{1,0:T(8,128)(2,1)} %collective-permute-done.5.refs_1_, bf16[256,512]{1,0:T(8,128)(2,1)S(1)} %copy-done.6, bf16[256,512]{1,0:T(8,128)(2,1)} %collective-permute-done.6.refs_3_, bf16[256,1024]{1,0:T(8,128)(2,1)S(1)} %copy-done.3, ...), custom_call_target="tpu_custom_call" | custom-call | tf_op jit(solution)/shard_map/pallas_call | solution.py:277
  131.9 5.7 %all-to-all-done.3 = bf16[16,16,1024]{2,1,0:T(8,128)(2,1)S(1)} async-done(((bf16[16,16,1024]{2,1,0:T(8,128)(2,1)}), bf16[16,16,1024]{2,1,0:T(8,128)(2,1)S(1)}, u32[]{:S(2)}, u32[]{:S(2)}) %all-to-all-start.3) | async-done | bytes 524320 | tf_op jit(solution)/shard_map/all_to_all | solution.py:274
  137.7 0.8 shard_map.117
  (2 shorter events, 0.0 us)
Async XLA Ops:
  0.6 79.9 %copy-start = (bf16[1,256,1024]{2,1,0:T(8,128)(2,1)S(1)}, bf16[1,256,1024]{2,1,0:T(8,128)(2,1)}, u32[]{:S(2)}) copy-start(bf16[1,256,1024]{2,1,0:T(8,128)(2,1)} %param.16) | copy-start | bytes 1572868
  0.6 37.3 %collective-permute-start.1 = (bf16[512,1024]{1,0:T(8,128)(2,1)}, bf16[512,1024]{1,0:T(8,128)(2,1)}, u32[]{:S(2)}, u32[]{:S(2)}) collective-permute-start(bf16[512,1024]{1,0:T(8,128)(2,1)} %bitcast.13.own), channel_id=1, source_target_pairs={{0,256},{128,384},{256,0},{384,128},{1,257},{129,385},{257,1},{385... | collective-permute-start | bytes 3145736 | tf_op jit(solution)/shard_map/ppermute | solution.py:181
  10.5 31.7 %copy-start.1 = (bf16[1,1,256,1024]{3,2,1,0:T(8,128)(2,1)S(1)}, bf16[1,1,256,1024]{3,2,1,0:T(8,128)(2,1)}, u32[]{:S(2)}) copy-start(bf16[1,1,256,1024]{3,2,1,0:T(8,128)(2,1)} %param.9) | copy-start | bytes 1572868
  10.5 31.7 %copy-start.7 = (f32[1,1024]{1,0:T(1,128)S(1)}, f32[1,1024]{1,0:T(1,128)}, u32[]{:S(2)}) copy-start(f32[1,1024]{1,0:T(1,128)} %gain.3) | copy-start | bytes 12292
  10.5 31.6 %collective-permute-start = (bf16[512,1024]{1,0:T(8,128)(2,1)}, bf16[512,1024]{1,0:T(8,128)(2,1)}, u32[]{:S(2)}, u32[]{:S(2)}) collective-permute-start(bf16[512,1024]{1,0:T(8,128)(2,1)} %bitcast.13.own), channel_id=1, source_target_pairs={{0,128},{128,0},{256,384},{384,256},{1,129},{129,1},{257,385},{385... | collective-permute-start | bytes 3145736 | tf_op jit(solution)/shard_map/ppermute | solution.py:181
  12.6 29.6 %all-to-all-start = ((bf16[8,272,256]{2,1,0:T(8,128)(2,1)}), bf16[8,272,256]{2,1,0:T(8,128)(2,1)S(1)}, u32[]{:S(2)}, u32[]{:S(2)}) async-start(bf16[8,272,256]{2,1,0:T(8,128)(2,1)} %shard_map.112), calls=%async_computation | async-start | bytes 2228224 | tf_op jit(solution)/shard_map/all_to_all | solution.py:222
  38.0 7.1 %collective-permute-start.2 = (bf16[512,1024]{1,0:T(8,128)(2,1)}, bf16[512,1024]{1,0:T(8,128)(2,1)S(1)}, u32[]{:S(2)}, u32[]{:S(2)}) collective-permute-start(bf16[512,1024]{1,0:T(8,128)(2,1)} %collective-permute-done.1.far), channel_id=1, source_target_pairs={{0,128},{128,0},{256,384},{384,256},{1,129},{129,1},{257,385},{385... | collective-permute-start | bytes 3145736 | tf_op jit(solution)/shard_map/ppermute | solution.py:181
  45.1 0.8 copy-start.2
  45.1 0.9 copy-start.4
  45.1 0.9 copy-start.8
  45.1 1.0 copy-start.9
  58.3 16.3 %copy-start.3 = (bf16[256,1024]{1,0:T(8,128)(2,1)S(1)}, bf16[256,1024]{1,0:T(8,128)(2,1)}, u32[]{:S(2)}) copy-start(bf16[256,1024]{1,0:T(8,128)(2,1)} %copy-done.2) | copy-start | bytes 1572868
  58.3 18.9 %copy-start.10 = (bf16[256,512]{1,0:T(8,128)(2,1)S(1)}, bf16[256,512]{1,0:T(8,128)(2,1)}, u32[]{:S(2)}) copy-start(bf16[256,512]{1,0:T(8,128)(2,1)} %copy-done.9) | copy-start | bytes 786436
  59.4 43.2 %all-to-all-start.2 = ((bf16[16,16,1024]{2,1,0:T(8,128)(2,1)}), bf16[16,16,1024]{2,1,0:T(8,128)(2,1)S(1)}, u32[]{:S(2)}, u32[]{:S(2)}) async-start(bf16[16,16,1024]{2,1,0:T(8,128)(2,1)} %bitcast.14), calls=%async_computation.2 | async-start | bytes 1048576 | tf_op jit(solution)/shard_map/all_to_all | solution.py:269
  74.6 19.9 %collective-permute-start.3 = (bf16[256,1024]{1,0:T(8,128)(2,1)S(1)}, bf16[256,1024]{1,0:T(8,128)(2,1)S(1)}, u32[]{:S(2)}, u32[]{:S(2)}) collective-permute-start(bf16[256,1024]{1,0:T(8,128)(2,1)S(1)} %copy-done.3), channel_id=1, source_target_pairs={{0,256},{128,384},{256,0},{384,128},{1,257},{129,385},{257,1},{385... | collective-permute-start | bytes 1572872 | tf_op jit(solution)/shard_map/ppermute | solution.py:181
  77.2 17.3 %collective-permute-start.4 = (bf16[256,512]{1,0:T(8,128)(2,1)S(1)}, bf16[256,512]{1,0:T(8,128)(2,1)S(1)}, u32[]{:S(2)}, u32[]{:S(2)}) collective-permute-start(bf16[256,512]{1,0:T(8,128)(2,1)S(1)} %copy-done.10), channel_id=1, source_target_pairs={{0,256},{128,384},{256,0},{384,128},{1,257},{129,385},{257,1},{385... | collective-permute-start | bytes 786440 | tf_op jit(solution)/shard_map/ppermute | solution.py:181
  94.5 9.0 %copy-start.5 = (bf16[256,512]{1,0:T(8,128)(2,1)}, bf16[256,512]{1,0:T(8,128)(2,1)S(1)}, u32[]{:S(2)}) copy-start(bf16[256,512]{1,0:T(8,128)(2,1)S(1)} %collective-permute-done.4.refs_2_) | copy-start | bytes 786436
  103.4 34.2 %all-to-all-start.3 = ((bf16[16,16,1024]{2,1,0:T(8,128)(2,1)}), bf16[16,16,1024]{2,1,0:T(8,128)(2,1)S(1)}, u32[]{:S(2)}, u32[]{:S(2)}) async-start(bf16[16,16,1024]{2,1,0:T(8,128)(2,1)} %shard_map.116), calls=%async_computation.3 | async-start | bytes 1048576 | tf_op jit(solution)/shard_map/all_to_all | solution.py:274
  110.1 17.4 %collective-permute-start.7 = (bf16[256,1024]{1,0:T(8,128)(2,1)S(1)}, bf16[256,1024]{1,0:T(8,128)(2,1)S(1)}, u32[]{:S(2)}, u32[]{:S(2)}) collective-permute-start(bf16[256,1024]{1,0:T(8,128)(2,1)S(1)} %copy-done.3), channel_id=1, source_target_pairs={{0,128},{128,0},{256,384},{384,256},{1,129},{129,1},{257,385},{385... | collective-permute-start | bytes 1572872 | tf_op jit(solution)/shard_map/ppermute | solution.py:181
  112.0 15.5 %collective-permute-start.8 = (bf16[256,1024]{1,0:T(8,128)(2,1)S(1)}, bf16[256,1024]{1,0:T(8,128)(2,1)S(1)}, u32[]{:S(2)}, u32[]{:S(2)}) collective-permute-start(bf16[256,1024]{1,0:T(8,128)(2,1)S(1)} %collective-permute-done.3.refs_6_), channel_id=1, source_target_pairs={{0,128},{128,0},{256,384},{384,256},{1,129},{129,1},{257,385},{385... | collective-permute-start | bytes 1572872 | tf_op jit(solution)/shard_map/ppermute | solution.py:181
  114.5 13.1 %collective-permute-start.6 = (bf16[256,512]{1,0:T(8,128)(2,1)}, bf16[256,512]{1,0:T(8,128)(2,1)}, u32[]{:S(2)}, u32[]{:S(2)}) collective-permute-start(bf16[256,512]{1,0:T(8,128)(2,1)} %copy-done.4), channel_id=1, source_target_pairs={{0,384},{128,256},{256,128},{384,0},{1,385},{129,257},{257,129},{3... | collective-permute-start | bytes 786440 | tf_op jit(solution)/shard_map/ppermute | solution.py:181
  116.7 10.9 %collective-permute-start.5 = (bf16[256,512]{1,0:T(8,128)(2,1)}, bf16[256,512]{1,0:T(8,128)(2,1)}, u32[]{:S(2)}, u32[]{:S(2)}) collective-permute-start(bf16[256,512]{1,0:T(8,128)(2,1)} %copy-done.8), channel_id=1, source_target_pairs={{0,128},{128,0},{256,384},{384,256},{1,129},{129,1},{257,385},{385... | collective-permute-start | bytes 786440 | tf_op jit(solution)/shard_map/ppermute | solution.py:181
  127.6 1.0 copy-start.6

commit v6 on v5

--- a/solution.py
+++ b/solution.py
@@ -13,7 +13,6 @@
 HD = 128
 GROUP = H // KVH
 EPSILON = 1e-05
-EXTRA = 16
 LOG2E = 1.4426950408889634
 F32 = jnp.float32
 BF16 = jnp.bfloat16
@@ -52,17 +51,8 @@
     return jnp.sum(jnp.where(across == down, row, 0.0), axis=1, keepdims=True)
 
 
-def in_three_rows(row):
-    high = row.astype(BF16).astype(F32)
-    middle = (row - high).astype(BF16).astype(F32)
-    low = row - high - middle
-    place = lax.broadcasted_iota(jnp.int32, (EXTRA, row.shape[1]), 0)
-    rows = jnp.where(place == 0, high, jnp.where(place == 1, middle, jnp.where(place == 2, low, 0.0)))
-    return rows.astype(BF16)
-
-
-def attention_kernel(lengths, query, key, value, out_grad, inputs, out, *scratch):
-    query_v, key_v, value_v, grad_v, inputs_v, result, sems, out_sems = scratch
+def attention_kernel(lengths, query, key, value, out_grad, out, *scratch):
+    query_v, key_v, value_v, grad_v, result, sems, out_sems = scratch
     tokens = query.shape[0]
     loads = [pltpu.make_async_copy(key, key_v, sems.at[0]), pltpu.make_async_copy(value, value_v, sems.at[1])]
     step = 2 * HD
@@ -70,7 +60,6 @@
         span = pl.ds(part * step, step)
         loads.append(pltpu.make_async_copy(query.at[:, span], query_v.at[:, span], sems.at[2 + 2 * part]))
         loads.append(pltpu.make_async_copy(out_grad.at[:, span], grad_v.at[:, span], sems.at[3 + 2 * part]))
-    loads.append(pltpu.make_async_copy(inputs, inputs_v, sems.at[2 + GROUP]))
     for load in loads:
         load.start()
     key_place = lax.broadcasted_iota(jnp.int32, (tokens, tokens), 0)
@@ -102,13 +91,9 @@
         centre = jnp.sum(probs * grad_probs, axis=0, keepdims=True)
         grad_scores = (probs * ((grad_probs - centre) * factor)).astype(BF16)
         grad_keys += nn(grad_scores, rows)
-    loads[2 + GROUP].wait()
-    wide = inputs_v[...].astype(F32)
-    extra = in_three_rows(to_row(jnp.sum(wide * wide, axis=1, keepdims=True)))
     grad_keys, grad_values = grad_keys.astype(BF16), grad_values.astype(BF16)
-    result[:tokens, :HD] = grad_keys
-    result[:tokens, HD:] = grad_values
-    result[tokens:, :] = extra
+    result[:, :HD] = grad_keys
+    result[:, HD:] = grad_values
     stores = [
         pltpu.make_async_copy(result, out.at[copy], out_sems.at[copy])
         for copy in range(out.shape[0])
@@ -119,41 +104,42 @@
         store.wait()
 
 
-def gather_kernel(order, grad_kv, own, near, far, rows, gain, *outs):
-    shares, (norm_out, total_out, inverse_out) = outs[:4], outs[4:]
-    tokens, width = rows.shape
-    half = width // 2
-    sums = jnp.zeros((EXTRA, tokens), F32)
-    for block in range(grad_kv.shape[0]):
-        sums = sums + grad_kv[block, tokens:, :].astype(F32)
-    inverse = to_column(1.0 / jnp.sqrt(jnp.sum(sums, axis=0, keepdims=True) * (1.0 / D) + EPSILON))
-    inverse_out[...] = inverse
+def gather_kernel(order, grad_kv, own, near, far, rows, *outs):
+    shares, (total_out, squares_out) = outs[:4], outs[4:]
     for place, share in enumerate(shares):
         for part in range(2):
             span = slice(part * 2 * HD, (part + 1) * 2 * HD)
-            share[:, span] = grad_kv[order[2 * place + part], :tokens, :]
+            share[:, span] = grad_kv[order[2 * place + part]]
+    wide = rows[...].astype(F32)
+    squares_out[...] = to_row(jnp.sum(wide * wide, axis=1, keepdims=True))
     total_out[...] = (
         nn(shares[0][...], own[...]) + nn(shares[1][...], near[...]) + nn(shares[2][...], far[...])
     )
-    norm_out[...] = (rows[...].astype(F32) * inverse * gain[...]).astype(BF16)
-
-
-def project_kernel(part, share, piece, rows, gain, inverse, scaled_out, prods, gains_out):
+
+
+def project_kernel(part, share, piece, rows, gain, squares, total_out, sums_out):
     total = part[...] + nn(share[...], piece[...])
+    total_out[...] = total
+    prods = to_row(jnp.sum(total * gain[...] * rows[...].astype(F32), axis=1, keepdims=True))
+    for copy in range(sums_out.shape[0]):
+        sums_out[copy, 0:1, :] = prods
+        sums_out[copy, 1:2, :] = squares[...]
+
+
+def contrib_kernel(sums, total, rows, gain, out, inverse_out):
+    sums = jnp.sum(sums[...], axis=0)
+    across = 1.0 / jnp.sqrt(sums[1:2, :] * (1.0 / D) + EPSILON)
+    mean = to_column(sums[0:1, :] * across * (1.0 / D))
+    inverse = to_column(across)
+    inverse_out[...] = inverse
+    unit = rows[...].astype(F32) * inverse
+    out[...] = ((total[...] * gain[...] - unit * mean) * inverse).astype(BF16)
+
+
+def norm_kernel(rows, gain, inverse, total, out, gains_out):
     unit = rows[...].astype(F32) * inverse[...]
-    scaled = total * gain[...]
-    scaled_out[...] = scaled
-    gains_out[...] = jnp.sum(total * unit, axis=0, keepdims=True)
-    sums = to_row(jnp.sum(scaled * unit, axis=1, keepdims=True))
-    for copy in range(prods.shape[0]):
-        prods[copy] = sums
-
-
-def contrib_kernel(prods, scaled, rows, inverse, out):
-    mean = to_column(jnp.sum(prods[...], axis=0) * (1.0 / D))
-    scale = inverse[...]
-    unit = rows[...].astype(F32) * scale
-    out[...] = ((scaled[...] - unit * mean) * scale).astype(BF16)
+    out[...] = (unit * gain[...]).astype(BF16)
+    gains_out[...] = jnp.sum(total[...] * unit, axis=0, keepdims=True)
 
 
 def term_kernel(scale, *refs):
@@ -202,22 +188,21 @@
 
     copies = pl.pallas_call(
         attention_kernel,
-        out_shape=jax.ShapeDtypeStruct((tensor, tokens + EXTRA, 2 * HD), BF16),
-        in_specs=[SMEM] + [ANY] * 5,
+        out_shape=jax.ShapeDtypeStruct((tensor, tokens, 2 * HD), BF16),
+        in_specs=[SMEM] + [ANY] * 4,
         out_specs=ANY,
         scratch_shapes=[
             pltpu.VMEM((tokens, GROUP * HD), BF16),
             pltpu.VMEM((tokens, HD), BF16),
             pltpu.VMEM((tokens, HD), BF16),
             pltpu.VMEM((tokens, GROUP * HD), BF16),
-            pltpu.VMEM((tokens, width), BF16),
-            pltpu.VMEM((tokens + EXTRA, 2 * HD), BF16),
-            pltpu.SemaphoreType.DMA((3 + GROUP,)),
+            pltpu.VMEM((tokens, 2 * HD), BF16),
+            pltpu.SemaphoreType.DMA((2 + GROUP,)),
             pltpu.SemaphoreType.DMA((tensor,)),
         ],
         compiler_params=WHOLE,
         cost_estimate=pl.CostEstimate(flops=int(3e+10), bytes_accessed=4000000, transcendentals=0),
-    )(doc_lengths, queries[0, 0], saved_keys[0, 0], saved_values[0, 0], attn_out_grad[0, 0], rows)
+    )(doc_lengths, queries[0, 0], saved_keys[0, 0], saved_values[0, 0], attn_out_grad[0, 0])
     copies, whole = lax.optimization_barrier((copies, own))
     grad_kv = lax.all_to_all(copies, "tensor", 0, 0)
     near = swap(whole, "dp", 1)
@@ -226,33 +211,23 @@
 
     wide = jax.ShapeDtypeStruct((tokens, width), F32)
     share_shape = jax.ShapeDtypeStruct((tokens, tensor // dp * 2 * HD), BF16)
-    *shares, norm, total, inverse = pl.pallas_call(
+    *shares, total, squares = pl.pallas_call(
         gather_kernel,
         out_shape=(share_shape,) * dp
-        + (
-            jax.ShapeDtypeStruct((tokens, width), BF16),
-            wide,
-            jax.ShapeDtypeStruct((tokens, 1), F32),
-        ),
-        in_specs=[SMEM] + [VMEM] * 6,
-        out_specs=(VMEM,) * (dp + 3),
+        + (wide, jax.ShapeDtypeStruct((1, tokens), F32)),
+        in_specs=[SMEM] + [VMEM] * 5,
+        out_specs=(VMEM,) * (dp + 2),
         compiler_params=PARAMS,
         cost_estimate=pl.CostEstimate(flops=int(3e10), bytes_accessed=0, transcendentals=0),
-    )(jnp.stack(order).astype(jnp.int32), grad_kv, own, near, far, rows, norm_gain)
-    scaled, prods, gains = pl.pallas_call(
+    )(jnp.stack(order).astype(jnp.int32), grad_kv, own, near, far, rows)
+    total, sums = pl.pallas_call(
         project_kernel,
-        out_shape=(
-            wide,
-            jax.ShapeDtypeStruct((tensor, 1, tokens), F32),
-            jax.ShapeDtypeStruct((1, width), F32),
-        ),
+        out_shape=(wide, jax.ShapeDtypeStruct((tensor, 2, tokens), F32)),
         in_specs=[VMEM] * 6,
-        out_specs=(VMEM,) * 3,
+        out_specs=(VMEM,) * 2,
         compiler_params=PARAMS,
-    )(total, shares[3], far_near, rows, norm_gain, inverse)
-    prods = lax.all_to_all(prods, "tensor", 0, 0)
-
-    far_norm, far_share = swap(norm, "dp", 2), swap(shares[2], "dp", 2)
+    )(total, shares[3], far_near, rows, norm_gain, squares)
+    sums = lax.all_to_all(sums, "tensor", 0, 0)
 
     def local(kernel, shape, *operands):
         return pl.pallas_call(
@@ -263,9 +238,29 @@
             compiler_params=SMALL,
         )(*operands)
 
-    contrib = local(contrib_kernel, (tokens, width), prods, scaled, rows, inverse)
+    contrib, inverse = pl.pallas_call(
+        contrib_kernel,
+        out_shape=(
+            jax.ShapeDtypeStruct((tokens, width), BF16),
+            jax.ShapeDtypeStruct((tokens, 1), F32),
+        ),
+        in_specs=[VMEM] * 4,
+        out_specs=(VMEM,) * 2,
+        compiler_params=SMALL,
+    )(sums, total, rows, norm_gain)
     small = tokens // sections
+    norm, gains = pl.pallas_call(
+        norm_kernel,
+        out_shape=(
+            jax.ShapeDtypeStruct((tokens, width), BF16),
+            jax.ShapeDtypeStruct((1, width), F32),
+        ),
+        in_specs=[VMEM] * 4,
+        out_specs=(VMEM,) * 2,
+        compiler_params=SMALL,
+    )(rows, norm_gain, inverse, total)
     own_top = lax.dynamic_slice_in_dim(top_grad[0], stage * small, small, 0)
+    far_norm, far_share = swap(norm, "dp", 2), swap(shares[2], "dp", 2)
     parts = lax.all_to_all(contrib.reshape(sections, small, width), "pipe", 0, 0)
     parts, far_norm, far_share, gains = lax.optimization_barrier((parts, far_norm, far_share, gains))
     norms = [norm, swap(norm, "dp", 1), far_norm, swap(far_norm, "dp", 1)]

time: 139 us -> 140 us (level)
    pallas_call x1 -> x3, Pallas kernels: 2.88 us -> 4.8 us  [the longest x1 3.43 us: body(): pl.pallas_call(gather_kernel, out_shape=(share_shape,) * dp + (wide, jax....]
    pallas_call x3 -> x2, Pallas kernels: 2.82 us -> 1.71 us  [local(): pl.pallas_call(kernel, out_shape=jax.ShapeDtypeStruct(shape, BF16), in_sp...]
where the time goes in v6:
time: 140 us; the launch traced here: 139 us
  starting transfers between devices  50.9 us (36%)
  waiting for transfers between devices  48.1 us (34%)
  blocking collectives  20.8 us (15%)
  Pallas kernels  16.4 us (12%)
  local copies, waits for them, and re-layouts  1.75 us (1%)
    ppermute x9, waiting for transfers between devices, swap(): lax.ppermute(value, axis, [(source, source ^ distance) for source in rang...  32.4 us
    ppermute x9, starting transfers between devices, swap(): lax.ppermute(value, axis, [(source, source ^ distance) for source in rang...  22.4 us
    all_to_all x1, starting transfers between devices, body(): lax.all_to_all(contrib.reshape(sections, small, width), 'pipe', 0, 0)  15.2 us
    all_to_all x1, blocking collectives, body(): sums = lax.all_to_all(sums, 'tensor', 0, 0)  12.4 us
    psum x1, blocking collectives, body(): gain_grad = lax.psum(gains * scale, 'dp')  8.45 us
    all_to_all x1, waiting for transfers between devices, body(): lax.all_to_all(contrib.reshape(sections, small, width), 'pipe', 0, 0)  7.83 us
    all_to_all x1, starting transfers between devices, body(): lax.all_to_all(suffixes, 'pipe', 0, 0).reshape(tokens, width)  6.67 us
    all_to_all x1, starting transfers between devices, body(): grad_kv = lax.all_to_all(copies, 'tensor', 0, 0)  6.65 us
  transfers between devices with their start and end apart: 12, of which 5 were waited for; matrix products, arithmetic and copies ran while one was open for 0% of the time, Pallas kernels for 9%

profile of v6, /device:TPU:32, one launch (start us, length us, event | category | flops | bytes accessed | tf_op | source)
XLA Modules:
  0.0 138.8 jit_solution(3476094122462069964)
XLA Ops:
  0.6 0.0 copy-start
  0.6 3.6 %collective-permute-start.1 = (bf16[512,1024]{1,0:T(8,128)(2,1)}, bf16[512,1024]{1,0:T(8,128)(2,1)}, u32[]{:S(2)}, u32[]{:S(2)}) collective-permute-start(bf16[512,1024]{1,0:T(8,128)(2,1)} %bitcast.12.own), channel_id=1, source_target_pairs={{0,256},{128,384},{256,0},{384,128},{1,257},{129,385},{257,1},{385... | collective-permute-start | bytes 3145736 | tf_op jit(solution)/shard_map/ppermute | solution.py:167
  4.3 6.0 %shard_map.112 = bf16[8,256,256]{2,1,0:T(8,128)(2,1)} custom-call(s32[1,4]{1,0:T(1,128)} %lengths.1, bf16[256,1024]{1,0:T(8,128)(2,1)} %bitcast.27, bf16[256,128]{1,0:T(8,128)(2,1)} %bitcast.29, bf16[256,128]{1,0:T(8,128)(2,1)} %bitcast.30, bf16[256,1024]{1,0:T(8,128)(2,1)} %bitcast.28), custom_call_target="tpu_custom_call" | custom-call | flops 30000001024 | bytes 4000000 | tf_op jit(solution)/shard_map/pallas_call | solution.py:189
  10.2 0.0 copy-start.1
  10.2 2.1 %collective-permute-start = (bf16[512,1024]{1,0:T(8,128)(2,1)}, bf16[512,1024]{1,0:T(8,128)(2,1)}, u32[]{:S(2)}, u32[]{:S(2)}) collective-permute-start(bf16[512,1024]{1,0:T(8,128)(2,1)} %bitcast.12.own), channel_id=1, source_target_pairs={{0,128},{128,0},{256,384},{384,256},{1,129},{129,1},{257,385},{385... | collective-permute-start | bytes 3145736 | tf_op jit(solution)/shard_map/ppermute | solution.py:167
  12.3 6.7 %all-to-all-start = ((bf16[8,256,256]{2,1,0:T(8,128)(2,1)}), bf16[8,256,256]{2,1,0:T(8,128)(2,1)S(1)}, u32[]{:S(2)}, u32[]{:S(2)}) async-start(bf16[8,256,256]{2,1,0:T(8,128)(2,1)} %shard_map.112), calls=%async_computation | async-start | bytes 2097152 | tf_op jit(solution)/shard_map/all_to_all | solution.py:207
  19.0 0.1 stack.35.order
  19.0 18.4 %collective-permute-done.1.far = bf16[512,1024]{1,0:T(8,128)(2,1)} collective-permute-done((bf16[512,1024]{1,0:T(8,128)(2,1)}, bf16[512,1024]{1,0:T(8,128)(2,1)}, u32[]{:S(2)}, u32[]{:S(2)}) %collective-permute-start.1) | collective-permute-done | bytes 1048608 | tf_op jit(solution)/shard_map/ppermute | solution.py:167
  37.5 1.9 %collective-permute-start.2 = (bf16[512,1024]{1,0:T(8,128)(2,1)}, bf16[512,1024]{1,0:T(8,128)(2,1)S(1)}, u32[]{:S(2)}, u32[]{:S(2)}) collective-permute-start(bf16[512,1024]{1,0:T(8,128)(2,1)} %collective-permute-done.1.far), channel_id=1, source_target_pairs={{0,128},{128,0},{256,384},{384,256},{1,129},{129,1},{257,385},{385... | collective-permute-start | bytes 3145736 | tf_op jit(solution)/shard_map/ppermute | solution.py:167
  39.4 2.1 %all-to-all-done.grad_kv = bf16[8,256,256]{2,1,0:T(8,128)(2,1)S(1)} async-done(((bf16[8,256,256]{2,1,0:T(8,128)(2,1)}), bf16[8,256,256]{2,1,0:T(8,128)(2,1)S(1)}, u32[]{:S(2)}, u32[]{:S(2)}) %all-to-all-start) | async-done | bytes 1048608 | tf_op jit(solution)/shard_map/all_to_all | solution.py:207
  41.5 0.0 collective-permute-done.near
  41.5 0.0 copy-done.1
  41.5 3.4 %shard_map.113 = (bf16[256,512]{1,0:T(8,128)(2,1)S(1)}, bf16[256,512]{1,0:T(8,128)(2,1)S(1)}, bf16[256,512]{1,0:T(8,128)(2,1)}, bf16[256,512]{1,0:T(8,128)(2,1)S...) custom-call(s32[8]{0:T(128)S(1)} %stack.35.order, bf16[8,256,256]{2,1,0:T(8,128)(2,1)S(1)} %all-to-all-done.grad_kv, ...), custom_call_target="tpu_custom_call" | custom-call | flops 30000001024 | tf_op jit(solution)/shard_map/pallas_call | solution.py:214
  44.9 0.0 copy-start.4
  44.9 0.0 copy-start.6
  44.9 0.0 copy-start.5
  44.9 0.0 collective-permute-done.2.piece
  44.9 0.7 copy-done.5
  45.6 0.6 shard_map.114
  46.2 0.0 copy-done.4
  46.2 0.0 copy-done.6
  46.2 12.4 %all_to_all.20.sums = f32[8,2,256]{2,1,0:T(2,128)S(1)} all-to-all(f32[8,2,256]{2,1,0:T(2,128)S(1)} %get-tuple-element.26), channel_id=1, replica_groups=mesh['dp'=4,'pipe'=16,'tensor'=8] {'tensor'}, dimensions={0} | all-to-all | bytes 32768 | tf_op jit(solution)/shard_map/all_to_all | solution.py:230
  58.6 1.1 shard_map.115
  59.7 15.2 %all-to-all-start.2 = ((bf16[16,16,1024]{2,1,0:T(8,128)(2,1)}), bf16[16,16,1024]{2,1,0:T(8,128)(2,1)S(1)}, u32[]{:S(2)}, u32[]{:S(2)}) async-start(bf16[16,16,1024]{2,1,0:T(8,128)(2,1)} %bitcast.14), calls=%async_computation.2 | async-start | bytes 1048576 | tf_op jit(solution)/shard_map/all_to_all | solution.py:264
  74.9 0.3 shard_map.116
  75.2 2.6 %collective-permute-start.3 = (bf16[256,1024]{1,0:T(8,128)(2,1)S(1)}, bf16[256,1024]{1,0:T(8,128)(2,1)S(1)}, u32[]{:S(2)}, u32[]{:S(2)}) collective-permute-start(bf16[256,1024]{1,0:T(8,128)(2,1)S(1)} %get-tuple-element.30.refs_4_), channel_id=1, source_target_pairs={{0,256},{128,384},{256,0},{384,128},{1,257},{129,385},{257,1},{385... | collective-permute-start | bytes 1572872 | tf_op jit(solution)/shard_map/ppermute | solution.py:167
  77.8 3.3 %collective-permute-start.4 = (bf16[256,512]{1,0:T(8,128)(2,1)}, bf16[256,512]{1,0:T(8,128)(2,1)S(1)}, u32[]{:S(2)}, u32[]{:S(2)}) collective-permute-start(bf16[256,512]{1,0:T(8,128)(2,1)} %get-tuple-element.31), channel_id=1, source_target_pairs={{0,256},{128,384},{256,0},{384,128},{1,257},{129,385},{257,1},{385... | collective-permute-start | bytes 786440 | tf_op jit(solution)/shard_map/ppermute | solution.py:167
  81.0 0.0 copy-done
  81.1 14.0 %collective-permute-done.4.refs_2_ = bf16[256,512]{1,0:T(8,128)(2,1)S(1)} collective-permute-done((bf16[256,512]{1,0:T(8,128)(2,1)}, bf16[256,512]{1,0:T(8,128)(2,1)S(1)}, u32[]{:S(2)}, u32[]{:S(2)}) %collective-permute-start.4) | collective-permute-done | bytes 262176 | tf_op jit(solution)/shard_map/ppermute | solution.py:167
  95.0 0.0 copy-start.2
  95.0 0.0 collective-permute-done.3.refs_6_
  95.0 7.8 %all-to-all-done.2.parts = bf16[16,16,1024]{2,1,0:T(8,128)(2,1)S(1)} async-done(((bf16[16,16,1024]{2,1,0:T(8,128)(2,1)}), bf16[16,16,1024]{2,1,0:T(8,128)(2,1)S(1)}, u32[]{:S(2)}, u32[]{:S(2)}) %all-to-all-start.2) | async-done | bytes 524320 | tf_op jit(solution)/shard_map/all_to_all | solution.py:264
  102.9 0.9 shard_map.117
  103.7 0.0 copy-done.2
  103.8 6.7 %all-to-all-start.3 = ((bf16[16,16,1024]{2,1,0:T(8,128)(2,1)}), bf16[16,16,1024]{2,1,0:T(8,128)(2,1)S(1)}, u32[]{:S(2)}, u32[]{:S(2)}) async-start(bf16[16,16,1024]{2,1,0:T(8,128)(2,1)} %shard_map.117), calls=%async_computation.3 | async-start | bytes 1048576 | tf_op jit(solution)/shard_map/all_to_all | solution.py:269
  110.4 1.9 %collective-permute-start.7 = (bf16[256,1024]{1,0:T(8,128)(2,1)S(1)}, bf16[256,1024]{1,0:T(8,128)(2,1)S(1)}, u32[]{:S(2)}, u32[]{:S(2)}) collective-permute-start(bf16[256,1024]{1,0:T(8,128)(2,1)S(1)} %get-tuple-element.30.refs_4_), channel_id=1, source_target_pairs={{0,128},{128,0},{256,384},{384,256},{1,129},{129,1},{257,385},{385... | collective-permute-start | bytes 1572872 | tf_op jit(solution)/shard_map/ppermute | solution.py:167
  112.3 2.4 %collective-permute-start.8 = (bf16[256,1024]{1,0:T(8,128)(2,1)S(1)}, bf16[256,1024]{1,0:T(8,128)(2,1)S(1)}, u32[]{:S(2)}, u32[]{:S(2)}) collective-permute-start(bf16[256,1024]{1,0:T(8,128)(2,1)S(1)} %collective-permute-done.3.refs_6_), channel_id=1, source_target_pairs={{0,128},{128,0},{256,384},{384,256},{1,129},{129,1},{257,385},{385... | collective-permute-start | bytes 1572872 | tf_op jit(solution)/shard_map/ppermute | solution.py:167
  114.8 2.2 %collective-permute-start.6 = (bf16[256,512]{1,0:T(8,128)(2,1)}, bf16[256,512]{1,0:T(8,128)(2,1)}, u32[]{:S(2)}, u32[]{:S(2)}) collective-permute-start(bf16[256,512]{1,0:T(8,128)(2,1)} %copy-done.4), channel_id=1, source_target_pairs={{0,384},{128,256},{256,128},{384,0},{1,385},{129,257},{257,129},{3... | collective-permute-start | bytes 786440 | tf_op jit(solution)/shard_map/ppermute | solution.py:167
  117.0 2.4 %collective-permute-start.5 = (bf16[256,512]{1,0:T(8,128)(2,1)}, bf16[256,512]{1,0:T(8,128)(2,1)}, u32[]{:S(2)}, u32[]{:S(2)}) collective-permute-start(bf16[256,512]{1,0:T(8,128)(2,1)} %copy-done.6), channel_id=1, source_target_pairs={{0,128},{128,0},{256,384},{384,256},{1,129},{129,1},{257,385},{385... | collective-permute-start | bytes 786440 | tf_op jit(solution)/shard_map/ppermute | solution.py:167
  119.4 8.5 %psum.7 = f32[1,1024]{1,0:T(1,128)} all-reduce(f32[1,1024]{1,0:T(1,128)S(1)} %broadcast_multiply_fusion), channel_id=1, replica_groups=mesh['dp'=4,'pipe'=16,'tensor'=8] {'dp'}, use_global_device_ids=true, to_apply=%region_0.0 | all-reduce | flops 1024 | bytes 8192 | tf_op jit(solution)/shard_map/psum | solution.py:279
  127.8 0.0 collective-permute-done.6.refs_3_
  127.8 0.0 collective-permute-done.5.refs_1_
  127.9 0.0 collective-permute-done.7.refs_5_
  127.9 0.0 collective-permute-done.8.refs_7_
  127.9 0.0 copy-start.3
  127.9 0.9 copy-done.3
  128.8 3.4 %shard_map.119 = bf16[512,1024]{1,0:T(8,128)(2,1)} custom-call(bf16[256,512]{1,0:T(8,128)(2,1)S(1)} %get-tuple-element.34.refs_0_, bf16[256,512]{1,0:T(8,128)(2,1)} %collective-permute-done.5.refs_1_, bf16[256,512]{1,0:T(8,128)(2,1)S(1)} %copy-done.3, bf16[256,512]{1,0:T(8,128)(2,1)} %collective-permute-done.6.refs_3_, ...), custom_call_target="tpu_custom_call" | custom-call | tf_op jit(solution)/shard_map/pallas_call | solution.py:272
  132.2 5.7 %all-to-all-done.3 = bf16[16,16,1024]{2,1,0:T(8,128)(2,1)S(1)} async-done(((bf16[16,16,1024]{2,1,0:T(8,128)(2,1)}), bf16[16,16,1024]{2,1,0:T(8,128)(2,1)S(1)}, u32[]{:S(2)}, u32[]{:S(2)}) %all-to-all-start.3) | async-done | bytes 524320 | tf_op jit(solution)/shard_map/all_to_all | solution.py:269
  137.9 0.8 shard_map.118
  (2 shorter events, 0.0 us)
Async XLA Ops:
  0.6 80.4 %copy-start = (bf16[1,256,1024]{2,1,0:T(8,128)(2,1)S(1)}, bf16[1,256,1024]{2,1,0:T(8,128)(2,1)}, u32[]{:S(2)}) copy-start(bf16[1,256,1024]{2,1,0:T(8,128)(2,1)} %param.16) | copy-start | bytes 1572868
  0.6 36.8 %collective-permute-start.1 = (bf16[512,1024]{1,0:T(8,128)(2,1)}, bf16[512,1024]{1,0:T(8,128)(2,1)}, u32[]{:S(2)}, u32[]{:S(2)}) collective-permute-start(bf16[512,1024]{1,0:T(8,128)(2,1)} %bitcast.12.own), channel_id=1, source_target_pairs={{0,256},{128,384},{256,0},{384,128},{1,257},{129,385},{257,1},{385... | collective-permute-start | bytes 3145736 | tf_op jit(solution)/shard_map/ppermute | solution.py:167
  10.2 31.2 %copy-start.1 = (bf16[1,1,256,1024]{3,2,1,0:T(8,128)(2,1)S(1)}, bf16[1,1,256,1024]{3,2,1,0:T(8,128)(2,1)}, u32[]{:S(2)}) copy-start(bf16[1,1,256,1024]{3,2,1,0:T(8,128)(2,1)} %param.9) | copy-start | bytes 1572868
  10.2 31.2 %collective-permute-start = (bf16[512,1024]{1,0:T(8,128)(2,1)}, bf16[512,1024]{1,0:T(8,128)(2,1)}, u32[]{:S(2)}, u32[]{:S(2)}) collective-permute-start(bf16[512,1024]{1,0:T(8,128)(2,1)} %bitcast.12.own), channel_id=1, source_target_pairs={{0,128},{128,0},{256,384},{384,256},{1,129},{129,1},{257,385},{385... | collective-permute-start | bytes 3145736 | tf_op jit(solution)/shard_map/ppermute | solution.py:167
  12.3 29.2 %all-to-all-start = ((bf16[8,256,256]{2,1,0:T(8,128)(2,1)}), bf16[8,256,256]{2,1,0:T(8,128)(2,1)S(1)}, u32[]{:S(2)}, u32[]{:S(2)}) async-start(bf16[8,256,256]{2,1,0:T(8,128)(2,1)} %shard_map.112), calls=%async_computation | async-start | bytes 2097152 | tf_op jit(solution)/shard_map/all_to_all | solution.py:207
  37.5 7.5 %collective-permute-start.2 = (bf16[512,1024]{1,0:T(8,128)(2,1)}, bf16[512,1024]{1,0:T(8,128)(2,1)S(1)}, u32[]{:S(2)}, u32[]{:S(2)}) collective-permute-start(bf16[512,1024]{1,0:T(8,128)(2,1)} %collective-permute-done.1.far), channel_id=1, source_target_pairs={{0,128},{128,0},{256,384},{384,256},{1,129},{129,1},{257,385},{385... | collective-permute-start | bytes 3145736 | tf_op jit(solution)/shard_map/ppermute | solution.py:167
  44.9 1.3 copy-start.4
  44.9 1.3 copy-start.6
  44.9 0.7 copy-start.5
  59.7 43.2 %all-to-all-start.2 = ((bf16[16,16,1024]{2,1,0:T(8,128)(2,1)}), bf16[16,16,1024]{2,1,0:T(8,128)(2,1)S(1)}, u32[]{:S(2)}, u32[]{:S(2)}) async-start(bf16[16,16,1024]{2,1,0:T(8,128)(2,1)} %bitcast.14), calls=%async_computation.2 | async-start | bytes 1048576 | tf_op jit(solution)/shard_map/all_to_all | solution.py:264
  75.2 19.9 %collective-permute-start.3 = (bf16[256,1024]{1,0:T(8,128)(2,1)S(1)}, bf16[256,1024]{1,0:T(8,128)(2,1)S(1)}, u32[]{:S(2)}, u32[]{:S(2)}) collective-permute-start(bf16[256,1024]{1,0:T(8,128)(2,1)S(1)} %get-tuple-element.30.refs_4_), channel_id=1, source_target_pairs={{0,256},{128,384},{256,0},{384,128},{1,257},{129,385},{257,1},{385... | collective-permute-start | bytes 1572872 | tf_op jit(solution)/shard_map/ppermute | solution.py:167
  77.8 17.3 %collective-permute-start.4 = (bf16[256,512]{1,0:T(8,128)(2,1)}, bf16[256,512]{1,0:T(8,128)(2,1)S(1)}, u32[]{:S(2)}, u32[]{:S(2)}) collective-permute-start(bf16[256,512]{1,0:T(8,128)(2,1)} %get-tuple-element.31), channel_id=1, source_target_pairs={{0,256},{128,384},{256,0},{384,128},{1,257},{129,385},{257,1},{385... | collective-permute-start | bytes 786440 | tf_op jit(solution)/shard_map/ppermute | solution.py:167
  95.0 8.7 %copy-start.2 = (bf16[256,512]{1,0:T(8,128)(2,1)}, bf16[256,512]{1,0:T(8,128)(2,1)S(1)}, u32[]{:S(2)}) copy-start(bf16[256,512]{1,0:T(8,128)(2,1)S(1)} %collective-permute-done.4.refs_2_) | copy-start | bytes 786436
  103.8 34.2 %all-to-all-start.3 = ((bf16[16,16,1024]{2,1,0:T(8,128)(2,1)}), bf16[16,16,1024]{2,1,0:T(8,128)(2,1)S(1)}, u32[]{:S(2)}, u32[]{:S(2)}) async-start(bf16[16,16,1024]{2,1,0:T(8,128)(2,1)} %shard_map.117), calls=%async_computation.3 | async-start | bytes 1048576 | tf_op jit(solution)/shard_map/all_to_all | solution.py:269
  110.4 17.4 %collective-permute-start.7 = (bf16[256,1024]{1,0:T(8,128)(2,1)S(1)}, bf16[256,1024]{1,0:T(8,128)(2,1)S(1)}, u32[]{:S(2)}, u32[]{:S(2)}) collective-permute-start(bf16[256,1024]{1,0:T(8,128)(2,1)S(1)} %get-tuple-element.30.refs_4_), channel_id=1, source_target_pairs={{0,128},{128,0},{256,384},{384,256},{1,129},{129,1},{257,385},{385... | collective-permute-start | bytes 1572872 | tf_op jit(solution)/shard_map/ppermute | solution.py:167
  112.3 15.5 %collective-permute-start.8 = (bf16[256,1024]{1,0:T(8,128)(2,1)S(1)}, bf16[256,1024]{1,0:T(8,128)(2,1)S(1)}, u32[]{:S(2)}, u32[]{:S(2)}) collective-permute-start(bf16[256,1024]{1,0:T(8,128)(2,1)S(1)} %collective-permute-done.3.refs_6_), channel_id=1, source_target_pairs={{0,128},{128,0},{256,384},{384,256},{1,129},{129,1},{257,385},{385... | collective-permute-start | bytes 1572872 | tf_op jit(solution)/shard_map/ppermute | solution.py:167
  114.8 13.1 %collective-permute-start.6 = (bf16[256,512]{1,0:T(8,128)(2,1)}, bf16[256,512]{1,0:T(8,128)(2,1)}, u32[]{:S(2)}, u32[]{:S(2)}) collective-permute-start(bf16[256,512]{1,0:T(8,128)(2,1)} %copy-done.4), channel_id=1, source_target_pairs={{0,384},{128,256},{256,128},{384,0},{1,385},{129,257},{257,129},{3... | collective-permute-start | bytes 786440 | tf_op jit(solution)/shard_map/ppermute | solution.py:167
  117.0 10.9 %collective-permute-start.5 = (bf16[256,512]{1,0:T(8,128)(2,1)}, bf16[256,512]{1,0:T(8,128)(2,1)}, u32[]{:S(2)}, u32[]{:S(2)}) collective-permute-start(bf16[256,512]{1,0:T(8,128)(2,1)} %copy-done.6), channel_id=1, source_target_pairs={{0,128},{128,0},{256,384},{384,256},{1,129},{129,1},{257,385},{385... | collective-permute-start | bytes 786440 | tf_op jit(solution)/shard_map/ppermute | solution.py:167
  127.9 1.0 copy-start.3

commit v7 on v5

--- a/solution.py
+++ b/solution.py
@@ -119,10 +119,9 @@
         store.wait()
 
 
-def gather_kernel(order, grad_kv, own, near, far, rows, gain, *outs):
-    shares, (norm_out, total_out, inverse_out) = outs[:4], outs[4:]
-    tokens, width = rows.shape
-    half = width // 2
+def gather_kernel(order, grad_kv, own, near, far, *outs):
+    shares, (total_out, inverse_out) = outs[:4], outs[4:]
+    tokens = total_out.shape[0]
     sums = jnp.zeros((EXTRA, tokens), F32)
     for block in range(grad_kv.shape[0]):
         sums = sums + grad_kv[block, tokens:, :].astype(F32)
@@ -135,7 +134,10 @@
     total_out[...] = (
         nn(shares[0][...], own[...]) + nn(shares[1][...], near[...]) + nn(shares[2][...], far[...])
     )
-    norm_out[...] = (rows[...].astype(F32) * inverse * gain[...]).astype(BF16)
+
+
+def norm_kernel(rows, gain, inverse, out):
+    out[...] = (rows[...].astype(F32) * inverse[...] * gain[...]).astype(BF16)
 
 
 def project_kernel(part, share, piece, rows, gain, inverse, scaled_out, prods, gains_out):
@@ -226,19 +228,15 @@
 
     wide = jax.ShapeDtypeStruct((tokens, width), F32)
     share_shape = jax.ShapeDtypeStruct((tokens, tensor // dp * 2 * HD), BF16)
-    *shares, norm, total, inverse = pl.pallas_call(
+    *shares, total, inverse = pl.pallas_call(
         gather_kernel,
         out_shape=(share_shape,) * dp
-        + (
-            jax.ShapeDtypeStruct((tokens, width), BF16),
-            wide,
-            jax.ShapeDtypeStruct((tokens, 1), F32),
-        ),
-        in_specs=[SMEM] + [VMEM] * 6,
-        out_specs=(VMEM,) * (dp + 3),
+        + (wide, jax.ShapeDtypeStruct((tokens, 1), F32)),
+        in_specs=[SMEM] + [VMEM] * 4,
+        out_specs=(VMEM,) * (dp + 2),
         compiler_params=PARAMS,
         cost_estimate=pl.CostEstimate(flops=int(3e10), bytes_accessed=0, transcendentals=0),
-    )(jnp.stack(order).astype(jnp.int32), grad_kv, own, near, far, rows, norm_gain)
+    )(jnp.stack(order).astype(jnp.int32), grad_kv, own, near, far)
     scaled, prods, gains = pl.pallas_call(
         project_kernel,
         out_shape=(
@@ -252,7 +250,6 @@
     )(total, shares[3], far_near, rows, norm_gain, inverse)
     prods = lax.all_to_all(prods, "tensor", 0, 0)
 
-    far_norm, far_share = swap(norm, "dp", 2), swap(shares[2], "dp", 2)
 
     def local(kernel, shape, *operands):
         return pl.pallas_call(
@@ -266,6 +263,9 @@
     contrib = local(contrib_kernel, (tokens, width), prods, scaled, rows, inverse)
     small = tokens // sections
     own_top = lax.dynamic_slice_in_dim(top_grad[0], stage * small, small, 0)
+    contrib, late = lax.optimization_barrier((contrib, inverse))
+    norm = local(norm_kernel, (tokens, width), rows, norm_gain, late)
+    far_norm, far_share = swap(norm, "dp", 2), swap(shares[2], "dp", 2)
     parts = lax.all_to_all(contrib.reshape(sections, small, width), "pipe", 0, 0)
     parts, far_norm, far_share, gains = lax.optimization_barrier((parts, far_norm, far_share, gains))
     norms = [norm, swap(norm, "dp", 1), far_norm, swap(far_norm, "dp", 1)]

time: 139 us -> 139 us (level)
    pallas_call x3 -> x4, Pallas kernels: 2.82 us -> 3.02 us  [local(): pl.pallas_call(kernel, out_shape=jax.ShapeDtypeStruct(shape, BF16), in_sp...]
where the time goes in v7:
time: 139 us; the launch traced here: 138 us
  starting transfers between devices  50.9 us (37%)
  waiting for transfers between devices  48.7 us (35%)
  blocking collectives  20.6 us (15%)
  Pallas kernels  16.1 us (12%)
    ppermute x9, waiting for transfers between devices, swap(): lax.ppermute(value, axis, [(source, source ^ distance) for source in rang...  32.8 us
    ppermute x9, starting transfers between devices, swap(): lax.ppermute(value, axis, [(source, source ^ distance) for source in rang...  22.2 us
    all_to_all x1, starting transfers between devices, body(): lax.all_to_all(contrib.reshape(sections, small, width), 'pipe', 0, 0)  15.4 us
    all_to_all x1, blocking collectives, body(): prods = lax.all_to_all(prods, 'tensor', 0, 0)  12.2 us
    psum x1, blocking collectives, body(): gain_grad = lax.psum(gains * scale, 'dp')  8.45 us
    all_to_all x1, waiting for transfers between devices, body(): lax.all_to_all(contrib.reshape(sections, small, width), 'pipe', 0, 0)  7.9 us
    all_to_all x1, starting transfers between devices, body(): lax.all_to_all(suffixes, 'pipe', 0, 0).reshape(tokens, width)  6.68 us
    all_to_all x1, starting transfers between devices, body(): grad_kv = lax.all_to_all(copies, 'tensor', 0, 0)  6.65 us
  transfers between devices with their start and end apart: 12, of which 5 were waited for; matrix products, arithmetic and copies ran while one was open for 0% of the time, Pallas kernels for 9%

profile of v7, /device:TPU:32, one launch (start us, length us, event | category | flops | bytes accessed | tf_op | source)
XLA Modules:
  0.0 138.3 jit_solution(6214034830009526917)
XLA Ops:
  0.6 0.0 copy-start
  0.6 3.6 %collective-permute-start.1 = (bf16[512,1024]{1,0:T(8,128)(2,1)}, bf16[512,1024]{1,0:T(8,128)(2,1)}, u32[]{:S(2)}, u32[]{:S(2)}) collective-permute-start(bf16[512,1024]{1,0:T(8,128)(2,1)} %bitcast.13.own), channel_id=1, source_target_pairs={{0,256},{128,384},{256,0},{384,128},{1,257},{129,385},{257,1},{385... | collective-permute-start | bytes 3145736 | tf_op jit(solution)/shard_map/ppermute | solution.py:183
  4.3 6.2 %shard_map.112 = bf16[8,272,256]{2,1,0:T(8,128)(2,1)} custom-call(s32[1,4]{1,0:T(1,128)} %lengths.1, bf16[256,1024]{1,0:T(8,128)(2,1)} %bitcast.27, bf16[256,128]{1,0:T(8,128)(2,1)} %bitcast.29, bf16[256,128]{1,0:T(8,128)(2,1)} %bitcast.30, bf16[256,1024]{1,0:T(8,128)(2,1)} %bitcast.28, bf16[256,1024]{1,0:T(8,128)(2,1)} %bitcast.20), custom_call_target="tpu_custom_call" | custom-call | flops 30000001024 | bytes 4000000 | tf_op jit(solution)/shard_map/pallas_call | solution.py:205
  10.5 1.9 %collective-permute-start = (bf16[512,1024]{1,0:T(8,128)(2,1)}, bf16[512,1024]{1,0:T(8,128)(2,1)}, u32[]{:S(2)}, u32[]{:S(2)}) collective-permute-start(bf16[512,1024]{1,0:T(8,128)(2,1)} %bitcast.13.own), channel_id=1, source_target_pairs={{0,128},{128,0},{256,384},{384,256},{1,129},{129,1},{257,385},{385... | collective-permute-start | bytes 3145736 | tf_op jit(solution)/shard_map/ppermute | solution.py:183
  12.4 6.7 %all-to-all-start = ((bf16[8,272,256]{2,1,0:T(8,128)(2,1)}), bf16[8,272,256]{2,1,0:T(8,128)(2,1)S(1)}, u32[]{:S(2)}, u32[]{:S(2)}) async-start(bf16[8,272,256]{2,1,0:T(8,128)(2,1)} %shard_map.112), calls=%async_computation | async-start | bytes 2228224 | tf_op jit(solution)/shard_map/all_to_all | solution.py:224
  19.1 0.1 stack.35.order
  19.2 0.0 copy-start.1
  19.2 0.0 copy-start.7
  19.2 18.8 %collective-permute-done.1.far = bf16[512,1024]{1,0:T(8,128)(2,1)} collective-permute-done((bf16[512,1024]{1,0:T(8,128)(2,1)}, bf16[512,1024]{1,0:T(8,128)(2,1)}, u32[]{:S(2)}, u32[]{:S(2)}) %collective-permute-start.1) | collective-permute-done | bytes 1048608 | tf_op jit(solution)/shard_map/ppermute | solution.py:183
  38.0 1.9 %collective-permute-start.2 = (bf16[512,1024]{1,0:T(8,128)(2,1)}, bf16[512,1024]{1,0:T(8,128)(2,1)S(1)}, u32[]{:S(2)}, u32[]{:S(2)}) collective-permute-start(bf16[512,1024]{1,0:T(8,128)(2,1)} %collective-permute-done.1.far), channel_id=1, source_target_pairs={{0,128},{128,0},{256,384},{384,256},{1,129},{129,1},{257,385},{385... | collective-permute-start | bytes 3145736 | tf_op jit(solution)/shard_map/ppermute | solution.py:183
  39.9 2.3 %all-to-all-done.grad_kv = bf16[8,272,256]{2,1,0:T(8,128)(2,1)S(1)} async-done(((bf16[8,272,256]{2,1,0:T(8,128)(2,1)}), bf16[8,272,256]{2,1,0:T(8,128)(2,1)S(1)}, u32[]{:S(2)}, u32[]{:S(2)}) %all-to-all-start) | async-done | bytes 1114144 | tf_op jit(solution)/shard_map/all_to_all | solution.py:224
  42.2 0.0 collective-permute-done.near
  42.2 2.9 %shard_map.113 = (bf16[256,512]{1,0:T(8,128)(2,1)S(1)}, bf16[256,512]{1,0:T(8,128)(2,1)S(1)}, bf16[256,512]{1,0:T(8,128)(2,1)S(1)}, bf16[256,512]{1,0:T(8,128)(2...) custom-call(s32[8]{0:T(128)S(1)} %stack.35.order, bf16[8,272,256]{2,1,0:T(8,128)(2,1)S(1)} %all-to-all-done.grad_kv, ...), custom_call_target="tpu_custom_call" | custom-call | flops 30000001024 | tf_op jit(solution)/shard_map/pallas_call | solution.py:231
  45.0 0.0 copy-start.2
  45.1 0.0 copy-start.9
  45.1 0.0 copy-start.4
  45.1 0.0 copy-start.8
  45.1 0.0 collective-permute-done.2.piece
  45.1 0.0 copy-done.1
  45.1 0.0 copy-done.7
  45.1 0.6 shard_map.114
  45.8 0.0 copy-done.2
  45.8 0.0 copy-done.9
  45.8 12.2 %all_to_all.20.prods = f32[8,1,256]{2,1,0:T(1,128)S(1)} all-to-all(f32[8,1,256]{2,1,0:T(1,128)S(1)} %get-tuple-element.25), channel_id=1, replica_groups=mesh['dp'=4,'pipe'=16,'tensor'=8] {'tensor'}, dimensions={0} | all-to-all | bytes 16384 | tf_op jit(solution)/shard_map/all_to_all | solution.py:251
  58.0 1.1 shard_map.115
  59.1 0.0 copy-done.4
  59.1 0.0 copy-done.8
  59.1 0.0 copy-start.10
  59.1 15.4 %all-to-all-start.2 = ((bf16[16,16,1024]{2,1,0:T(8,128)(2,1)}), bf16[16,16,1024]{2,1,0:T(8,128)(2,1)S(1)}, u32[]{:S(2)}, u32[]{:S(2)}) async-start(bf16[16,16,1024]{2,1,0:T(8,128)(2,1)} %bitcast.14), calls=%async_computation.2 | async-start | bytes 1048576 | tf_op jit(solution)/shard_map/all_to_all | solution.py:269
  74.5 0.2 shard_map.116.refs_4_
  74.7 2.6 %collective-permute-start.3 = (bf16[256,1024]{1,0:T(8,128)(2,1)S(1)}, bf16[256,1024]{1,0:T(8,128)(2,1)S(1)}, u32[]{:S(2)}, u32[]{:S(2)}) collective-permute-start(bf16[256,1024]{1,0:T(8,128)(2,1)S(1)} %shard_map.116.refs_4_), channel_id=1, source_target_pairs={{0,256},{128,384},{256,0},{384,128},{1,257},{129,385},{257,1},{385... | collective-permute-start | bytes 1572872 | tf_op jit(solution)/shard_map/ppermute | solution.py:183
  77.2 0.0 copy-done.10
  77.3 3.3 %collective-permute-start.4 = (bf16[256,512]{1,0:T(8,128)(2,1)S(1)}, bf16[256,512]{1,0:T(8,128)(2,1)S(1)}, u32[]{:S(2)}, u32[]{:S(2)}) collective-permute-start(bf16[256,512]{1,0:T(8,128)(2,1)S(1)} %copy-done.10), channel_id=1, source_target_pairs={{0,256},{128,384},{256,0},{384,128},{1,257},{129,385},{257,1},{385... | collective-permute-start | bytes 786440 | tf_op jit(solution)/shard_map/ppermute | solution.py:183
  80.5 0.0 copy-start.3
  80.5 0.0 copy-done
  80.6 13.9 %collective-permute-done.4.refs_2_ = bf16[256,512]{1,0:T(8,128)(2,1)S(1)} collective-permute-done((bf16[256,512]{1,0:T(8,128)(2,1)S(1)}, bf16[256,512]{1,0:T(8,128)(2,1)S(1)}, u32[]{:S(2)}, u32[]{:S(2)}) %collective-permute-start.4) | collective-permute-done | bytes 262176 | tf_op jit(solution)/shard_map/ppermute | solution.py:183
  94.5 0.0 copy-start.5
  94.5 0.0 collective-permute-done.3.refs_6_
  94.5 7.9 %all-to-all-done.2.parts = bf16[16,16,1024]{2,1,0:T(8,128)(2,1)S(1)} async-done(((bf16[16,16,1024]{2,1,0:T(8,128)(2,1)}), bf16[16,16,1024]{2,1,0:T(8,128)(2,1)S(1)}, u32[]{:S(2)}, u32[]{:S(2)}) %all-to-all-start.2) | async-done | bytes 524320 | tf_op jit(solution)/shard_map/all_to_all | solution.py:269
  102.4 0.9 shard_map.117
  103.3 0.0 copy-done.5
  103.3 6.7 %all-to-all-start.3 = ((bf16[16,16,1024]{2,1,0:T(8,128)(2,1)}), bf16[16,16,1024]{2,1,0:T(8,128)(2,1)S(1)}, u32[]{:S(2)}, u32[]{:S(2)}) async-start(bf16[16,16,1024]{2,1,0:T(8,128)(2,1)} %shard_map.117), calls=%async_computation.3 | async-start | bytes 1048576 | tf_op jit(solution)/shard_map/all_to_all | solution.py:274
  110.0 1.9 %collective-permute-start.7 = (bf16[256,1024]{1,0:T(8,128)(2,1)S(1)}, bf16[256,1024]{1,0:T(8,128)(2,1)S(1)}, u32[]{:S(2)}, u32[]{:S(2)}) collective-permute-start(bf16[256,1024]{1,0:T(8,128)(2,1)S(1)} %shard_map.116.refs_4_), channel_id=1, source_target_pairs={{0,128},{128,0},{256,384},{384,256},{1,129},{129,1},{257,385},{385... | collective-permute-start | bytes 1572872 | tf_op jit(solution)/shard_map/ppermute | solution.py:183
  111.9 2.4 %collective-permute-start.8 = (bf16[256,1024]{1,0:T(8,128)(2,1)S(1)}, bf16[256,1024]{1,0:T(8,128)(2,1)S(1)}, u32[]{:S(2)}, u32[]{:S(2)}) collective-permute-start(bf16[256,1024]{1,0:T(8,128)(2,1)S(1)} %collective-permute-done.3.refs_6_), channel_id=1, source_target_pairs={{0,128},{128,0},{256,384},{384,256},{1,129},{129,1},{257,385},{385... | collective-permute-start | bytes 1572872 | tf_op jit(solution)/shard_map/ppermute | solution.py:183
  114.3 2.2 %collective-permute-start.6 = (bf16[256,512]{1,0:T(8,128)(2,1)}, bf16[256,512]{1,0:T(8,128)(2,1)}, u32[]{:S(2)}, u32[]{:S(2)}) collective-permute-start(bf16[256,512]{1,0:T(8,128)(2,1)} %copy-done.4), channel_id=1, source_target_pairs={{0,384},{128,256},{256,128},{384,0},{1,385},{129,257},{257,129},{3... | collective-permute-start | bytes 786440 | tf_op jit(solution)/shard_map/ppermute | solution.py:183
  116.5 2.4 %collective-permute-start.5 = (bf16[256,512]{1,0:T(8,128)(2,1)}, bf16[256,512]{1,0:T(8,128)(2,1)}, u32[]{:S(2)}, u32[]{:S(2)}) collective-permute-start(bf16[256,512]{1,0:T(8,128)(2,1)} %copy-done.8), channel_id=1, source_target_pairs={{0,128},{128,0},{256,384},{384,256},{1,129},{129,1},{257,385},{385... | collective-permute-start | bytes 786440 | tf_op jit(solution)/shard_map/ppermute | solution.py:183
  118.9 8.5 %psum.7 = f32[1,1024]{1,0:T(1,128)} all-reduce(f32[1,1024]{1,0:T(1,128)S(1)} %broadcast_multiply_fusion), channel_id=1, replica_groups=mesh['dp'=4,'pipe'=16,'tensor'=8] {'dp'}, use_global_device_ids=true, to_apply=%region_0.0 | all-reduce | flops 1024 | bytes 8192 | tf_op jit(solution)/shard_map/psum | solution.py:284
  127.4 0.0 collective-permute-done.6.refs_3_
  127.4 0.0 collective-permute-done.5.refs_1_
  127.4 0.0 collective-permute-done.7.refs_5_
  127.4 0.0 collective-permute-done.8.refs_7_
  127.4 0.0 copy-done.3
  127.4 0.0 copy-start.6
  127.4 0.9 copy-done.6
  128.4 3.4 %shard_map.119 = bf16[512,1024]{1,0:T(8,128)(2,1)} custom-call(bf16[256,512]{1,0:T(8,128)(2,1)S(1)} %copy-done.3, bf16[256,512]{1,0:T(8,128)(2,1)} %collective-permute-done.5.refs_1_, bf16[256,512]{1,0:T(8,128)(2,1)S(1)} %copy-done.6, bf16[256,512]{1,0:T(8,128)(2,1)} %collective-permute-done.6.refs_3_, bf16[256,1024]{1,0:T(8,128)(2,1)S(1)} %shard_map.116.refs_4_, ...), custom_call_target="tpu_custom_call" | custom-call | tf_op jit(solution)/shard_map/pallas_call | solution.py:277
  131.8 5.7 %all-to-all-done.3 = bf16[16,16,1024]{2,1,0:T(8,128)(2,1)S(1)} async-done(((bf16[16,16,1024]{2,1,0:T(8,128)(2,1)}), bf16[16,16,1024]{2,1,0:T(8,128)(2,1)S(1)}, u32[]{:S(2)}, u32[]{:S(2)}) %all-to-all-start.3) | async-done | bytes 524320 | tf_op jit(solution)/shard_map/all_to_all | solution.py:274
  137.5 0.8 shard_map.118
  (2 shorter events, 0.0 us)
Async XLA Ops:
  0.6 79.9 %copy-start = (bf16[1,256,1024]{2,1,0:T(8,128)(2,1)S(1)}, bf16[1,256,1024]{2,1,0:T(8,128)(2,1)}, u32[]{:S(2)}) copy-start(bf16[1,256,1024]{2,1,0:T(8,128)(2,1)} %param.16) | copy-start | bytes 1572868
  0.6 37.3 %collective-permute-start.1 = (bf16[512,1024]{1,0:T(8,128)(2,1)}, bf16[512,1024]{1,0:T(8,128)(2,1)}, u32[]{:S(2)}, u32[]{:S(2)}) collective-permute-start(bf16[512,1024]{1,0:T(8,128)(2,1)} %bitcast.13.own), channel_id=1, source_target_pairs={{0,256},{128,384},{256,0},{384,128},{1,257},{129,385},{257,1},{385... | collective-permute-start | bytes 3145736 | tf_op jit(solution)/shard_map/ppermute | solution.py:183
  10.5 31.7 %collective-permute-start = (bf16[512,1024]{1,0:T(8,128)(2,1)}, bf16[512,1024]{1,0:T(8,128)(2,1)}, u32[]{:S(2)}, u32[]{:S(2)}) collective-permute-start(bf16[512,1024]{1,0:T(8,128)(2,1)} %bitcast.13.own), channel_id=1, source_target_pairs={{0,128},{128,0},{256,384},{384,256},{1,129},{129,1},{257,385},{385... | collective-permute-start | bytes 3145736 | tf_op jit(solution)/shard_map/ppermute | solution.py:183
  12.4 29.7 %all-to-all-start = ((bf16[8,272,256]{2,1,0:T(8,128)(2,1)}), bf16[8,272,256]{2,1,0:T(8,128)(2,1)S(1)}, u32[]{:S(2)}, u32[]{:S(2)}) async-start(bf16[8,272,256]{2,1,0:T(8,128)(2,1)} %shard_map.112), calls=%async_computation | async-start | bytes 2228224 | tf_op jit(solution)/shard_map/all_to_all | solution.py:224
  19.2 25.9 %copy-start.1 = (bf16[1,1,256,1024]{3,2,1,0:T(8,128)(2,1)S(1)}, bf16[1,1,256,1024]{3,2,1,0:T(8,128)(2,1)}, u32[]{:S(2)}) copy-start(bf16[1,1,256,1024]{3,2,1,0:T(8,128)(2,1)} %param.9) | copy-start | bytes 1572868
  19.2 25.9 %copy-start.7 = (f32[1,1024]{1,0:T(1,128)S(1)}, f32[1,1024]{1,0:T(1,128)}, u32[]{:S(2)}) copy-start(f32[1,1024]{1,0:T(1,128)} %gain.3) | copy-start | bytes 12292
  38.0 7.1 %collective-permute-start.2 = (bf16[512,1024]{1,0:T(8,128)(2,1)}, bf16[512,1024]{1,0:T(8,128)(2,1)S(1)}, u32[]{:S(2)}, u32[]{:S(2)}) collective-permute-start(bf16[512,1024]{1,0:T(8,128)(2,1)} %collective-permute-done.1.far), channel_id=1, source_target_pairs={{0,128},{128,0},{256,384},{384,256},{1,129},{129,1},{257,385},{385... | collective-permute-start | bytes 3145736 | tf_op jit(solution)/shard_map/ppermute | solution.py:183
  45.0 0.7 copy-start.2
  45.1 0.8 copy-start.9
  45.1 14.0 %copy-start.4 = (bf16[256,512]{1,0:T(8,128)(2,1)}, bf16[256,512]{1,0:T(8,128)(2,1)S(1)}, u32[]{:S(2)}) copy-start(bf16[256,512]{1,0:T(8,128)(2,1)S(1)} %get-tuple-element.23.share) | copy-start | bytes 786436
  45.1 14.0 %copy-start.8 = (bf16[256,512]{1,0:T(8,128)(2,1)}, bf16[256,512]{1,0:T(8,128)(2,1)S(1)}, u32[]{:S(2)}) copy-start(bf16[256,512]{1,0:T(8,128)(2,1)S(1)} %get-tuple-element.33) | copy-start | bytes 786436
  59.1 18.1 %copy-start.10 = (bf16[256,512]{1,0:T(8,128)(2,1)S(1)}, bf16[256,512]{1,0:T(8,128)(2,1)}, u32[]{:S(2)}) copy-start(bf16[256,512]{1,0:T(8,128)(2,1)} %copy-done.9) | copy-start | bytes 786436
  59.1 43.3 %all-to-all-start.2 = ((bf16[16,16,1024]{2,1,0:T(8,128)(2,1)}), bf16[16,16,1024]{2,1,0:T(8,128)(2,1)S(1)}, u32[]{:S(2)}, u32[]{:S(2)}) async-start(bf16[16,16,1024]{2,1,0:T(8,128)(2,1)} %bitcast.14), calls=%async_computation.2 | async-start | bytes 1048576 | tf_op jit(solution)/shard_map/all_to_all | solution.py:269
  74.7 19.8 %collective-permute-start.3 = (bf16[256,1024]{1,0:T(8,128)(2,1)S(1)}, bf16[256,1024]{1,0:T(8,128)(2,1)S(1)}, u32[]{:S(2)}, u32[]{:S(2)}) collective-permute-start(bf16[256,1024]{1,0:T(8,128)(2,1)S(1)} %shard_map.116.refs_4_), channel_id=1, source_target_pairs={{0,256},{128,384},{256,0},{384,128},{1,257},{129,385},{257,1},{385... | collective-permute-start | bytes 1572872 | tf_op jit(solution)/shard_map/ppermute | solution.py:183
  77.3 17.2 %collective-permute-start.4 = (bf16[256,512]{1,0:T(8,128)(2,1)S(1)}, bf16[256,512]{1,0:T(8,128)(2,1)S(1)}, u32[]{:S(2)}, u32[]{:S(2)}) collective-permute-start(bf16[256,512]{1,0:T(8,128)(2,1)S(1)} %copy-done.10), channel_id=1, source_target_pairs={{0,256},{128,384},{256,0},{384,128},{1,257},{129,385},{257,1},{385... | collective-permute-start | bytes 786440 | tf_op jit(solution)/shard_map/ppermute | solution.py:183
  80.5 46.9 %copy-start.3 = (bf16[256,512]{1,0:T(8,128)(2,1)S(1)}, bf16[256,512]{1,0:T(8,128)(2,1)}, u32[]{:S(2)}) copy-start(bf16[256,512]{1,0:T(8,128)(2,1)} %copy-done.2) | copy-start | bytes 786436
  94.5 8.8 %copy-start.5 = (bf16[256,512]{1,0:T(8,128)(2,1)}, bf16[256,512]{1,0:T(8,128)(2,1)S(1)}, u32[]{:S(2)}) copy-start(bf16[256,512]{1,0:T(8,128)(2,1)S(1)} %collective-permute-done.4.refs_2_) | copy-start | bytes 786436
  103.3 34.2 %all-to-all-start.3 = ((bf16[16,16,1024]{2,1,0:T(8,128)(2,1)}), bf16[16,16,1024]{2,1,0:T(8,128)(2,1)S(1)}, u32[]{:S(2)}, u32[]{:S(2)}) async-start(bf16[16,16,1024]{2,1,0:T(8,128)(2,1)} %shard_map.117), calls=%async_computation.3 | async-start | bytes 1048576 | tf_op jit(solution)/shard_map/all_to_all | solution.py:274
  110.0 17.4 %collective-permute-start.7 = (bf16[256,1024]{1,0:T(8,128)(2,1)S(1)}, bf16[256,1024]{1,0:T(8,128)(2,1)S(1)}, u32[]{:S(2)}, u32[]{:S(2)}) collective-permute-start(bf16[256,1024]{1,0:T(8,128)(2,1)S(1)} %shard_map.116.refs_4_), channel_id=1, source_target_pairs={{0,128},{128,0},{256,384},{384,256},{1,129},{129,1},{257,385},{385... | collective-permute-start | bytes 1572872 | tf_op jit(solution)/shard_map/ppermute | solution.py:183
  111.9 15.5 %collective-permute-start.8 = (bf16[256,1024]{1,0:T(8,128)(2,1)S(1)}, bf16[256,1024]{1,0:T(8,128)(2,1)S(1)}, u32[]{:S(2)}, u32[]{:S(2)}) collective-permute-start(bf16[256,1024]{1,0:T(8,128)(2,1)S(1)} %collective-permute-done.3.refs_6_), channel_id=1, source_target_pairs={{0,128},{128,0},{256,384},{384,256},{1,129},{129,1},{257,385},{385... | collective-permute-start | bytes 1572872 | tf_op jit(solution)/shard_map/ppermute | solution.py:183
  114.3 13.1 %collective-permute-start.6 = (bf16[256,512]{1,0:T(8,128)(2,1)}, bf16[256,512]{1,0:T(8,128)(2,1)}, u32[]{:S(2)}, u32[]{:S(2)}) collective-permute-start(bf16[256,512]{1,0:T(8,128)(2,1)} %copy-done.4), channel_id=1, source_target_pairs={{0,384},{128,256},{256,128},{384,0},{1,385},{129,257},{257,129},{3... | collective-permute-start | bytes 786440 | tf_op jit(solution)/shard_map/ppermute | solution.py:183
  116.5 10.9 %collective-permute-start.5 = (bf16[256,512]{1,0:T(8,128)(2,1)}, bf16[256,512]{1,0:T(8,128)(2,1)}, u32[]{:S(2)}, u32[]{:S(2)}) collective-permute-start(bf16[256,512]{1,0:T(8,128)(2,1)} %copy-done.8), channel_id=1, source_target_pairs={{0,128},{128,0},{256,384},{384,256},{1,129},{129,1},{257,385},{385... | collective-permute-start | bytes 786440 | tf_op jit(solution)/shard_map/ppermute | solution.py:183
  127.4 1.0 copy-start.6
